TPU v7x, 32 devices: a whole 2x2x4 slice. The times are simulated.
32 devices in a mesh: rep: 16 (over z, y, core), voc: 2 (over x).
Axes of the slice: x: 2, y: 2, z: 4, core: 2. Of those that a mesh axis runs over, the one named last changes fastest.
Arguments:
- states: bfloat16 [2, 256, 6144], P(None, None, 'rep'), may hold values from -6 to 6
- head_weight: bfloat16 [6144, 4096], P('rep', 'voc'), may hold values from -0.21875 to 0.21875
- pair_order: int32 [2, 8], replicated, may hold values from 0 to 7, each once within a row
- row_example: int32 [2, 8, 256], replicated, may hold values from 0 to 255, each once within a row
Outputs:
- state_grad: bfloat16 [2, 256, 6144], P(None, None, 'rep')
- head_grad: bfloat16 [6144, 4096], P('rep', 'voc')
Inputs may be any that keep to these rules, and one draw needn't show every extreme that they name: Each row pair_order[m] holds every replica once. Each row row_example[m, r] holds every number of 0 to 255 once.
All inputs are finite; a program needn't handle non-finite values.
Results may differ from a plain program's by a relative error of at most 0.0055.
Values may be sent and summed in bfloat16 or wider, within the bound.
No kernel may reach another device: no remote copies, remote signals or barrier semaphores. Data moves between devices by JAX's collectives and lax.ppermute only.
A program may use at most 64 MiB of HBM per device.

v0:
```python
import jax
import jax.numpy as jnp
from jax import lax
from jax.sharding import PartitionSpec as P

distill_weight = 0.0625


def partner_2(block, axis, apart):
    count = lax.axis_size(axis)
    route = []
    for low in range(count):
        high = low | 1 << apart
        if high != low and high < count:
            route += [(low, high), (high, low)]
    return lax.ppermute(block, axis, route)


def partner_table(pair_order):
    slot_count = pair_order.shape[1]
    slot_ids = jnp.arange(slot_count, dtype=jnp.int32)
    matches = pair_order[:, None, :] == slot_ids[None, :, None]
    position = jnp.sum(jnp.where(matches, slot_ids[None, None, :], 0), axis=2)
    following = (position + 1) % slot_count
    return jnp.take_along_axis(pair_order, following, axis=1)


def to_examples(rows_in, examples):
    slot_count = examples.shape[1]
    slot_ids = jnp.arange(slot_count, dtype=jnp.int32)
    onehot = (examples[:, None, :] == slot_ids[None, :, None]).astype(jnp.bfloat16)
    return jnp.einsum("mei,miw->mew", onehot, rows_in, preferred_element_type=jnp.float32).astype(
        jnp.bfloat16
    )


def differences(received, pair_table):
    partner_rows = jax.vmap(
        lambda source_block, index_row: jnp.take(source_block, index_row, axis=0)
    )(received, pair_table)
    spread = received.astype(jnp.float32) - partner_rows.astype(jnp.float32)
    return (distill_weight * spread).astype(jnp.bfloat16)


def body(states, head_weight, pair_order, row_example):
    micro_count, row_count, half_width = states.shape
    vocab_shard = head_weight.shape[1]
    devices = lax.axis_size("rep")
    rep_place = lax.axis_index("rep")
    replica = rep_place // 2
    pair_side = rep_place % 2
    examples = lax.dynamic_index_in_dim(row_example, replica, 1, keepdims=False)
    ordered = to_examples(states, examples)
    flat_states = ordered.reshape(micro_count * row_count, half_width)
    partial_logits = jnp.dot(flat_states, head_weight, preferred_element_type=jnp.float32)
    partial_logits = partial_logits.reshape(micro_count, row_count, vocab_shard)
    partner = partner_table(pair_order)
    sources = jnp.arange(devices, dtype=jnp.int32)
    partner_dev = 2 * jnp.take(partner, sources // 2, axis=1) + sources % 2
    row_span = row_count // 2
    own_rows = lax.dynamic_slice_in_dim(partial_logits, pair_side * row_span, row_span, 1)
    theirs = lax.dynamic_slice_in_dim(partial_logits, (1 - pair_side) * row_span, row_span, 1)
    logits = (own_rows + partner_2(theirs, "rep", 0)).astype(jnp.bfloat16)
    logit_tiles = logits.reshape(micro_count, devices, row_span // devices, vocab_shard)
    pieces = []
    for micro_index in range(micro_count):
        pair_table = partner_dev[micro_index : micro_index + 1]

        def settle_each(received, pair_table=pair_table):
            return lax.all_to_all(
                differences(received, pair_table), "rep", split_axis=1, concat_axis=1, tiled=True
            )

        pieces.append(
            settle_each(
                lax.all_to_all(
                    logit_tiles[micro_index : micro_index + 1],
                    "rep",
                    split_axis=1,
                    concat_axis=1,
                    tiled=True,
                )
            )
        )
    graded = jnp.concatenate(pieces, axis=0)
    graded = graded.reshape(micro_count, row_span, vocab_shard)
    other_half = partner_2(graded, "rep", 0)
    first_rows = jnp.where(pair_side == 0, graded, other_half)
    second_rows = jnp.where(pair_side == 0, other_half, graded)
    gradient = jnp.concatenate([first_rows, second_rows], axis=1)
    flat_grad = gradient.reshape(micro_count * row_count, vocab_shard)
    head_grad = jnp.einsum(
        "rw,rv->wv", flat_states, flat_grad, preferred_element_type=jnp.float32
    ).astype(jnp.bfloat16)
    local_state = jnp.einsum(
        "rv,wv->rw", flat_grad, head_weight, preferred_element_type=jnp.float32
    )
    state_canon = lax.psum(local_state, "voc").astype(jnp.bfloat16)
    state_canon = state_canon.reshape(micro_count, row_count, half_width)
    state_grad = jnp.take_along_axis(state_canon, examples[:, :, None], axis=1)
    return (state_grad, head_grad)


def solution(mesh):
    return jax.shard_map(
        body,
        mesh=mesh,
        in_specs=(P(None, None, "rep"), P("rep", "voc"), P(), P()),
        out_specs=(P(None, None, "rep"), P("rep", "voc")),
        check_vma=False,
    )
```

profile of v0, /device:TPU:0, one launch (start us, length us, event | category | flops | bytes accessed | tf_op | source)
XLA Modules:
  0.0 132.4 jit_solution(12628385690307313803)
XLA Ops:
  0.7 0.8 fusion.10
  1.5 1.3 convolution_convert_fusion
  2.9 3.2 %fusion = f32[2,256,2048]{2,1,0:T(8,128)} fusion(bf16[2,256,384]{2,1,0:T(8,128)(2,1)S(1)} %convolution_convert_fusion, bf16[384,2048]{1,0:T(8,128)(2,1)S(1)} %copy-done), kind=kOutput, calls=%fused_computation.8 | convolution fusion | flops 805306368 | bytes 6160384 | tf_op jit(solution)/shard_map/dot_general | solution.py:55
  6.1 3.2 %constant_dynamic-slice_fusion = f32[2,128,2048]{2,1,0:T(8,128)} fusion(f32[2,256,2048]{2,1,0:T(8,128)} %fusion, s32[]{:T(128)S(6)} %select_n.159), kind=kLoop, calls=%fused_computation.72 | loop fusion | bytes 4194308 | tf_op jit(solution)/shard_map/dynamic_slice | solution.py:62
  9.2 0.5 collective-permute-start
  10.0 3.8 %collective-permute-done = f32[2,128,2048]{2,1,0:T(8,128)} collective-permute-done((f32[2,128,2048]{2,1,0:T(8,128)}, f32[2,128,2048]{2,1,0:T(8,128)}, u32[]{:S(2)}, u32[]{:S(2)}) %collective-permute-start) | collective-permute-done | bytes 2097184 | tf_op jit(solution)/shard_map/ppermute | solution.py:16
  13.8 2.5 %add_convert_fusion = bf16[2,128,2048]{2,1,0:T(8,128)(2,1)S(1)} fusion(f32[2,128,2048]{2,1,0:T(8,128)} %collective-permute-done, f32[2,256,2048]{2,1,0:T(8,128)} %fusion, s32[]{:T(128)S(6)} %select_n.158), kind=kLoop, calls=%fused_computation.7 | loop fusion | flops 1048576 | bytes 5242884 | tf_op jit(solution)/shard_map/convert_element_type | solution.py:63
  16.3 1.0 slice_bitcast_fusion.1
  17.3 7.3 %all-to-all-start = ((bf16[1,16,8,2048]{3,2,0,1:T(8,128)(2,1)}), bf16[1,16,8,2048]{3,2,0,1:T(8,128)(2,1)S(1)}, u32[]{:S(2)}, u32[]{:S(2)}) async-start(bf16[1,16,8,2048]{3,2,0,1:T(8,128)(2,1)} %get-tuple-element.11), calls=%async_computation | async-start | bytes 1048576 | tf_op jit(solution)/shard_map/all_to_all | solution.py:76
  24.8 0.7 gather_fusion.1
  25.6 0.6 gather_fusion
  26.3 12.8 %all-to-all-done = bf16[1,16,8,2048]{3,2,0,1:T(8,128)(2,1)S(1)} async-done(((bf16[1,16,8,2048]{3,2,0,1:T(8,128)(2,1)}), bf16[1,16,8,2048]{3,2,0,1:T(8,128)(2,1)S(1)}, u32[]{:S(2)}, u32[]{:S(2)}) %all-to-all-start) | async-done | bytes 524320 | tf_op jit(solution)/shard_map/all_to_all | solution.py:76
  39.1 4.1 %all-to-all-start.2 = ((bf16[1,16,8,2048]{3,2,0,1:T(8,128)(2,1)}), bf16[1,16,8,2048]{3,2,0,1:T(8,128)(2,1)S(1)}, u32[]{:S(2)}, u32[]{:S(2)}) async-start(bf16[1,16,8,2048]{3,2,0,1:T(8,128)(2,1)} %get-tuple-element.12), calls=%async_computation.2 | async-start | bytes 1048576 | tf_op jit(solution)/shard_map/all_to_all | solution.py:76
  43.2 0.7 fusion.5
  43.9 0.6 and_reduce_fusion.1
  44.6 0.6 gather_fusion.3
  45.2 1.7 %fusion.2 = bf16[1,16,8,2048]{3,2,0,1:T(8,128)(2,1)} fusion(bf16[16,8,2048]{2,1,0:T(8,128)(2,1)S(1)} %gather_fusion.3, bf16[1,16,8,2048]{3,2,0,1:T(8,128)(2,1)S(1)} %all-to-all-done, pred[16]{0:T(512)(128)(4,1)} %get-tuple-element.3), kind=kLoop, calls=%fused_computation.17 | loop fusion | flops 1572864 | bytes 1572880 | tf_op jit(solution)/shard_map/convert_element_type | solution.py:42
  46.9 10.8 %all-to-all-done.2 = bf16[1,16,8,2048]{3,2,0,1:T(8,128)(2,1)S(1)} async-done(((bf16[1,16,8,2048]{3,2,0,1:T(8,128)(2,1)}), bf16[1,16,8,2048]{3,2,0,1:T(8,128)(2,1)S(1)}, u32[]{:S(2)}, u32[]{:S(2)}) %all-to-all-start.2) | async-done | bytes 524320 | tf_op jit(solution)/shard_map/all_to_all | solution.py:76
  57.7 4.1 %all-to-all-start.1 = ((bf16[1,16,8,2048]{3,2,0,1:T(8,128)(2,1)}), bf16[1,16,8,2048]{3,2,0,1:T(8,128)(2,1)S(1)}, u32[]{:S(2)}, u32[]{:S(2)}) async-start(bf16[1,16,8,2048]{3,2,0,1:T(8,128)(2,1)} %fusion.2), calls=%async_computation.1 | async-start | bytes 1048576 | tf_op jit(solution)/shard_map/all_to_all | solution.py:70
  61.8 1.4 %gather_fusion.4 = bf16[16,8,2048]{2,1,0:T(8,128)(2,1)} fusion(bf16[1,16,8,2048]{3,2,0,1:T(8,128)(2,1)S(1)} %all-to-all-done.2, s32[16]{0:T(128)S(1)} %or_bitcast_fusion), kind=kCustom, calls=%fused_computation.1.clone | custom fusion | bytes 1048704 | tf_op jit(solution)/shard_map/vmap(jit(_take))/gather | solution.py:39
  63.2 1.3 fusion.3
  64.5 11.7 %all-to-all-done.1 = bf16[1,16,8,2048]{3,2,0,1:T(8,128)(2,1)S(1)} async-done(((bf16[1,16,8,2048]{3,2,0,1:T(8,128)(2,1)}), bf16[1,16,8,2048]{3,2,0,1:T(8,128)(2,1)S(1)}, u32[]{:S(2)}, u32[]{:S(2)}) %all-to-all-start.1) | async-done | bytes 524320 | tf_op jit(solution)/shard_map/all_to_all | solution.py:70
  76.3 18.4 %all_to_all.20 = bf16[1,16,8,2048]{3,2,0,1:T(8,128)(2,1)S(1)} all-to-all(bf16[1,16,8,2048]{3,2,0,1:T(8,128)(2,1)S(1)} %fusion.3), channel_id=1, replica_groups=mesh['rep'=16,'voc'=2] {'rep'}, dimensions={1} | all-to-all | bytes 1048576 | tf_op jit(solution)/shard_map/all_to_all | solution.py:70
  94.6 1.1 copy_bitcast_fusion
  95.7 3.0 %collective-permute-done.1 = bf16[2,128,2048]{2,1,0:T(8,128)(2,1)} collective-permute-done((bf16[2,128,2048]{2,1,0:T(8,128)(2,1)}, bf16[2,128,2048]{2,1,0:T(8,128)(2,1)}, u32[]{:S(2)}, u32[]{:S(2)}) %collective-permute-start.1) | collective-permute-done | bytes 1048608 | tf_op jit(solution)/shard_map/ppermute | solution.py:16
  98.7 1.8 %broadcast_select_fusion.1 = (bf16[2,128,2048]{2,1,0:T(8,128)(2,1)S(1)}, bf16[2,128,2048]{2,1,0:T(8,128)(2,1)S(1)}) fusion(bf16[2,128,2048]{2,1,0:T(8,128)(2,1)} %collective-permute-done.1, pred[]{:T(512)S(6)} %eq.20, bf16[1,16,8,2048]{3,2,0,1:T(8,128)(2,1)S(1)} %all_to_all.20, bf16[1,16,8,2048]{3,2,0,1:T(8,128)(2,1)S(1)} %all-to-all-done.1), kind=kLoop, calls=%fused_computation.16 | loop fusion | flops 1572864 | bytes 4194305 | tf_op jit(solution)/shard_map/jit(_where)/select_n | solution.py:88
  100.4 2.2 %bitcast_convert_fusion = bf16[384,2048]{1,0:T(8,128)(2,1)} fusion(bf16[2,256,384]{2,1,0:T(8,128)(2,1)S(1)} %convolution_convert_fusion, bf16[2,128,2048]{2,1,0:T(8,128)(2,1)S(1)} %get-tuple-element.10, bf16[2,128,2048]{2,1,0:T(8,128)(2,1)S(1)} %get-tuple-element.9), kind=kOutput, calls=%fused_computation.5 | convolution fusion | flops 810287104 | bytes 4063232 | tf_op jit(solution)/shard_map/rw,rv->wv/dot_general | solution.py:92
  102.6 0.2 pad_maximum_fusion
  102.8 1.3 fusion.16
  104.1 23.7 %all-reduce.1 = bf16[512,384]{1,0:T(8,128)(2,1)S(1)} all-reduce(f32[512,384]{1,0:T(8,128)S(1)} %fusion.16), channel_id=1, replica_groups=mesh['rep'=16,'voc'=2] {'voc'}, use_global_device_ids=true, to_apply=%region_1.3 | all-reduce | flops 196608 | bytes 1179648 | tf_op jit(solution)/shard_map/psum | solution.py:98
  127.8 3.7 %gather_fusion.2 = bf16[512,384]{1,0:T(8,128)(2,1)S(1)} fusion(bf16[2,256,384]{2,1,0:T(8,128)(2,1)S(1)} %bitcast.70, s32[512]{0:T(512)S(1)} %bitcast.69), kind=kCustom, calls=%fused_computation.4 | custom fusion | bytes 790528 | tf_op jit(solution)/shard_map/jit(take_along_axis)/gather | solution.py:100
  131.5 0.9 broadcast_select_fusion.2
  (27 shorter events, 0.8 us)
Async XLA Ops:
  0.6 2.2 %copy-start = (bf16[384,2048]{1,0:T(8,128)(2,1)S(1)}, bf16[384,2048]{1,0:T(8,128)(2,1)}, u32[]{:S(2)}) copy-start(bf16[384,2048]{1,0:T(8,128)(2,1)} %param.7) | copy-start | bytes 4718596
  6.1 3.6 %copy-start.1 = (s32[2,8]{1,0:T(2,128)S(1)}, s32[2,8]{1,0:T(2,128)}, u32[]{:S(2)}) copy-start(s32[2,8]{1,0:T(2,128)} %param.8) | copy-start | bytes 196
  9.2 4.6 %collective-permute-start = (f32[2,128,2048]{2,1,0:T(8,128)}, f32[2,128,2048]{2,1,0:T(8,128)}, u32[]{:S(2)}, u32[]{:S(2)}) collective-permute-start(f32[2,128,2048]{2,1,0:T(8,128)} %constant_dynamic-slice_fusion), channel_id=1, source_target_pairs={{0,2},{2,0},{4,6},{6,4},{8,10},{10,8},{12,14},{14,12},{16,18},{18,... | collective-permute-start | bytes 6291464 | tf_op jit(solution)/shard_map/ppermute | solution.py:16
  17.3 21.8 %all-to-all-start = ((bf16[1,16,8,2048]{3,2,0,1:T(8,128)(2,1)}), bf16[1,16,8,2048]{3,2,0,1:T(8,128)(2,1)S(1)}, u32[]{:S(2)}, u32[]{:S(2)}) async-start(bf16[1,16,8,2048]{3,2,0,1:T(8,128)(2,1)} %get-tuple-element.11), calls=%async_computation | async-start | bytes 1048576 | tf_op jit(solution)/shard_map/all_to_all | solution.py:76
  39.1 18.6 %all-to-all-start.2 = ((bf16[1,16,8,2048]{3,2,0,1:T(8,128)(2,1)}), bf16[1,16,8,2048]{3,2,0,1:T(8,128)(2,1)S(1)}, u32[]{:S(2)}, u32[]{:S(2)}) async-start(bf16[1,16,8,2048]{3,2,0,1:T(8,128)(2,1)} %get-tuple-element.12), calls=%async_computation.2 | async-start | bytes 1048576 | tf_op jit(solution)/shard_map/all_to_all | solution.py:76
  45.1 16.6 %copy-start.2 = (s32[16]{0:T(128)S(1)}, s32[16]{0:T(128)}, u32[]{:S(2)}) copy-start(s32[16]{0:T(128)} %get-tuple-element.6) | copy-start | bytes 196
  57.7 18.6 %all-to-all-start.1 = ((bf16[1,16,8,2048]{3,2,0,1:T(8,128)(2,1)}), bf16[1,16,8,2048]{3,2,0,1:T(8,128)(2,1)S(1)}, u32[]{:S(2)}, u32[]{:S(2)}) async-start(bf16[1,16,8,2048]{3,2,0,1:T(8,128)(2,1)} %fusion.2), calls=%async_computation.1 | async-start | bytes 1048576 | tf_op jit(solution)/shard_map/all_to_all | solution.py:70
  95.7 3.0 %collective-permute-start.1 = (bf16[2,128,2048]{2,1,0:T(8,128)(2,1)}, bf16[2,128,2048]{2,1,0:T(8,128)(2,1)}, u32[]{:S(2)}, u32[]{:S(2)}) collective-permute-start(bf16[2,128,2048]{2,1,0:T(8,128)(2,1)} %copy_bitcast_fusion), channel_id=1, source_target_pairs={{0,2},{2,0},{4,6},{6,4},{8,10},{10,8},{12,14},{14,12},{16,18},{18,... | collective-permute-start | bytes 3145736 | tf_op jit(solution)/shard_map/ppermute | solution.py:16
where the time goes:
time: 133 us; the launch traced here: 132 us
  waiting for transfers between devices  42.1 us (32%)
  blocking collectives  42 us (32%)
  starting transfers between devices  16 us (12%)
  other arithmetic  11.9 us (9%)
  local copies, waits for them, and re-layouts  11.5 us (9%)
  matrix products  7.96 us (6%)
    psum x1, blocking collectives, body(): state_canon = lax.psum(local_state, 'voc').astype(jnp.bfloat16)  23.7 us
    all_to_all x2, waiting for transfers between devices, body(): lax.all_to_all(logit_tiles[micro_index:micro_index + 1], 'rep', split_axi...  23.6 us
    all_to_all x1, blocking collectives, settle_each(): lax.all_to_all(differences(received, pair_table), 'rep', split_axis=1, co...  18.4 us
    all_to_all x1, waiting for transfers between devices, settle_each(): lax.all_to_all(differences(received, pair_table), 'rep', split_axis=1, co...  11.7 us
    all_to_all x2, starting transfers between devices, body(): lax.all_to_all(logit_tiles[micro_index:micro_index + 1], 'rep', split_axi...  11.4 us
    ppermute x2, waiting for transfers between devices, partner_2(): return lax.ppermute(block, axis, route)  6.79 us
    all_to_all x1, starting transfers between devices, settle_each(): lax.all_to_all(differences(received, pair_table), 'rep', split_axis=1, co...  4.1 us
    gather x1, local copies, waits for them, and re-layouts, body(): state_grad = jnp.take_along_axis(state_canon, examples[:, :, None], axis=1)  3.68 us
  transfers between devices with their start and end apart: 5, of which 5 were waited for; matrix products, arithmetic and copies ran while one was open for 6% of the time, Pallas kernels for 0%

commit v1 on v0

v1 whole, which is shorter than its diff:
```python
import functools
import itertools
import math

import jax
import jax.numpy as jnp
from jax import lax
from jax.experimental import pallas as pl
from jax.experimental.pallas import tpu as pltpu
from jax.sharding import PartitionSpec as P

distill_weight = 0.0625
max_branches = 24


def partner_table(pair_order):
    slot_count = pair_order.shape[1]
    slot_ids = jnp.arange(slot_count, dtype=jnp.int32)
    matches = pair_order[:, None, :] == slot_ids[None, :, None]
    following = jnp.roll(pair_order, -1, axis=1)
    return jnp.sum(jnp.where(matches, following[:, None, :], 0), axis=2)


def route_kernel(order_ref, branch_ref, parity_ref, dest, src, color):
    micro_count, replicas = order_ref.shape
    pairs = replicas // 2
    for m in range(micro_count):
        for k in range(replicas):
            to, frm = order_ref[m, k], order_ref[m, (k + 1) % replicas]
            dest[frm] = to
            src[to] = frm
            color[k] = -1
        for start in range(0, replicas, 2):
            at = jnp.where(color[start] == 1, start + 1, start)
            for _ in range(pairs):
                color[at] = 0
                color[at ^ 1] = 1
                at = src[dest[at ^ 1] ^ 1]
        for z in range(pairs):
            parity_ref[m, 0, z] = color[2 * z]
            parity_ref[m, 1, z] = color[src[2 * z]]
        for c in range(2):
            sigma = []
            place = jnp.int32(0)
            for z in range(pairs):
                leaves = jnp.where(color[2 * z] == c, 2 * z, 2 * z + 1)
                to = dest[leaves] // 2
                smaller = to
                for earlier in sigma:
                    smaller = smaller - jnp.where(earlier < to, 1, 0)
                place = place * (pairs - z) + smaller
                sigma.append(to)
            branch_ref[m, c] = place


def routes(pair_order):
    micro_count, replicas = pair_order.shape
    smem = pl.BlockSpec(memory_space=pltpu.SMEM)
    return pl.pallas_call(
        route_kernel,
        out_shape=(
            jax.ShapeDtypeStruct((micro_count, 2), jnp.int32),
            jax.ShapeDtypeStruct((micro_count, 2, replicas // 2), jnp.int32),
        ),
        in_specs=[smem],
        out_specs=(smem, smem),
        scratch_shapes=[pltpu.SMEM((replicas,), jnp.int32)] * 3,
    )(pair_order)


def move_pairs(block, branch, pairs):
    def one(sigma, moved):
        if all(z == to for z, to in enumerate(sigma)):
            return moved
        route = [(z * 4 + low, to * 4 + low) for z, to in enumerate(sigma) for low in range(4)]
        return lax.ppermute(moved, "rep", route)

    every = [functools.partial(one, sigma) for sigma in itertools.permutations(range(pairs))]
    return lax.switch(branch, every, block)


def swap(block, axis, bit):
    count = lax.axis_size(axis)
    return lax.ppermute(block, axis, [(i, i ^ bit) for i in range(count)])


def difference(own, other):
    spread = own.astype(jnp.float32) - other.astype(jnp.float32)
    return (distill_weight * spread).astype(jnp.bfloat16)


def sum_over(block, axis):
    if lax.axis_size(axis) == 2:
        return block + swap(block, axis, 1)
    return lax.psum(block, axis)


def paired_body(states, head_weight, pair_order, row_example):
    micro_count, row_count, half_width = states.shape
    place = lax.axis_index("rep")
    replica, side = place // 2, place % 2
    pair, parity = replica // 2, replica % 2
    pairs = pair_order.shape[1] // 2
    quarter = row_count // 4
    local = jnp.arange(row_count, dtype=jnp.int32)
    block = local // quarter
    example_of = (
        (side ^ (block & 1)) * (2 * quarter) + (parity ^ (block >> 1)) * quarter + local % quarter
    )
    examples = lax.dynamic_index_in_dim(row_example, replica, 1, keepdims=False)
    onehot = (examples[:, None, :] == example_of[None, :, None]).astype(jnp.bfloat16)
    branch, sides = routes(pair_order)
    mine = lax.dynamic_index_in_dim(sides, pair, 2, keepdims=False)

    ordered, homes, sibs = [], [], []
    for m in range(micro_count):
        rows = jnp.dot(onehot[m], states[m], preferred_element_type=jnp.float32)
        ordered.append(rows.astype(jnp.bfloat16))
        partial = jnp.dot(ordered[m], head_weight, preferred_element_type=jnp.float32)
        partial = partial.reshape(2, 2, quarter, -1)
        logits = (partial[:, 0] + swap(partial[:, 1], "rep", 1)).astype(jnp.bfloat16)
        homes.append(logits[0])
        sibs.append(swap(logits[1], "rep", 2))

    head_parts, state_parts = [], []
    for m in range(micro_count):
        home, sib = homes[m], sibs[m]
        home_first = mine[m, 0] == parity
        first = move_pairs(jnp.where(home_first, home, sib), branch[m, 0], pairs)
        second = move_pairs(jnp.where(home_first, sib, home), branch[m, 1], pairs)
        to_home_first = mine[m, 1] == parity
        grad_home = difference(home, jnp.where(to_home_first, first, second))
        grad_sib = difference(sib, jnp.where(to_home_first, second, first))
        near = jnp.concatenate([grad_home, swap(grad_home, "rep", 1)], axis=0)
        grad_far = swap(grad_sib, "rep", 2)
        far = jnp.concatenate([grad_far, swap(grad_far, "rep", 1)], axis=0)
        states_here = []
        for part, gradient in enumerate((near, far)):
            rows = ordered[m][part * 2 * quarter : (part + 1) * 2 * quarter]
            head_parts.append((rows, gradient))
            back = jnp.einsum(
                "rv,wv->rw", gradient, head_weight, preferred_element_type=jnp.float32
            )
            states_here.append(sum_over(back, "voc").astype(jnp.bfloat16))
        state_canon = jnp.concatenate(states_here, axis=0)
        state_parts.append(
            jnp.einsum("ei,ew->iw", onehot[m], state_canon, preferred_element_type=jnp.float32)
        )
    state_grad = jnp.stack(state_parts).astype(jnp.bfloat16)
    rows = jnp.concatenate([r for r, _ in head_parts], axis=0)
    gradient = jnp.concatenate([g for _, g in head_parts], axis=0)
    head_grad = jnp.einsum("rw,rv->wv", rows, gradient, preferred_element_type=jnp.float32)
    return state_grad, head_grad.astype(jnp.bfloat16)


def spread_body(states, head_weight, pair_order, row_example):
    micro_count, row_count, half_width = states.shape
    devices = lax.axis_size("rep")
    place = lax.axis_index("rep")
    replica, side = place // 2, place % 2
    half = row_count // 2
    local = jnp.arange(row_count, dtype=jnp.int32)
    example_of = (side ^ (local // half)) * half + local % half
    examples = lax.dynamic_index_in_dim(row_example, replica, 1, keepdims=False)
    onehot = (examples[:, None, :] == example_of[None, :, None]).astype(jnp.bfloat16)
    ordered = jnp.einsum("mei,miw->mew", onehot, states, preferred_element_type=jnp.float32)
    ordered = ordered.astype(jnp.bfloat16)
    partner = partner_table(pair_order)
    sources = jnp.arange(devices, dtype=jnp.int32)
    partner_dev = 2 * jnp.repeat(partner, 2, axis=1) + sources % 2
    state_parts, gradients = [], []
    for m in range(micro_count):
        partial = jnp.dot(ordered[m], head_weight, preferred_element_type=jnp.float32)
        logits = (partial[:half] + swap(partial[half:], "rep", 1)).astype(jnp.bfloat16)
        tiles = logits.reshape(devices, half // devices, -1)
        tiles = lax.all_to_all(tiles, "rep", split_axis=0, concat_axis=0, tiled=True)
        mates = (partner_dev[m][:, None] == sources[None, :]).astype(jnp.bfloat16)
        mate_tiles = jnp.einsum("ds,srv->drv", mates, tiles, preferred_element_type=jnp.float32)
        graded = difference(tiles, mate_tiles)
        graded = lax.all_to_all(graded, "rep", split_axis=0, concat_axis=0, tiled=True)
        graded = graded.reshape(half, -1)
        gradient = jnp.concatenate([graded, swap(graded, "rep", 1)], axis=0)
        gradients.append(gradient)
        back = jnp.einsum("rv,wv->rw", gradient, head_weight, preferred_element_type=jnp.float32)
        state_canon = sum_over(back, "voc").astype(jnp.bfloat16)
        state_parts.append(
            jnp.einsum("ei,ew->iw", onehot[m], state_canon, preferred_element_type=jnp.float32)
        )
    state_grad = jnp.stack(state_parts).astype(jnp.bfloat16)
    head_grad = jnp.einsum(
        "mrw,mrv->wv", ordered, jnp.stack(gradients), preferred_element_type=jnp.float32
    )
    return state_grad, head_grad.astype(jnp.bfloat16)


def solution(mesh):
    replicas = mesh.shape["rep"] // 2
    few = replicas % 2 == 0 and math.factorial(replicas // 2) <= max_branches
    return jax.shard_map(
        paired_body if few else spread_body,
        mesh=mesh,
        in_specs=(P(None, None, "rep"), P("rep", "voc"), P(), P()),
        out_specs=(P(None, None, "rep"), P("rep", "voc")),
        check_vma=False,
    )
```

time: 133 us -> 109 us (0.82); the launches traced: 132 us -> 111 us
  blocking collectives: 42 us -> 0 us
  starting transfers between devices: 16 us -> 32.1 us
  between operations: 0.86 us -> 6.05 us
  local copies, waits for them, and re-layouts: 11.5 us -> 9.1 us
  other arithmetic: 11.9 us -> 9.62 us
  Pallas kernels: 0 us -> 1.68 us
    ppermute x2 -> x18, waiting for transfers between devices: 6.79 us -> 43.3 us  [the longest x4 25.4 us: one(): return lax.ppermute(moved, 'rep', route)]
    all_to_all x3 -> x0, waiting for transfers between devices: 35.3 us -> none  [the longest x2 23.6 us: body(): lax.all_to_all(logit_tiles[micro_index:micro_index + 1], 'rep', split_axi...]
    ppermute x2 -> x18, starting transfers between devices: 0.47 us -> 32.1 us  [the longest x4 19.9 us: one(): return lax.ppermute(moved, 'rep', route)]
    psum x1 -> x0, blocking collectives: 23.7 us -> none  [body(): state_canon = lax.psum(local_state, 'voc').astype(jnp.bfloat16)]
    all_to_all x1 -> x0, blocking collectives: 18.4 us -> none  [settle_each(): lax.all_to_all(differences(received, pair_table), 'rep', split_axis=1, co...]
    all_to_all x3 -> x0, starting transfers between devices: 15.5 us -> none  [the longest x2 11.4 us: body(): lax.all_to_all(logit_tiles[micro_index:micro_index + 1], 'rep', split_axi...]
    gather x10 -> x0, local copies, waits for them, and re-layouts: 7.14 us -> none  [the longest x1 3.68 us: body(): state_grad = jnp.take_along_axis(state_canon, examples[:, :, None], axis=1)]
    unnamed x0 -> x2, other arithmetic: none -> 2.87 us
  transfers between devices with their start and end apart: 5 -> 18, of which waited for: 5 -> 8; matrix products, arithmetic and copies ran while one was open for 6% -> 18% of each run, Pallas kernels for 0% -> 2%
where the time goes in v1:
time: 109 us; the launch traced here: 111 us
  waiting for transfers between devices  43.3 us (40%)
  starting transfers between devices  32.1 us (29%)
  other arithmetic  9.62 us (9%)
  local copies, waits for them, and re-layouts  9.1 us (8%)
  matrix products  8.89 us (8%)
  between operations  6.05 us (6%)
  Pallas kernels  1.68 us (2%)
    ppermute x4, waiting for transfers between devices, one(): return lax.ppermute(moved, 'rep', route)  25.4 us
    ppermute x4, starting transfers between devices, one(): return lax.ppermute(moved, 'rep', route)  19.9 us
    ppermute x14, waiting for transfers between devices, swap(): return lax.ppermute(block, axis, [(i, i ^ bit) for i in range(count)])  17.9 us
    ppermute x14, starting transfers between devices, swap(): return lax.ppermute(block, axis, [(i, i ^ bit) for i in range(count)])  12.2 us
    dot_general x4, matrix products, paired_body(): jnp.einsum('rv,wv->rw', gradient, head_weight, preferred_element_type=jnp...  3.33 us
    convert_element_type x2, other arithmetic, paired_body(): (partial[:, 0] + swap(partial[:, 1], 'rep', 1)).astype(jnp.bfloat16)  2.99 us
    unnamed x2, other arithmetic  2.87 us
    unnamed x26, local copies, waits for them, and re-layouts  2.5 us
  transfers between devices with their start and end apart: 18, of which 8 were waited for; matrix products, arithmetic and copies ran while one was open for 18% of the time, Pallas kernels for 2%

profile of v1, /device:TPU:0, one launch (start us, length us, event | category | flops | bytes accessed | tf_op | source)
XLA Modules:
  0.0 111.0 jit_solution(12853716057545148748)
XLA Ops:
  1.7 1.2 %convolution_convert_fusion.4 = bf16[256,384]{1,0:T(8,128)(2,1)S(1)} fusion(pred[2,256,256]{2,1,0:T(32,128)(4,1)S(1)} %broadcast_compare_fusion, bf16[2,256,384]{2,1,0:T(8,128)(2,1)} %param.100), kind=kOutput, calls=%fused_computation.52 | convolution fusion | flops 50429952 | bytes 458752 | tf_op jit(solution)/shard_map/dot_general | solution.py:117
  3.6 1.1 %slice_bitcast_fusion.2 = f32[2,64,2048]{2,1,0:T(8,128)} fusion(f32[2,2,64,2048]{3,2,1,0:T(8,128)S(1)} %bitcast.84), kind=kLoop, calls=%fused_computation.59 | loop fusion | bytes 2097152 | tf_op jit(solution)/shard_map/squeeze | solution.py:121
  6.3 1.3 %copy-done.1 = f32[256,2048]{1,0:T(8,128)} copy-done((f32[256,2048]{1,0:T(8,128)}, f32[256,2048]{1,0:T(8,128)S(1)}, u32[]{:S(2)}) %copy-start.1) | copy-done | bytes 2097176
  8.2 1.7 %shard_map.59 = (s32[2,2]{1,0:T(2,128)}, s32[2,2,4]{2,1,0:T(2,128)}) custom-call(s32[2,8]{1,0:T(2,128)} %order_ref.1), custom_call_target="tpu_custom_call" | custom-call | tf_op jit(solution)/shard_map/pallas_call | solution.py:59
  14.0 1.5 %fusion.46 = (s32[1,1]{1,0:T(1,128)}, s32[1,1]{1,0:T(1,128)}, s32[1,1]{1,0:T(1,128)}, s32[1,1]{1,0:T(1,128)}) fusion(s32[2,2]{1,0:T(2,128)} %get-tuple-element.683), kind=kLoop, calls=%fused_computation.137 | loop fusion | bytes 32 | tf_op jit(solution)/shard_map/slice | solution.py:130
  18.0 1.7 %fusion.5 = bf16[2,64,2048]{2,1,0:T(8,128)(2,1)S(1)} fusion(f32[2,64,2048]{2,1,0:T(8,128)} %collective-permute-done.92, f32[2,2,64,2048]{3,2,1,0:T(8,128)} %bitcast.85), kind=kLoop, calls=%fused_computation.62 | loop fusion | flops 524288 | bytes 2621440 | tf_op jit(solution)/shard_map/convert_element_type | solution.py:121
  19.7 2.6 %collective-permute-start.93 = (bf16[64,2048]{1,0:T(8,128)(2,1)S(1)}, bf16[64,2048]{1,0:T(8,128)(2,1)S(1)}, u32[]{:S(2)}, u32[]{:S(2)}) collective-permute-start(bf16[64,2048]{1,0:T(8,128)(2,1)S(1)} %get-tuple-element.689), channel_id=1, source_target_pairs={{0,4},{2,6},{4,0},{6,2},{8,12},{10,14},{12,8},{14,10},{16,20},{18,... | collective-permute-start | bytes 786440 | tf_op jit(solution)/shard_map/ppermute | solution.py:84
  22.3 1.3 %fusion.3 = bf16[2,64,2048]{2,1,0:T(8,128)(2,1)S(1)} fusion(f32[2,64,2048]{2,1,0:T(8,128)} %collective-permute-done.99, f32[2,2,64,2048]{3,2,1,0:T(8,128)S(1)} %bitcast.83), kind=kLoop, calls=%fused_computation.58 | loop fusion | flops 524288 | bytes 2621440 | tf_op jit(solution)/shard_map/convert_element_type | solution.py:121
  24.4 5.0 %collective-permute-done.93 = bf16[64,2048]{1,0:T(8,128)(2,1)S(1)} collective-permute-done((bf16[64,2048]{1,0:T(8,128)(2,1)S(1)}, bf16[64,2048]{1,0:T(8,128)(2,1)S(1)}, u32[]{:S(2)}, u32[]{:S(2)}) %collective-permute-start.93) | collective-permute-done | bytes 262176 | tf_op jit(solution)/shard_map/ppermute | solution.py:84
  29.5 1.4 %conditional.5 = (bf16[64,2048]{1,0:T(8,128)(2,1)}) conditional(s32[]{:T(128)} %bitcast.10, (pred[]{:T(512)}, bf16[64,2048]{1,0:T(8,128)(2,1)S(1)}, bf16[64,2048]{1,0:T(8,128)(2,1)S(1)}) %tuple.346, (pred[]{:T(512)}, bf16[64,2048]{1,0:T(8,128)(2,1)S(1)}, bf16[64,2048]{1,0:T(8,128)(2,1)S(1)}) %tuple.346, (pred[]{:T(512)}, ...), branch_computations={%region_24.25_spmd, %region_25.26_spmd, %region_26.27_spmd, %regio... | conditional | flops 131072 | bytes 1835057 | solution.py:79
  29.5 1.4 %collective-permute-start.47 = (bf16[64,2048]{1,0:T(8,128)(2,1)S(1)}, bf16[64,2048]{1,0:T(8,128)(2,1)}, u32[]{:S(2)}, u32[]{:S(2)}) collective-permute-start(bf16[64,2048]{1,0:T(8,128)(2,1)S(1)} %broadcast_select_fusion.2), channel_id=1, source_target_pairs={{0,0},{2,2},{4,4},{6,6},{8,16},{10,18},{12,20},{14,22},{16,8},{18,... | collective-permute-start | bytes 786440 | tf_op jit(solution)/shard_map/cond/branch_2_fun/ppermute | solution.py:76
  31.6 23.9 %conditional.4 = (bf16[64,2048]{1,0:T(8,128)(2,1)}) conditional(s32[]{:T(128)} %bitcast.7, bf16[64,2048]{1,0:T(8,128)(2,1)} %broadcast_select_fusion.49, bf16[64,2048]{1,0:T(8,128)(2,1)} %broadcast_select_fusion.49, bf16[64,2048]{1,0:T(8,128)(2,1)} %broadcast_select_fusion.49, ...), branch_computations={%region_0.1_spmd, %region_1.2_spmd, %region_2.3_spmd, %region_3.4_... | conditional | bytes 1572912 | solution.py:79
  31.6 5.9 %collective-permute-start.19 = (bf16[64,2048]{1,0:T(8,128)(2,1)}, bf16[64,2048]{1,0:T(8,128)(2,1)S(1)}, u32[]{:S(2)}, u32[]{:S(2)}) collective-permute-start(bf16[64,2048]{1,0:T(8,128)(2,1)} %param.20), channel_id=1, source_target_pairs={{0,24},{2,26},{4,28},{6,30},{8,8},{10,10},{12,12},{14,14},{16,0},{... | collective-permute-start | bytes 786440 | tf_op jit(solution)/shard_map/cond/branch_20_fun/ppermute | solution.py:76
  37.6 17.2 %collective-permute-done.19 = bf16[64,2048]{1,0:T(8,128)(2,1)S(1)} collective-permute-done((bf16[64,2048]{1,0:T(8,128)(2,1)}, bf16[64,2048]{1,0:T(8,128)(2,1)S(1)}, u32[]{:S(2)}, u32[]{:S(2)}) %collective-permute-start.19) | collective-permute-done | bytes 262176 | tf_op jit(solution)/shard_map/cond/branch_20_fun/ppermute | solution.py:76
  55.5 1.8 %multiply_convert_fusion.2 = bf16[64,2048]{1,0:T(8,128)(2,1)} fusion(bf16[64,2048]{1,0:T(8,128)(2,1)S(1)} %collective-permute-done.93, bf16[64,2048]{1,0:T(8,128)(2,1)} %get-tuple-element.701, bf16[64,2048]{1,0:T(8,128)(2,1)} %get-tuple-element.700, pred[]{:T(512)S(6)} %eq.36), kind=kLoop, calls=%fused_computation.81 | loop fusion | flops 786432 | bytes 1048577 | tf_op jit(solution)/shard_map/convert_element_type | solution.py:89
  57.3 1.5 %collective-permute-start.96 = (bf16[64,2048]{1,0:T(8,128)(2,1)}, bf16[64,2048]{1,0:T(8,128)(2,1)}, u32[]{:S(2)}, u32[]{:S(2)}) collective-permute-start(bf16[64,2048]{1,0:T(8,128)(2,1)} %multiply_convert_fusion.2), channel_id=1, source_target_pairs={{0,4},{2,6},{4,0},{6,2},{8,12},{10,14},{12,8},{14,10},{16,20},{18,... | collective-permute-start | bytes 786440 | tf_op jit(solution)/shard_map/ppermute | solution.py:84
  58.8 1.8 %constant_dynamic-update-slice_fusion.7 = (bf16[512,2048]{1,0:T(8,128)(2,1)}, bf16[64,2048]{1,0:T(8,128)(2,1)S(1)}) fusion(bf16[64,2048]{1,0:T(8,128)(2,1)} %get-tuple-element.700, bf16[64,2048]{1,0:T(8,128)(2,1)} %get-tuple-element.701, pred[]{:T(512)S(6)} %eq.36, bf16[2,64,2048]{2,1,0:T(8,128)(2,1)S(1)} %fusion.5), kind=kLoop, calls=%fused_computation.117 | loop fusion | flops 786431 | bytes 1310721
  60.6 1.4 %conditional.7 = (bf16[64,2048]{1,0:T(8,128)(2,1)}) conditional(s32[]{:T(128)} %bitcast.22, (pred[]{:T(512)}, bf16[64,2048]{1,0:T(8,128)(2,1)S(1)}, bf16[64,2048]{1,0:T(8,128)(2,1)S(1)}) %tuple.347, (pred[]{:T(512)}, bf16[64,2048]{1,0:T(8,128)(2,1)S(1)}, bf16[64,2048]{1,0:T(8,128)(2,1)S(1)}) %tuple.347, (pred[]{:T(512)}, ...), branch_computations={%region_72.73_spmd, %region_73.74_spmd, %region_74.75_spmd, %regio... | conditional | flops 131072 | bytes 1835057 | solution.py:79
  60.6 1.4 %collective-permute-start.71 = (bf16[64,2048]{1,0:T(8,128)(2,1)S(1)}, bf16[64,2048]{1,0:T(8,128)(2,1)}, u32[]{:S(2)}, u32[]{:S(2)}) collective-permute-start(bf16[64,2048]{1,0:T(8,128)(2,1)S(1)} %broadcast_select_fusion.27), channel_id=1, source_target_pairs={{0,0},{2,2},{4,4},{6,6},{8,16},{10,18},{12,20},{14,22},{16,24},{18... | collective-permute-start | bytes 786440 | tf_op jit(solution)/shard_map/cond/branch_3_fun/ppermute | solution.py:76
  62.0 19.7 %conditional.6 = (bf16[64,2048]{1,0:T(8,128)(2,1)S(1)}) conditional(s32[]{:T(128)} %bitcast.19, bf16[64,2048]{1,0:T(8,128)(2,1)S(1)} %broadcast_select_fusion.48, bf16[64,2048]{1,0:T(8,128)(2,1)S(1)} %broadcast_select_fusion.48, bf16[64,2048]{1,0:T(8,128)(2,1)S(1)} %broadcast_select_fusion.48, ...), branch_computations={%region_48.49_spmd, %region_49.50_spmd, %region_50.51_spmd, %regio... | conditional | bytes 1572912 | solution.py:79
  62.1 11.2 %collective-permute-start.30 = (bf16[64,2048]{1,0:T(8,128)(2,1)S(1)}, bf16[64,2048]{1,0:T(8,128)(2,1)S(1)}, u32[]{:S(2)}, u32[]{:S(2)}) collective-permute-start(bf16[64,2048]{1,0:T(8,128)(2,1)S(1)} %param.56), channel_id=1, source_target_pairs={{0,8},{2,10},{4,12},{6,14},{8,16},{10,18},{12,20},{14,22},{16,0},{... | collective-permute-start | bytes 786440 | tf_op jit(solution)/shard_map/cond/branch_8_fun/ppermute | solution.py:76
  73.3 8.2 %collective-permute-done.30 = bf16[64,2048]{1,0:T(8,128)(2,1)S(1)} collective-permute-done((bf16[64,2048]{1,0:T(8,128)(2,1)S(1)}, bf16[64,2048]{1,0:T(8,128)(2,1)S(1)}, u32[]{:S(2)}, u32[]{:S(2)}) %collective-permute-start.30) | collective-permute-done | bytes 262176 | tf_op jit(solution)/shard_map/cond/branch_8_fun/ppermute | solution.py:76
  81.9 1.7 %collective-permute-start.103 = (bf16[64,2048]{1,0:T(8,128)(2,1)S(1)}, bf16[64,2048]{1,0:T(8,128)(2,1)S(1)}, u32[]{:S(2)}, u32[]{:S(2)}) collective-permute-start(bf16[64,2048]{1,0:T(8,128)(2,1)S(1)} %multiply_convert_fusion), channel_id=1, source_target_pairs={{0,4},{2,6},{4,0},{6,2},{8,12},{10,14},{12,8},{14,10},{16,20},{18,... | collective-permute-start | bytes 786440 | tf_op jit(solution)/shard_map/ppermute | solution.py:84
  84.2 1.6 %collective-permute-start.95 = (f32[128,384]{1,0:T(8,128)S(1)}, f32[128,384]{1,0:T(8,128)S(1)}, u32[]{:S(2)}, u32[]{:S(2)}) collective-permute-start(f32[128,384]{1,0:T(8,128)S(1)} %fusion.6), channel_id=1, source_target_pairs={{0,1},{1,0},{2,3},{3,2},{4,5},{5,4},{6,7},{7,6},{8,9},{9,8},{10,11... | collective-permute-start | bytes 589832 | tf_op jit(solution)/shard_map/ppermute | solution.py:84
  86.7 2.6 %collective-permute-done.103 = bf16[64,2048]{1,0:T(8,128)(2,1)S(1)} collective-permute-done((bf16[64,2048]{1,0:T(8,128)(2,1)S(1)}, bf16[64,2048]{1,0:T(8,128)(2,1)S(1)}, u32[]{:S(2)}, u32[]{:S(2)}) %collective-permute-start.103) | collective-permute-done | bytes 262176 | tf_op jit(solution)/shard_map/ppermute | solution.py:84
  90.0 1.5 %fusion.10 = f32[128,384]{1,0:T(8,128)S(1)} fusion(bf16[384,2048]{1,0:T(8,128)(2,1)S(1)} %copy-done, bf16[64,2048]{1,0:T(8,128)(2,1)S(1)} %collective-permute-done.97, bf16[64,2048]{1,0:T(8,128)(2,1)} %collective-permute-done.96), kind=kOutput, calls=%fused_computation.67 | convolution fusion | flops 202375168 | bytes 2293760 | tf_op jit(solution)/shard_map/rv,wv->rw/dot_general | solution.py:141
  91.5 1.6 %collective-permute-start.98 = (f32[128,384]{1,0:T(8,128)S(1)}, f32[128,384]{1,0:T(8,128)S(1)}, u32[]{:S(2)}, u32[]{:S(2)}) collective-permute-start(f32[128,384]{1,0:T(8,128)S(1)} %fusion.10), channel_id=1, source_target_pairs={{0,1},{1,0},{2,3},{3,2},{4,5},{5,4},{6,7},{7,6},{8,9},{9,8},{10,11... | collective-permute-start | bytes 589832 | tf_op jit(solution)/shard_map/ppermute | solution.py:84
  95.5 3.1 %collective-permute-done.98 = f32[128,384]{1,0:T(8,128)S(1)} collective-permute-done((f32[128,384]{1,0:T(8,128)S(1)}, f32[128,384]{1,0:T(8,128)S(1)}, u32[]{:S(2)}, u32[]{:S(2)}) %collective-permute-start.98) | collective-permute-done | bytes 196640 | tf_op jit(solution)/shard_map/ppermute | solution.py:84
  98.9 3.6 %collective-permute-done.105 = f32[128,384]{1,0:T(8,128)S(1)} collective-permute-done((f32[128,384]{1,0:T(8,128)S(1)}, f32[128,384]{1,0:T(8,128)S(1)}, u32[]{:S(2)}, u32[]{:S(2)}) %collective-permute-start.105) | collective-permute-done | bytes 196640 | tf_op jit(solution)/shard_map/ppermute | solution.py:84
  103.2 1.6 %collective-permute-start.102 = (f32[128,384]{1,0:T(8,128)S(1)}, f32[128,384]{1,0:T(8,128)S(1)}, u32[]{:S(2)}, u32[]{:S(2)}) collective-permute-start(f32[128,384]{1,0:T(8,128)S(1)} %fusion.14), channel_id=1, source_target_pairs={{0,1},{1,0},{2,3},{3,2},{4,5},{5,4},{6,7},{7,6},{8,9},{9,8},{10,11... | collective-permute-start | bytes 589832 | tf_op jit(solution)/shard_map/ppermute | solution.py:84
  104.8 2.2 %convolution_convert_fusion = bf16[384,2048]{1,0:T(8,128)(2,1)} fusion(bf16[512,2048]{1,0:T(8,128)(2,1)S(1)} %constant_dynamic-update-slice_fusion, bf16[256,384]{1,0:T(8,128)(2,1)S(1)} %copy-done.7, bf16[256,384]{1,0:T(8,128)(2,1)S(1)} %copy-done.5), kind=kOutput, calls=%fused_computation.48 | convolution fusion | flops 806879232 | bytes 4063232 | tf_op jit(solution)/shard_map/rw,rv->wv/dot_general | solution.py:152
  107.0 2.9 %collective-permute-done.102 = f32[128,384]{1,0:T(8,128)S(1)} collective-permute-done((f32[128,384]{1,0:T(8,128)S(1)}, f32[128,384]{1,0:T(8,128)S(1)}, u32[]{:S(2)}, u32[]{:S(2)}) %collective-permute-start.102) | collective-permute-done | bytes 196640 | tf_op jit(solution)/shard_map/ppermute | solution.py:84
  (74 shorter events, 14.5 us)
Async XLA Ops:
  0.6 2.2 %copy-start = (bf16[384,2048]{1,0:T(8,128)(2,1)S(1)}, bf16[384,2048]{1,0:T(8,128)(2,1)}, u32[]{:S(2)}) copy-start(bf16[384,2048]{1,0:T(8,128)(2,1)} %param.101) | copy-start | bytes 4718596
  2.9 1.9 %copy-start.4 = (bf16[256,384]{1,0:T(8,128)(2,1)}, bf16[256,384]{1,0:T(8,128)(2,1)S(1)}, u32[]{:S(2)}) copy-start(bf16[256,384]{1,0:T(8,128)(2,1)S(1)} %convolution_convert_fusion.4) | copy-start | bytes 589828
  2.9 2.4 %copy-start.9 = (bf16[2,256,384]{2,1,0:T(8,128)(2,1)S(1)}, bf16[2,256,384]{2,1,0:T(8,128)(2,1)}, u32[]{:S(2)}) copy-start(bf16[2,256,384]{2,1,0:T(8,128)(2,1)} %param.100) | copy-start | bytes 1179652
  3.6 1.7 %copy-start.3 = (f32[256,2048]{1,0:T(8,128)}, f32[256,2048]{1,0:T(8,128)S(1)}, u32[]{:S(2)}) copy-start(f32[256,2048]{1,0:T(8,128)S(1)} %fusion.47) | copy-start | bytes 6291460
  4.8 13.2 %collective-permute-start.92 = (f32[2,64,2048]{2,1,0:T(8,128)}, f32[2,64,2048]{2,1,0:T(8,128)}, u32[]{:S(2)}, u32[]{:S(2)}) collective-permute-start(f32[2,64,2048]{2,1,0:T(8,128)} %slice_bitcast_fusion.2), channel_id=1, source_target_pairs={{0,2},{2,0},{4,6},{6,4},{8,10},{10,8},{12,14},{14,12},{16,18},{18,... | collective-permute-start | bytes 3145736 | tf_op jit(solution)/shard_map/ppermute | solution.py:84
  5.6 0.7 copy-start.6
  6.3 1.3 %copy-start.1 = (f32[256,2048]{1,0:T(8,128)}, f32[256,2048]{1,0:T(8,128)S(1)}, u32[]{:S(2)}) copy-start(f32[256,2048]{1,0:T(8,128)S(1)} %fusion.48) | copy-start | bytes 6291460
  7.7 14.6 %collective-permute-start.99 = (f32[2,64,2048]{2,1,0:T(8,128)S(1)}, f32[2,64,2048]{2,1,0:T(8,128)}, u32[]{:S(2)}, u32[]{:S(2)}) collective-permute-start(f32[2,64,2048]{2,1,0:T(8,128)S(1)} %slice_bitcast_fusion), channel_id=1, source_target_pairs={{0,2},{2,0},{4,6},{6,4},{8,10},{10,8},{12,14},{14,12},{16,18},{18,... | collective-permute-start | bytes 3145736 | tf_op jit(solution)/shard_map/ppermute | solution.py:84
  14.0 8.3 %copy-start.2 = (f32[256,2048]{1,0:T(8,128)S(1)}, f32[256,2048]{1,0:T(8,128)}, u32[]{:S(2)}) copy-start(f32[256,2048]{1,0:T(8,128)} %copy-done.1) | copy-start | bytes 6291460
  19.7 9.8 %collective-permute-start.93 = (bf16[64,2048]{1,0:T(8,128)(2,1)S(1)}, bf16[64,2048]{1,0:T(8,128)(2,1)S(1)}, u32[]{:S(2)}, u32[]{:S(2)}) collective-permute-start(bf16[64,2048]{1,0:T(8,128)(2,1)S(1)} %get-tuple-element.689), channel_id=1, source_target_pairs={{0,4},{2,6},{4,0},{6,2},{8,12},{10,14},{12,8},{14,10},{16,20},{18,... | collective-permute-start | bytes 786440 | tf_op jit(solution)/shard_map/ppermute | solution.py:84
  24.4 36.2 %collective-permute-start.100 = (bf16[64,2048]{1,0:T(8,128)(2,1)}, bf16[64,2048]{1,0:T(8,128)(2,1)S(1)}, u32[]{:S(2)}, u32[]{:S(2)}) collective-permute-start(bf16[64,2048]{1,0:T(8,128)(2,1)} %get-tuple-element.691), channel_id=1, source_target_pairs={{0,4},{2,6},{4,0},{6,2},{8,12},{10,14},{12,8},{14,10},{16,20},{18,... | collective-permute-start | bytes 786440 | tf_op jit(solution)/shard_map/ppermute | solution.py:84
  29.5 1.4 %collective-permute-start.47 = (bf16[64,2048]{1,0:T(8,128)(2,1)S(1)}, bf16[64,2048]{1,0:T(8,128)(2,1)}, u32[]{:S(2)}, u32[]{:S(2)}) collective-permute-start(bf16[64,2048]{1,0:T(8,128)(2,1)S(1)} %broadcast_select_fusion.2), channel_id=1, source_target_pairs={{0,0},{2,2},{4,4},{6,6},{8,16},{10,18},{12,20},{14,22},{16,8},{18,... | collective-permute-start | bytes 786440 | tf_op jit(solution)/shard_map/cond/branch_2_fun/ppermute | solution.py:76
  31.6 23.2 %collective-permute-start.19 = (bf16[64,2048]{1,0:T(8,128)(2,1)}, bf16[64,2048]{1,0:T(8,128)(2,1)S(1)}, u32[]{:S(2)}, u32[]{:S(2)}) collective-permute-start(bf16[64,2048]{1,0:T(8,128)(2,1)} %param.20), channel_id=1, source_target_pairs={{0,24},{2,26},{4,28},{6,30},{8,8},{10,10},{12,12},{14,14},{16,0},{... | collective-permute-start | bytes 786440 | tf_op jit(solution)/shard_map/cond/branch_20_fun/ppermute | solution.py:76
  57.3 28.5 %collective-permute-start.96 = (bf16[64,2048]{1,0:T(8,128)(2,1)}, bf16[64,2048]{1,0:T(8,128)(2,1)}, u32[]{:S(2)}, u32[]{:S(2)}) collective-permute-start(bf16[64,2048]{1,0:T(8,128)(2,1)} %multiply_convert_fusion.2), channel_id=1, source_target_pairs={{0,4},{2,6},{4,0},{6,2},{8,12},{10,14},{12,8},{14,10},{16,20},{18,... | collective-permute-start | bytes 786440 | tf_op jit(solution)/shard_map/ppermute | solution.py:84
  60.6 23.0 %collective-permute-start.94 = (bf16[64,2048]{1,0:T(8,128)(2,1)S(1)}, bf16[64,2048]{1,0:T(8,128)(2,1)S(1)}, u32[]{:S(2)}, u32[]{:S(2)}) collective-permute-start(bf16[64,2048]{1,0:T(8,128)(2,1)S(1)} %get-tuple-element.687), channel_id=1, source_target_pairs={{0,2},{2,0},{4,6},{6,4},{8,10},{10,8},{12,14},{14,12},{16,18},{18,... | collective-permute-start | bytes 786440 | tf_op jit(solution)/shard_map/ppermute | solution.py:84
  60.6 1.4 %collective-permute-start.71 = (bf16[64,2048]{1,0:T(8,128)(2,1)S(1)}, bf16[64,2048]{1,0:T(8,128)(2,1)}, u32[]{:S(2)}, u32[]{:S(2)}) collective-permute-start(bf16[64,2048]{1,0:T(8,128)(2,1)S(1)} %broadcast_select_fusion.27), channel_id=1, source_target_pairs={{0,0},{2,2},{4,4},{6,6},{8,16},{10,18},{12,20},{14,22},{16,24},{18... | collective-permute-start | bytes 786440 | tf_op jit(solution)/shard_map/cond/branch_3_fun/ppermute | solution.py:76
  62.1 19.5 %collective-permute-start.30 = (bf16[64,2048]{1,0:T(8,128)(2,1)S(1)}, bf16[64,2048]{1,0:T(8,128)(2,1)S(1)}, u32[]{:S(2)}, u32[]{:S(2)}) collective-permute-start(bf16[64,2048]{1,0:T(8,128)(2,1)S(1)} %param.56), channel_id=1, source_target_pairs={{0,8},{2,10},{4,12},{6,14},{8,16},{10,18},{12,20},{14,22},{16,0},{... | collective-permute-start | bytes 786440 | tf_op jit(solution)/shard_map/cond/branch_8_fun/ppermute | solution.py:76
  81.8 4.0 %copy-start.8 = (bf16[512,2048]{1,0:T(8,128)(2,1)S(1)}, bf16[512,2048]{1,0:T(8,128)(2,1)}, u32[]{:S(2)}) copy-start(bf16[512,2048]{1,0:T(8,128)(2,1)} %get-tuple-element.686) | copy-start | bytes 6291460
  81.9 7.4 %collective-permute-start.103 = (bf16[64,2048]{1,0:T(8,128)(2,1)S(1)}, bf16[64,2048]{1,0:T(8,128)(2,1)S(1)}, u32[]{:S(2)}, u32[]{:S(2)}) collective-permute-start(bf16[64,2048]{1,0:T(8,128)(2,1)S(1)} %multiply_convert_fusion), channel_id=1, source_target_pairs={{0,4},{2,6},{4,0},{6,2},{8,12},{10,14},{12,8},{14,10},{16,20},{18,... | collective-permute-start | bytes 786440 | tf_op jit(solution)/shard_map/ppermute | solution.py:84
  84.2 5.7 %collective-permute-start.95 = (f32[128,384]{1,0:T(8,128)S(1)}, f32[128,384]{1,0:T(8,128)S(1)}, u32[]{:S(2)}, u32[]{:S(2)}) collective-permute-start(f32[128,384]{1,0:T(8,128)S(1)} %fusion.6), channel_id=1, source_target_pairs={{0,1},{1,0},{2,3},{3,2},{4,5},{5,4},{6,7},{7,6},{8,9},{9,8},{10,11... | collective-permute-start | bytes 589832 | tf_op jit(solution)/shard_map/ppermute | solution.py:84
  85.7 4.2 %collective-permute-start.97 = (bf16[64,2048]{1,0:T(8,128)(2,1)}, bf16[64,2048]{1,0:T(8,128)(2,1)S(1)}, u32[]{:S(2)}, u32[]{:S(2)}) collective-permute-start(bf16[64,2048]{1,0:T(8,128)(2,1)} %collective-permute-done.96), channel_id=1, source_target_pairs={{0,2},{2,0},{4,6},{6,4},{8,10},{10,8},{12,14},{14,12},{16,18},{18,... | collective-permute-start | bytes 786440 | tf_op jit(solution)/shard_map/ppermute | solution.py:84
  89.3 4.9 %collective-permute-start.104 = (bf16[64,2048]{1,0:T(8,128)(2,1)S(1)}, bf16[64,2048]{1,0:T(8,128)(2,1)S(1)}, u32[]{:S(2)}, u32[]{:S(2)}) collective-permute-start(bf16[64,2048]{1,0:T(8,128)(2,1)S(1)} %collective-permute-done.103), channel_id=1, source_target_pairs={{0,2},{2,0},{4,6},{6,4},{8,10},{10,8},{12,14},{14,12},{16,18},{18,... | collective-permute-start | bytes 786440 | tf_op jit(solution)/shard_map/ppermute | solution.py:84
  91.5 7.0 %collective-permute-start.98 = (f32[128,384]{1,0:T(8,128)S(1)}, f32[128,384]{1,0:T(8,128)S(1)}, u32[]{:S(2)}, u32[]{:S(2)}) collective-permute-start(f32[128,384]{1,0:T(8,128)S(1)} %fusion.10), channel_id=1, source_target_pairs={{0,1},{1,0},{2,3},{3,2},{4,5},{5,4},{6,7},{7,6},{8,9},{9,8},{10,11... | collective-permute-start | bytes 589832 | tf_op jit(solution)/shard_map/ppermute | solution.py:84
  94.2 8.4 %collective-permute-start.101 = (bf16[64,2048]{1,0:T(8,128)(2,1)S(1)}, bf16[64,2048]{1,0:T(8,128)(2,1)S(1)}, u32[]{:S(2)}, u32[]{:S(2)}) collective-permute-start(bf16[64,2048]{1,0:T(8,128)(2,1)S(1)} %get-tuple-element.685), channel_id=1, source_target_pairs={{0,2},{2,0},{4,6},{6,4},{8,10},{10,8},{12,14},{14,12},{16,18},{18,... | collective-permute-start | bytes 786440 | tf_op jit(solution)/shard_map/ppermute | solution.py:84
  94.9 7.7 %collective-permute-start.105 = (f32[128,384]{1,0:T(8,128)S(1)}, f32[128,384]{1,0:T(8,128)S(1)}, u32[]{:S(2)}, u32[]{:S(2)}) collective-permute-start(f32[128,384]{1,0:T(8,128)S(1)} %fusion.18), channel_id=1, source_target_pairs={{0,1},{1,0},{2,3},{3,2},{4,5},{5,4},{6,7},{7,6},{8,9},{9,8},{10,11... | collective-permute-start | bytes 589832 | tf_op jit(solution)/shard_map/ppermute | solution.py:84
  98.9 5.9 %copy-start.5 = (bf16[256,384]{1,0:T(8,128)(2,1)S(1)}, bf16[256,384]{1,0:T(8,128)(2,1)}, u32[]{:S(2)}) copy-start(bf16[256,384]{1,0:T(8,128)(2,1)} %copy-done.4) | copy-start | bytes 589828
  98.9 5.9 %copy-start.7 = (bf16[256,384]{1,0:T(8,128)(2,1)S(1)}, bf16[256,384]{1,0:T(8,128)(2,1)}, u32[]{:S(2)}) copy-start(bf16[256,384]{1,0:T(8,128)(2,1)} %copy-done.6) | copy-start | bytes 589828
  103.2 6.7 %collective-permute-start.102 = (f32[128,384]{1,0:T(8,128)S(1)}, f32[128,384]{1,0:T(8,128)S(1)}, u32[]{:S(2)}, u32[]{:S(2)}) collective-permute-start(f32[128,384]{1,0:T(8,128)S(1)} %fusion.14), channel_id=1, source_target_pairs={{0,1},{1,0},{2,3},{3,2},{4,5},{5,4},{6,7},{7,6},{8,9},{9,8},{10,11... | collective-permute-start | bytes 589832 | tf_op jit(solution)/shard_map/ppermute | solution.py:84

commit v2 on v1

--- a/solution.py
+++ b/solution.py
@@ -95,6 +95,10 @@
     return lax.psum(block, axis)
 
 
+def after(block, *others):
+    return lax.optimization_barrier((block, *others))[0]
+
+
 def paired_body(states, head_weight, pair_order, row_example):
     micro_count, row_count, half_width = states.shape
     place = lax.axis_index("rep")
@@ -105,51 +109,85 @@
     local = jnp.arange(row_count, dtype=jnp.int32)
     block = local // quarter
     example_of = (
-        (side ^ (block & 1)) * (2 * quarter) + (parity ^ (block >> 1)) * quarter + local % quarter
+        (side ^ (block >> 1)) * (2 * quarter) + (parity ^ (block & 1)) * quarter + local % quarter
     )
     examples = lax.dynamic_index_in_dim(row_example, replica, 1, keepdims=False)
     onehot = (examples[:, None, :] == example_of[None, :, None]).astype(jnp.bfloat16)
-    branch, sides = routes(pair_order)
+
+    ordered, homes, fars = [], [], []
+    for m in range(micro_count):
+        rows = jnp.dot(onehot[m], states[m], preferred_element_type=jnp.float32)
+        rows = rows.astype(jnp.bfloat16)
+        ordered.append(rows)
+        theirs = jnp.dot(rows[2 * quarter :], head_weight, preferred_element_type=jnp.float32)
+        arrived = swap(theirs, "rep", 1)
+        own = jnp.dot(rows[: 2 * quarter], head_weight, preferred_element_type=jnp.float32)
+        fars.append((own[quarter:] + arrived[quarter:]).astype(jnp.bfloat16))
+        homes.append((own[:quarter] + arrived[:quarter]).astype(jnp.bfloat16))
+    sibs = []
+    for m in range(micro_count):
+        sibs.append(swap(after(fars[m], *sibs), "rep", 2))
+    branch, sides = routes(after(pair_order, homes[0], fars[0]))
     mine = lax.dynamic_index_in_dim(sides, pair, 2, keepdims=False)
 
-    ordered, homes, sibs = [], [], []
-    for m in range(micro_count):
-        rows = jnp.dot(onehot[m], states[m], preferred_element_type=jnp.float32)
-        ordered.append(rows.astype(jnp.bfloat16))
-        partial = jnp.dot(ordered[m], head_weight, preferred_element_type=jnp.float32)
-        partial = partial.reshape(2, 2, quarter, -1)
-        logits = (partial[:, 0] + swap(partial[:, 1], "rep", 1)).astype(jnp.bfloat16)
-        homes.append(logits[0])
-        sibs.append(swap(logits[1], "rep", 2))
-
-    head_parts, state_parts = [], []
+    grads_home, grads_sib, grads_far, nears, farthers = [], [], [], [], []
     for m in range(micro_count):
         home, sib = homes[m], sibs[m]
         home_first = mine[m, 0] == parity
-        first = move_pairs(jnp.where(home_first, home, sib), branch[m, 0], pairs)
-        second = move_pairs(jnp.where(home_first, sib, home), branch[m, 1], pairs)
+        sent_first = jnp.where(home_first, home, sib)
+        sent_second = jnp.where(home_first, sib, home)
+        if m > 0:
+            sent_first = after(sent_first, grads_home[-1], grads_sib[-1])
+        first = move_pairs(sent_first, branch[m, 0], pairs)
+        second = move_pairs(after(sent_second, first), branch[m, 1], pairs)
         to_home_first = mine[m, 1] == parity
-        grad_home = difference(home, jnp.where(to_home_first, first, second))
-        grad_sib = difference(sib, jnp.where(to_home_first, second, first))
-        near = jnp.concatenate([grad_home, swap(grad_home, "rep", 1)], axis=0)
-        grad_far = swap(grad_sib, "rep", 2)
-        far = jnp.concatenate([grad_far, swap(grad_far, "rep", 1)], axis=0)
-        states_here = []
-        for part, gradient in enumerate((near, far)):
-            rows = ordered[m][part * 2 * quarter : (part + 1) * 2 * quarter]
-            head_parts.append((rows, gradient))
-            back = jnp.einsum(
-                "rv,wv->rw", gradient, head_weight, preferred_element_type=jnp.float32
+        grads_sib.append(difference(sib, jnp.where(to_home_first, second, first)))
+        grads_home.append(difference(home, jnp.where(to_home_first, first, second)))
+        grads_far.append(swap(grads_sib[m], "rep", 2))
+        nears.append(swap(grads_home[m], "rep", 1))
+        farthers.append(swap(grads_far[m], "rep", 1))
+
+    state_blocks = [[None] * 4 for _ in range(micro_count)]
+
+    def back(gradient):
+        partial = jnp.einsum(
+            "rv,wv->rw", gradient, head_weight, preferred_element_type=jnp.float32
+        )
+        return partial, swap(partial.astype(jnp.bfloat16), "voc", 1)
+
+    held = []
+    for part in range(2):
+        for m in range(micro_count):
+            here, there = ((grads_home, nears), (grads_far, farthers))[part]
+            gradient = jnp.concatenate([here[m], there[m]], axis=0)
+            partial, sent = back(gradient)
+            held.append((m, part, gradient, partial, sent))
+    state_parts = []
+    for m in range(micro_count):
+        summed = [None, None]
+        for at, part, gradient, partial, sent in held:
+            if at == m:
+                summed[part] = (partial + sent.astype(jnp.float32)).astype(jnp.bfloat16)
+        canon = [summed[0][:quarter], summed[1][:quarter], summed[0][quarter:], summed[1][quarter:]]
+        state_parts.append(
+            jnp.einsum(
+                "ei,ew->iw",
+                onehot[m],
+                jnp.concatenate(canon, axis=0),
+                preferred_element_type=jnp.float32,
             )
-            states_here.append(sum_over(back, "voc").astype(jnp.bfloat16))
-        state_canon = jnp.concatenate(states_here, axis=0)
-        state_parts.append(
-            jnp.einsum("ei,ew->iw", onehot[m], state_canon, preferred_element_type=jnp.float32)
         )
     state_grad = jnp.stack(state_parts).astype(jnp.bfloat16)
-    rows = jnp.concatenate([r for r, _ in head_parts], axis=0)
-    gradient = jnp.concatenate([g for _, g in head_parts], axis=0)
-    head_grad = jnp.einsum("rw,rv->wv", rows, gradient, preferred_element_type=jnp.float32)
+    rows, gradients = [], []
+    for m, part, gradient, _, _ in held:
+        rows += [ordered[m][(2 * b + part) * quarter : (2 * b + part + 1) * quarter] for b in range(2)]
+        gradients.append(gradient)
+    head_grad = jnp.einsum(
+        "rw,rv->wv",
+        jnp.concatenate(rows, axis=0),
+        jnp.concatenate(gradients, axis=0),
+        preferred_element_type=jnp.float32,
+    )
     return state_grad, head_grad.astype(jnp.bfloat16)
 
 
@@ -196,6 +234,7 @@
 def solution(mesh):
     replicas = mesh.shape["rep"] // 2
     few = replicas % 2 == 0 and math.factorial(replicas // 2) <= max_branches
+    few = few and mesh.shape["voc"] == 2
     return jax.shard_map(
         paired_body if few else spread_body,
         mesh=mesh,

time: 109 us -> 108 us (level); the launches traced: 111 us -> 108 us
  waiting for transfers between devices: 43.3 us -> 32.5 us
  matrix products: 8.89 us -> 13.3 us
  local copies, waits for them, and re-layouts: 9.1 us -> 11.4 us
    ppermute x4, waiting for transfers between devices: 25.4 us -> 19.8 us  [one(): return lax.ppermute(moved, 'rep', route)]
    ppermute x14, waiting for transfers between devices: 17.9 us -> 12.7 us  [swap(): return lax.ppermute(block, axis, [(i, i ^ bit) for i in range(count)])]
    dot_general x9 -> x11, matrix products: 7.47 us -> 11.9 us  [the longest x4 3.42 us: back(): jnp.einsum('rv,wv->rw', gradient, head_weight, preferred_element_type=jnp...]
    unnamed x26 -> x27, local copies, waits for them, and re-layouts: 2.5 us -> 6.84 us
    squeeze x4 -> x0, local copies, waits for them, and re-layouts: 2.03 us -> none  [the longest x2 1.24 us: paired_body(): partial[:, 1]]
    ppermute x4, starting transfers between devices: 19.9 us -> 21.9 us  [one(): return lax.ppermute(moved, 'rep', route)]
    unnamed x2, other arithmetic: 2.87 us -> 1.76 us
  transfers between devices with their start and end apart: 18 -> 18, of which waited for: 8 -> 9; matrix products, arithmetic and copies ran while one was open for 18% -> 25% of each run, Pallas kernels for 2% -> 2%
where the time goes in v2:
time: 108 us
  starting transfers between devices  33.1 us (31%)
  waiting for transfers between devices  32.5 us (30%)
  matrix products  13.3 us (12%)
  local copies, waits for them, and re-layouts  11.4 us (11%)
  other arithmetic  9.24 us (9%)
  between operations  5.99 us (6%)
  Pallas kernels  1.69 us (2%)
    ppermute x4, starting transfers between devices, one(): return lax.ppermute(moved, 'rep', route)  21.9 us
    ppermute x4, waiting for transfers between devices, one(): return lax.ppermute(moved, 'rep', route)  19.8 us
    ppermute x14, waiting for transfers between devices, swap(): return lax.ppermute(block, axis, [(i, i ^ bit) for i in range(count)])  12.7 us
    ppermute x14, starting transfers between devices, swap(): return lax.ppermute(block, axis, [(i, i ^ bit) for i in range(count)])  11.2 us
    unnamed x27, local copies, waits for them, and re-layouts  6.84 us
    dot_general x4, matrix products, back(): jnp.einsum('rv,wv->rw', gradient, head_weight, preferred_element_type=jnp...  3.42 us
    dot_general x1, matrix products, paired_body(): jnp.einsum('rw,rv->wv', jnp.concatenate(rows, axis=0), jnp.concatenate(gr...  3.16 us
    dot_general x2, matrix products, paired_body(): jnp.dot(rows[2 * quarter:], head_weight, preferred_element_type=jnp.float32)  2.86 us
  transfers between devices with their start and end apart: 18, of which 9 were waited for; matrix products, arithmetic and copies ran while one was open for 25% of the time, Pallas kernels for 2%

profile of v2, /device:TPU:0, one launch (start us, length us, event | category | flops | bytes accessed | tf_op | source)
XLA Modules:
  0.0 107.6 jit_solution(5850266290593262560)
XLA Ops:
  1.7 1.2 %convolution_convert_fusion.4 = bf16[256,384]{1,0:T(8,128)(2,1)S(1)} fusion(pred[2,256,256]{2,1,0:T(32,128)(4,1)S(1)} %broadcast_compare_fusion, bf16[2,256,384]{2,1,0:T(8,128)(2,1)} %param.100), kind=kOutput, calls=%fused_computation.4 | convolution fusion | flops 50429952 | bytes 458752 | tf_op jit(solution)/shard_map/dot_general | solution.py:119
  2.9 1.4 %fusion.44 = f32[128,2048]{1,0:T(8,128)} fusion(bf16[384,2048]{1,0:T(8,128)(2,1)S(1)} %copy-done, bf16[256,384]{1,0:T(8,128)(2,1)S(1)} %convolution_convert_fusion.4), kind=kOutput, calls=%fused_computation.69 | convolution fusion | flops 201326592 | bytes 2719744 | tf_op jit(solution)/shard_map/dot_general | solution.py:122
  5.1 1.4 %fusion.40 = f32[128,2048]{1,0:T(8,128)} fusion(bf16[384,2048]{1,0:T(8,128)(2,1)S(1)} %copy-done, bf16[256,384]{1,0:T(8,128)(2,1)S(1)} %convolution_convert_fusion.2), kind=kOutput, calls=%fused_computation.65 | convolution fusion | flops 201326592 | bytes 2719744 | tf_op jit(solution)/shard_map/dot_general | solution.py:122
  12.0 1.4 %fusion.42 = f32[128,2048]{1,0:T(8,128)} fusion(bf16[384,2048]{1,0:T(8,128)(2,1)S(1)} %copy-done, bf16[256,384]{1,0:T(8,128)(2,1)S(1)} %convolution_convert_fusion.2), kind=kOutput, calls=%fused_computation.67 | convolution fusion | flops 201326592 | bytes 2719744 | tf_op jit(solution)/shard_map/dot_general | solution.py:124
  13.4 1.3 %fusion.5 = (bf16[64,2048]{1,0:T(8,128)(2,1)S(1)}, bf16[64,2048]{1,0:T(8,128)(2,1)S(1)}) fusion(f32[128,2048]{1,0:T(8,128)} %collective-permute-done.92, f32[128,2048]{1,0:T(8,128)S(1)} %fusion.46), kind=kLoop, calls=%fused_computation.14 | loop fusion | flops 524288 | bytes 2621440 | tf_op jit(solution)/shard_map/convert_element_type | solution.py:126
  14.7 1.7 %shard_map.59 = (s32[2,2]{1,0:T(2,128)}, s32[2,2,4]{2,1,0:T(2,128)}) custom-call(s32[2,8]{1,0:T(2,128)} %order_ref), custom_call_target="tpu_custom_call" | custom-call | tf_op jit(solution)/shard_map/pallas_call | solution.py:59
  18.6 3.0 %collective-permute-start.93 = (bf16[64,2048]{1,0:T(8,128)(2,1)S(1)}, bf16[64,2048]{1,0:T(8,128)(2,1)S(1)}, u32[]{:S(2)}, u32[]{:S(2)}) collective-permute-start(bf16[64,2048]{1,0:T(8,128)(2,1)S(1)} %get-tuple-element.219), channel_id=1, source_target_pairs={{0,4},{2,6},{4,0},{6,2},{8,12},{10,14},{12,8},{14,10},{16,20},{18,... | collective-permute-start | bytes 786440 | tf_op jit(solution)/shard_map/ppermute | solution.py:84
  21.6 1.5 %fusion.63 = (s32[1,1]{1,0:T(1,128)}, s32[1,1]{1,0:T(1,128)}, s32[1,1]{1,0:T(1,128)}, s32[1,1]{1,0:T(1,128)}) fusion(s32[2,2]{1,0:T(2,128)} %get-tuple-element.207), kind=kLoop, calls=%fused_computation.111 | loop fusion | bytes 32 | tf_op jit(solution)/shard_map/slice | solution.py:142
  27.4 2.0 %fusion.2 = bf16[64,2048]{1,0:T(8,128)(2,1)} fusion(f32[128,2048]{1,0:T(8,128)} %collective-permute-done.99, f32[128,2048]{1,0:T(8,128)} %fusion.42), kind=kLoop, calls=%fused_computation.8 | loop fusion | flops 262144 | bytes 1310720 | tf_op jit(solution)/shard_map/convert_element_type | solution.py:125
  30.1 9.9 %conditional.4 = (bf16[64,2048]{1,0:T(8,128)(2,1)S(1)}) conditional(s32[]{:T(128)} %bitcast.3, bf16[64,2048]{1,0:T(8,128)(2,1)S(1)} %get-tuple-element.221, bf16[64,2048]{1,0:T(8,128)(2,1)S(1)} %get-tuple-element.221, bf16[64,2048]{1,0:T(8,128)(2,1)S(1)} %get-tuple-element.221, ...), branch_computations={%region_0.1_spmd, %region_1.2_spmd, %region_2.3_spmd, %region_3.4_... | conditional | bytes 1572912 | solution.py:79
  30.1 2.6 %collective-permute-start.16 = (bf16[64,2048]{1,0:T(8,128)(2,1)S(1)}, bf16[64,2048]{1,0:T(8,128)(2,1)S(1)}, u32[]{:S(2)}, u32[]{:S(2)}) collective-permute-start(bf16[64,2048]{1,0:T(8,128)(2,1)S(1)} %param.17), channel_id=1, source_target_pairs={{0,16},{2,18},{4,20},{6,22},{8,24},{10,26},{12,28},{14,30},{16,8},... | collective-permute-start | bytes 786440 | tf_op jit(solution)/shard_map/cond/branch_17_fun/ppermute | solution.py:76
  32.7 7.3 %collective-permute-done.16 = bf16[64,2048]{1,0:T(8,128)(2,1)S(1)} collective-permute-done((bf16[64,2048]{1,0:T(8,128)(2,1)S(1)}, bf16[64,2048]{1,0:T(8,128)(2,1)S(1)}, u32[]{:S(2)}, u32[]{:S(2)}) %collective-permute-start.16) | collective-permute-done | bytes 262176 | tf_op jit(solution)/shard_map/cond/branch_17_fun/ppermute | solution.py:76
  40.8 0.9 constant_dynamic-update-slice_fusion.7
  42.3 1.8 %multiply_convert_fusion.2 = bf16[64,2048]{1,0:T(8,128)(2,1)} fusion(bf16[64,2048]{1,0:T(8,128)(2,1)} %copy-done.5, bf16[64,2048]{1,0:T(8,128)(2,1)S(1)} %get-tuple-element.247, bf16[64,2048]{1,0:T(8,128)(2,1)S(1)} %get-tuple-element.246, pred[]{:T(512)S(6)} %eq.36), kind=kLoop, calls=%fused_computation.33 | loop fusion | flops 786432 | bytes 1048577 | tf_op jit(solution)/shard_map/convert_element_type | solution.py:89
  44.1 1.5 %collective-permute-start.96 = (bf16[64,2048]{1,0:T(8,128)(2,1)}, bf16[64,2048]{1,0:T(8,128)(2,1)S(1)}, u32[]{:S(2)}, u32[]{:S(2)}) collective-permute-start(bf16[64,2048]{1,0:T(8,128)(2,1)} %multiply_convert_fusion.2), channel_id=1, source_target_pairs={{0,4},{2,6},{4,0},{6,2},{8,12},{10,14},{12,8},{14,10},{16,20},{18,... | collective-permute-start | bytes 786440 | tf_op jit(solution)/shard_map/ppermute | solution.py:84
  45.6 5.5 %collective-permute-done.100 = bf16[64,2048]{1,0:T(8,128)(2,1)S(1)} collective-permute-done((bf16[64,2048]{1,0:T(8,128)(2,1)}, bf16[64,2048]{1,0:T(8,128)(2,1)S(1)}, u32[]{:S(2)}, u32[]{:S(2)}) %collective-permute-start.100) | collective-permute-done | bytes 262176 | tf_op jit(solution)/shard_map/ppermute | solution.py:84
  51.1 1.2 %broadcast_select_fusion.1 = (bf16[64,2048]{1,0:T(8,128)(2,1)S(1)}, bf16[64,2048]{1,0:T(8,128)(2,1)S(1)}) fusion(bf16[64,2048]{1,0:T(8,128)(2,1)S(1)} %collective-permute-done.100, pred[]{:T(512)S(6)} %eq.39, f32[128,2048]{1,0:T(8,128)} %collective-permute-done.99, f32[128,2048]{1,0:T(8,128)S(1)} %copy-done.1), kind=kLoop, calls=%fused_computation.40 | loop fusion | flops 393216 | bytes 1835009 | tf_op jit(solution)/shard_map/jit(_where)/select_n | solution.py:137
  52.3 24.4 %conditional.6 = (bf16[64,2048]{1,0:T(8,128)(2,1)S(1)}) conditional(s32[]{:T(128)} %bitcast.10, bf16[64,2048]{1,0:T(8,128)(2,1)S(1)} %get-tuple-element.210, bf16[64,2048]{1,0:T(8,128)(2,1)S(1)} %get-tuple-element.210, bf16[64,2048]{1,0:T(8,128)(2,1)S(1)} %get-tuple-element.210, ...), branch_computations={%region_48.49_spmd, %region_49.50_spmd, %region_50.51_spmd, %regio... | conditional | bytes 1572912 | solution.py:79
  52.4 17.6 %collective-permute-start.53 = (bf16[64,2048]{1,0:T(8,128)(2,1)S(1)}, bf16[64,2048]{1,0:T(8,128)(2,1)S(1)}, u32[]{:S(2)}, u32[]{:S(2)}) collective-permute-start(bf16[64,2048]{1,0:T(8,128)(2,1)S(1)} %param.56), channel_id=1, source_target_pairs={{0,8},{2,10},{4,12},{6,14},{8,16},{10,18},{12,20},{14,22},{16,0},{... | collective-permute-start | bytes 786440 | tf_op jit(solution)/shard_map/cond/branch_8_fun/ppermute | solution.py:76
  70.0 6.5 %collective-permute-done.53 = bf16[64,2048]{1,0:T(8,128)(2,1)S(1)} collective-permute-done((bf16[64,2048]{1,0:T(8,128)(2,1)S(1)}, bf16[64,2048]{1,0:T(8,128)(2,1)S(1)}, u32[]{:S(2)}, u32[]{:S(2)}) %collective-permute-start.53) | collective-permute-done | bytes 262176 | tf_op jit(solution)/shard_map/cond/branch_8_fun/ppermute | solution.py:76
  76.8 7.1 %conditional.7 = (bf16[64,2048]{1,0:T(8,128)(2,1)S(1)}) conditional(s32[]{:T(128)} %bitcast.12, bf16[64,2048]{1,0:T(8,128)(2,1)S(1)} %broadcast_select_fusion, bf16[64,2048]{1,0:T(8,128)(2,1)S(1)} %broadcast_select_fusion, bf16[64,2048]{1,0:T(8,128)(2,1)S(1)} %broadcast_select_fusion, ...), branch_computations={%region_72.73_spmd, %region_73.74_spmd, %region_74.75_spmd, %regio... | conditional | bytes 1572912 | solution.py:79
  76.9 1.1 collective-permute-start.75
  77.9 5.9 %collective-permute-done.75 = bf16[64,2048]{1,0:T(8,128)(2,1)S(1)} collective-permute-done((bf16[64,2048]{1,0:T(8,128)(2,1)S(1)}, bf16[64,2048]{1,0:T(8,128)(2,1)S(1)}, u32[]{:S(2)}, u32[]{:S(2)}) %collective-permute-start.75) | collective-permute-done | bytes 262176 | tf_op jit(solution)/shard_map/cond/branch_7_fun/ppermute | solution.py:76
  83.9 1.7 %constant_dynamic-update-slice_fusion.6 = bf16[512,2048]{1,0:T(8,128)(2,1)} fusion(bf16[512,2048]{1,0:T(8,128)(2,1)} %get-tuple-element.214, bf16[64,2048]{1,0:T(8,128)(2,1)} %collective-permute-done.94), kind=kLoop, calls=%fused_computation.87 | loop fusion | bytes 524288
  86.4 1.6 %fusion.67 = (bf16[128,384]{1,0:T(8,128)(2,1)S(1)}, f32[128,384]{1,0:T(8,128)S(1)}) fusion(bf16[384,2048]{1,0:T(8,128)(2,1)S(1)} %copy-done, bf16[64,2048]{1,0:T(8,128)(2,1)} %collective-permute-done.94, bf16[64,2048]{1,0:T(8,128)(2,1)} %get-tuple-element.215), kind=kOutput, calls=%fused_computation.115 | convolution fusion | flops 202424320 | bytes 2392064 | tf_op jit(solution)/shard_map/rv,wv->rw/dot_general | solution.py:153
  88.0 1.6 %collective-permute-start.95 = (bf16[128,384]{1,0:T(8,128)(2,1)S(1)}, bf16[128,384]{1,0:T(8,128)(2,1)S(1)}, u32[]{:S(2)}, u32[]{:S(2)}) collective-permute-start(bf16[128,384]{1,0:T(8,128)(2,1)S(1)} %get-tuple-element.244), channel_id=1, source_target_pairs={{0,1},{1,0},{2,3},{3,2},{4,5},{5,4},{6,7},{7,6},{8,9},{9,8},{10,11... | collective-permute-start | bytes 294920 | tf_op jit(solution)/shard_map/ppermute | solution.py:84
  90.3 3.0 %collective-permute-done.95 = bf16[128,384]{1,0:T(8,128)(2,1)S(1)} collective-permute-done((bf16[128,384]{1,0:T(8,128)(2,1)S(1)}, bf16[128,384]{1,0:T(8,128)(2,1)S(1)}, u32[]{:S(2)}, u32[]{:S(2)}) %collective-permute-start.95) | collective-permute-done | bytes 98336 | tf_op jit(solution)/shard_map/ppermute | solution.py:84
  94.0 1.6 %collective-permute-start.98 = (bf16[128,384]{1,0:T(8,128)(2,1)S(1)}, bf16[128,384]{1,0:T(8,128)(2,1)S(1)}, u32[]{:S(2)}, u32[]{:S(2)}) collective-permute-start(bf16[128,384]{1,0:T(8,128)(2,1)S(1)} %get-tuple-element.242), channel_id=1, source_target_pairs={{0,1},{1,0},{2,3},{3,2},{4,5},{5,4},{6,7},{7,6},{8,9},{9,8},{10,11... | collective-permute-start | bytes 294920 | tf_op jit(solution)/shard_map/ppermute | solution.py:84
  96.8 1.4 %collective-permute-done.103 = bf16[64,2048]{1,0:T(8,128)(2,1)S(1)} collective-permute-done((bf16[64,2048]{1,0:T(8,128)(2,1)S(1)}, bf16[64,2048]{1,0:T(8,128)(2,1)S(1)}, u32[]{:S(2)}, u32[]{:S(2)}) %collective-permute-start.103) | collective-permute-done | bytes 262176 | tf_op jit(solution)/shard_map/ppermute | solution.py:84
  99.2 1.7 %collective-permute-done.102 = bf16[128,384]{1,0:T(8,128)(2,1)S(1)} collective-permute-done((bf16[128,384]{1,0:T(8,128)(2,1)S(1)}, bf16[128,384]{1,0:T(8,128)(2,1)S(1)}, u32[]{:S(2)}, u32[]{:S(2)}) %collective-permute-start.102) | collective-permute-done | bytes 98336 | tf_op jit(solution)/shard_map/ppermute | solution.py:84
  101.8 1.3 %collective-permute-start.105 = (bf16[128,384]{1,0:T(8,128)(2,1)S(1)}, bf16[128,384]{1,0:T(8,128)(2,1)S(1)}, u32[]{:S(2)}, u32[]{:S(2)}) collective-permute-start(bf16[128,384]{1,0:T(8,128)(2,1)S(1)} %get-tuple-element.238), channel_id=1, source_target_pairs={{0,1},{1,0},{2,3},{3,2},{4,5},{5,4},{6,7},{7,6},{8,9},{9,8},{10,11... | collective-permute-start | bytes 294920 | tf_op jit(solution)/shard_map/ppermute | solution.py:84
  103.1 3.2 %convolution_convert_fusion = bf16[384,2048]{1,0:T(8,128)(2,1)} fusion(bf16[512,384]{1,0:T(8,128)(2,1)} %slice_dynamic-update-slice_fusion, bf16[512,2048]{1,0:T(8,128)(2,1)S(1)} %constant_dynamic-update-slice_fusion), kind=kOutput, calls=%fused_computation | convolution fusion | flops 806092800 | bytes 4063232 | tf_op jit(solution)/shard_map/rw,rv->wv/dot_general | solution.py:185
  (79 shorter events, 18.1 us)
Async XLA Ops:
  0.6 2.3 %copy-start = (bf16[384,2048]{1,0:T(8,128)(2,1)S(1)}, bf16[384,2048]{1,0:T(8,128)(2,1)}, u32[]{:S(2)}) copy-start(bf16[384,2048]{1,0:T(8,128)(2,1)} %param.101) | copy-start | bytes 4718596
  0.6 4.2 %copy-start.6 = (bf16[2,256,384]{2,1,0:T(8,128)(2,1)S(1)}, bf16[2,256,384]{2,1,0:T(8,128)(2,1)}, u32[]{:S(2)}) copy-start(bf16[2,256,384]{2,1,0:T(8,128)(2,1)} %param.100) | copy-start | bytes 1179652
  4.4 9.1 %collective-permute-start.92 = (f32[128,2048]{1,0:T(8,128)}, f32[128,2048]{1,0:T(8,128)}, u32[]{:S(2)}, u32[]{:S(2)}) collective-permute-start(f32[128,2048]{1,0:T(8,128)} %fusion.44), channel_id=1, source_target_pairs={{0,2},{2,0},{4,6},{6,4},{8,10},{10,8},{12,14},{14,12},{16,18},{18,... | collective-permute-start | bytes 3145736 | tf_op jit(solution)/shard_map/ppermute | solution.py:84
  6.5 21.0 %collective-permute-start.99 = (f32[128,2048]{1,0:T(8,128)}, f32[128,2048]{1,0:T(8,128)}, u32[]{:S(2)}, u32[]{:S(2)}) collective-permute-start(f32[128,2048]{1,0:T(8,128)} %fusion.40), channel_id=1, source_target_pairs={{0,2},{2,0},{4,6},{6,4},{8,10},{10,8},{12,14},{14,12},{16,18},{18,... | collective-permute-start | bytes 3145736 | tf_op jit(solution)/shard_map/ppermute | solution.py:84
  18.6 10.8 %collective-permute-start.93 = (bf16[64,2048]{1,0:T(8,128)(2,1)S(1)}, bf16[64,2048]{1,0:T(8,128)(2,1)S(1)}, u32[]{:S(2)}, u32[]{:S(2)}) collective-permute-start(bf16[64,2048]{1,0:T(8,128)(2,1)S(1)} %get-tuple-element.219), channel_id=1, source_target_pairs={{0,4},{2,6},{4,0},{6,2},{8,12},{10,14},{12,8},{14,10},{16,20},{18,... | collective-permute-start | bytes 786440 | tf_op jit(solution)/shard_map/ppermute | solution.py:84
  29.4 0.7 copy-start.5
  30.1 9.9 %collective-permute-start.16 = (bf16[64,2048]{1,0:T(8,128)(2,1)S(1)}, bf16[64,2048]{1,0:T(8,128)(2,1)S(1)}, u32[]{:S(2)}, u32[]{:S(2)}) collective-permute-start(bf16[64,2048]{1,0:T(8,128)(2,1)S(1)} %param.17), channel_id=1, source_target_pairs={{0,16},{2,18},{4,20},{6,22},{8,24},{10,26},{12,28},{14,30},{16,8},... | collective-permute-start | bytes 786440 | tf_op jit(solution)/shard_map/cond/branch_17_fun/ppermute | solution.py:76
  40.1 0.7 collective-permute-start.26
  40.8 10.3 %copy-start.1 = (f32[128,2048]{1,0:T(8,128)S(1)}, f32[128,2048]{1,0:T(8,128)}, u32[]{:S(2)}) copy-start(f32[128,2048]{1,0:T(8,128)} %fusion.42) | copy-start | bytes 3145732
  41.8 42.1 %collective-permute-start.94 = (bf16[64,2048]{1,0:T(8,128)(2,1)}, bf16[64,2048]{1,0:T(8,128)(2,1)}, u32[]{:S(2)}, u32[]{:S(2)}) collective-permute-start(bf16[64,2048]{1,0:T(8,128)(2,1)} %get-tuple-element.215), channel_id=1, source_target_pairs={{0,2},{2,0},{4,6},{6,4},{8,10},{10,8},{12,14},{14,12},{16,18},{18,... | collective-permute-start | bytes 786440 | tf_op jit(solution)/shard_map/ppermute | solution.py:84
  41.8 9.3 %collective-permute-start.100 = (bf16[64,2048]{1,0:T(8,128)(2,1)}, bf16[64,2048]{1,0:T(8,128)(2,1)S(1)}, u32[]{:S(2)}, u32[]{:S(2)}) collective-permute-start(bf16[64,2048]{1,0:T(8,128)(2,1)} %fusion.2), channel_id=1, source_target_pairs={{0,4},{2,6},{4,0},{6,2},{8,12},{10,14},{12,8},{14,10},{16,20},{18,... | collective-permute-start | bytes 786440 | tf_op jit(solution)/shard_map/ppermute | solution.py:84
  44.1 46.2 %collective-permute-start.96 = (bf16[64,2048]{1,0:T(8,128)(2,1)}, bf16[64,2048]{1,0:T(8,128)(2,1)S(1)}, u32[]{:S(2)}, u32[]{:S(2)}) collective-permute-start(bf16[64,2048]{1,0:T(8,128)(2,1)} %multiply_convert_fusion.2), channel_id=1, source_target_pairs={{0,4},{2,6},{4,0},{6,2},{8,12},{10,14},{12,8},{14,10},{16,20},{18,... | collective-permute-start | bytes 786440 | tf_op jit(solution)/shard_map/ppermute | solution.py:84
  51.1 1.2 %copy-start.3 = (bf16[64,2048]{1,0:T(8,128)(2,1)}, bf16[64,2048]{1,0:T(8,128)(2,1)S(1)}, u32[]{:S(2)}) copy-start(bf16[64,2048]{1,0:T(8,128)(2,1)S(1)} %collective-permute-done.100) | copy-start | bytes 786436
  52.3 24.4 %copy-start.4 = (bf16[64,2048]{1,0:T(8,128)(2,1)S(1)}, bf16[64,2048]{1,0:T(8,128)(2,1)}, u32[]{:S(2)}) copy-start(bf16[64,2048]{1,0:T(8,128)(2,1)} %copy-done.3) | copy-start | bytes 786436
  52.4 24.1 %collective-permute-start.53 = (bf16[64,2048]{1,0:T(8,128)(2,1)S(1)}, bf16[64,2048]{1,0:T(8,128)(2,1)S(1)}, u32[]{:S(2)}, u32[]{:S(2)}) collective-permute-start(bf16[64,2048]{1,0:T(8,128)(2,1)S(1)} %param.56), channel_id=1, source_target_pairs={{0,8},{2,10},{4,12},{6,14},{8,16},{10,18},{12,20},{14,22},{16,0},{... | collective-permute-start | bytes 786440 | tf_op jit(solution)/shard_map/cond/branch_8_fun/ppermute | solution.py:76
  76.9 7.0 %collective-permute-start.75 = (bf16[64,2048]{1,0:T(8,128)(2,1)S(1)}, bf16[64,2048]{1,0:T(8,128)(2,1)S(1)}, u32[]{:S(2)}, u32[]{:S(2)}) collective-permute-start(bf16[64,2048]{1,0:T(8,128)(2,1)S(1)} %param.79), channel_id=1, source_target_pairs={{0,8},{2,10},{4,12},{6,14},{8,0},{10,2},{12,4},{14,6},{16,24},{18,... | collective-permute-start | bytes 786440 | tf_op jit(solution)/shard_map/cond/branch_7_fun/ppermute | solution.py:76
  86.4 9.1 %collective-permute-start.101 = (bf16[64,2048]{1,0:T(8,128)(2,1)S(1)}, bf16[64,2048]{1,0:T(8,128)(2,1)S(1)}, u32[]{:S(2)}, u32[]{:S(2)}) collective-permute-start(bf16[64,2048]{1,0:T(8,128)(2,1)S(1)} %get-tuple-element.213), channel_id=1, source_target_pairs={{0,2},{2,0},{4,6},{6,4},{8,10},{10,8},{12,14},{14,12},{16,18},{18,... | collective-permute-start | bytes 786440 | tf_op jit(solution)/shard_map/ppermute | solution.py:84
  88.0 5.3 %collective-permute-start.95 = (bf16[128,384]{1,0:T(8,128)(2,1)S(1)}, bf16[128,384]{1,0:T(8,128)(2,1)S(1)}, u32[]{:S(2)}, u32[]{:S(2)}) collective-permute-start(bf16[128,384]{1,0:T(8,128)(2,1)S(1)} %get-tuple-element.244), channel_id=1, source_target_pairs={{0,1},{1,0},{2,3},{3,2},{4,5},{5,4},{6,7},{7,6},{8,9},{9,8},{10,11... | collective-permute-start | bytes 294920 | tf_op jit(solution)/shard_map/ppermute | solution.py:84
  89.7 8.5 %collective-permute-start.103 = (bf16[64,2048]{1,0:T(8,128)(2,1)S(1)}, bf16[64,2048]{1,0:T(8,128)(2,1)S(1)}, u32[]{:S(2)}, u32[]{:S(2)}) collective-permute-start(bf16[64,2048]{1,0:T(8,128)(2,1)S(1)} %multiply_convert_fusion), channel_id=1, source_target_pairs={{0,4},{2,6},{4,0},{6,2},{8,12},{10,14},{12,8},{14,10},{16,20},{18,... | collective-permute-start | bytes 786440 | tf_op jit(solution)/shard_map/ppermute | solution.py:84
  90.3 3.1 %collective-permute-start.97 = (bf16[64,2048]{1,0:T(8,128)(2,1)S(1)}, bf16[64,2048]{1,0:T(8,128)(2,1)S(1)}, u32[]{:S(2)}, u32[]{:S(2)}) collective-permute-start(bf16[64,2048]{1,0:T(8,128)(2,1)S(1)} %collective-permute-done.96), channel_id=1, source_target_pairs={{0,2},{2,0},{4,6},{6,4},{8,10},{10,8},{12,14},{14,12},{16,18},{18,... | collective-permute-start | bytes 786440 | tf_op jit(solution)/shard_map/ppermute | solution.py:84
  93.4 3.4 %copy-start.2 = (bf16[512,2048]{1,0:T(8,128)(2,1)S(1)}, bf16[512,2048]{1,0:T(8,128)(2,1)}, u32[]{:S(2)}) copy-start(bf16[512,2048]{1,0:T(8,128)(2,1)} %get-tuple-element.212) | copy-start | bytes 6291460
  94.0 5.1 %collective-permute-start.98 = (bf16[128,384]{1,0:T(8,128)(2,1)S(1)}, bf16[128,384]{1,0:T(8,128)(2,1)S(1)}, u32[]{:S(2)}, u32[]{:S(2)}) collective-permute-start(bf16[128,384]{1,0:T(8,128)(2,1)S(1)} %get-tuple-element.242), channel_id=1, source_target_pairs={{0,1},{1,0},{2,3},{3,2},{4,5},{5,4},{6,7},{7,6},{8,9},{9,8},{10,11... | collective-permute-start | bytes 294920 | tf_op jit(solution)/shard_map/ppermute | solution.py:84
  96.2 4.7 %collective-permute-start.102 = (bf16[128,384]{1,0:T(8,128)(2,1)S(1)}, bf16[128,384]{1,0:T(8,128)(2,1)S(1)}, u32[]{:S(2)}, u32[]{:S(2)}) collective-permute-start(bf16[128,384]{1,0:T(8,128)(2,1)S(1)} %get-tuple-element.240), channel_id=1, source_target_pairs={{0,1},{1,0},{2,3},{3,2},{4,5},{5,4},{6,7},{7,6},{8,9},{9,8},{10,11... | collective-permute-start | bytes 294920 | tf_op jit(solution)/shard_map/ppermute | solution.py:84
  98.2 2.9 %collective-permute-start.104 = (bf16[64,2048]{1,0:T(8,128)(2,1)S(1)}, bf16[64,2048]{1,0:T(8,128)(2,1)S(1)}, u32[]{:S(2)}, u32[]{:S(2)}) collective-permute-start(bf16[64,2048]{1,0:T(8,128)(2,1)S(1)} %collective-permute-done.103), channel_id=1, source_target_pairs={{0,2},{2,0},{4,6},{6,4},{8,10},{10,8},{12,14},{14,12},{16,18},{18,... | collective-permute-start | bytes 786440 | tf_op jit(solution)/shard_map/ppermute | solution.py:84
  101.8 4.7 %collective-permute-start.105 = (bf16[128,384]{1,0:T(8,128)(2,1)S(1)}, bf16[128,384]{1,0:T(8,128)(2,1)S(1)}, u32[]{:S(2)}, u32[]{:S(2)}) collective-permute-start(bf16[128,384]{1,0:T(8,128)(2,1)S(1)} %get-tuple-element.238), channel_id=1, source_target_pairs={{0,1},{1,0},{2,3},{3,2},{4,5},{5,4},{6,7},{7,6},{8,9},{9,8},{10,11... | collective-permute-start | bytes 294920 | tf_op jit(solution)/shard_map/ppermute | solution.py:84

commit v3 on v2

v3 whole, which is shorter than its diff:
```python
import functools
import itertools
import math

import jax
import jax.numpy as jnp
from jax import lax
from jax.experimental import pallas as pl
from jax.experimental.pallas import tpu as pltpu
from jax.sharding import PartitionSpec as P

distill_weight = 0.0625
max_branches = 24


def partner_table(pair_order):
    slot_count = pair_order.shape[1]
    slot_ids = jnp.arange(slot_count, dtype=jnp.int32)
    matches = pair_order[:, None, :] == slot_ids[None, :, None]
    following = jnp.roll(pair_order, -1, axis=1)
    return jnp.sum(jnp.where(matches, following[:, None, :], 0), axis=2)


def route_kernel(order_ref, code_ref, dest, src, color):
    micro_count, replicas = order_ref.shape
    pairs = replicas // 2
    bits = branch_bits(pairs)
    replica = lax.axis_index("rep") // 2
    for m in range(micro_count):
        for k in range(replicas):
            to, frm = order_ref[m, k], order_ref[m, (k + 1) % replicas]
            dest[frm] = to
            src[to] = frm
            color[k] = -1
        for start in range(0, replicas, 2):
            at = jnp.where(color[start] == 1, start + 1, start)
            for _ in range(pairs):
                color[at] = 0
                color[at ^ 1] = 1
                at = src[dest[at ^ 1] ^ 1]
        code = (1 - color[src[replica]]) * 2 + (1 - color[replica])
        for c in (1, 0):
            sigma = []
            place = jnp.int32(0)
            for z in range(pairs):
                leaves = jnp.where(color[2 * z] == c, 2 * z, 2 * z + 1)
                to = dest[leaves] // 2
                smaller = to
                for earlier in sigma:
                    smaller = smaller - jnp.where(earlier < to, 1, 0)
                place = place * (pairs - z) + smaller
                sigma.append(to)
            code = (code << bits) + place
        code_ref[m] = code


def branch_bits(pairs):
    return (math.factorial(pairs) - 1).bit_length()


def routes(pair_order):
    micro_count, replicas = pair_order.shape
    smem = pl.BlockSpec(memory_space=pltpu.SMEM)
    codes = pl.pallas_call(
        route_kernel,
        out_shape=jax.ShapeDtypeStruct((micro_count,), jnp.int32),
        in_specs=[smem],
        out_specs=smem,
        scratch_shapes=[pltpu.SMEM((replicas,), jnp.int32)] * 3,
    )(pair_order)
    bits = branch_bits(replicas // 2)
    mask = (1 << bits) - 1
    found = []
    for m in range(micro_count):
        code = codes[m]
        flags = code >> (2 * bits)
        found.append((code & mask, (code >> bits) & mask, (flags & 1) == 1, flags >= 2))
    return found


def move_pairs(block, branch, pairs, beside, *given):
    def one(sigma, moved, *rest):
        if any(z != to for z, to in enumerate(sigma)):
            route = [(z * 4 + low, to * 4 + low) for z, to in enumerate(sigma) for low in range(4)]
            moved = lax.ppermute(moved, "rep", route)
        return moved, *beside(*rest)

    every = [functools.partial(one, sigma) for sigma in itertools.permutations(range(pairs))]
    return lax.switch(branch, every, block, *given)


def swap(block, axis, bit):
    count = lax.axis_size(axis)
    return lax.ppermute(block, axis, [(i, i ^ bit) for i in range(count)])


def difference(own, other):
    spread = own.astype(jnp.float32) - other.astype(jnp.float32)
    return (distill_weight * spread).astype(jnp.bfloat16)


def sum_over(block, axis):
    if lax.axis_size(axis) == 2:
        return block + swap(block, axis, 1)
    return lax.psum(block, axis)


def after(block, *others):
    return lax.optimization_barrier((block, *others))[0]


def head_kernel(*refs):
    rows_ref, *blocks, out_ref, whole = refs
    height = blocks[0].shape[0]
    for at, block in enumerate(blocks):
        whole[pl.ds(at * height, height), :] = block[...]
    out_ref[...] = lax.dot_general(
        rows_ref[...], whole[...], (((0,), (0,)), ((), ())), preferred_element_type=jnp.float32
    ).astype(out_ref.dtype)


def head_gradient(rows, blocks):
    count, width = rows.shape
    height, vocab = blocks[0].shape
    step = vocab // 4
    return pl.pallas_call(
        head_kernel,
        grid=(vocab // step,),
        out_shape=jax.ShapeDtypeStruct((width, vocab), jnp.bfloat16),
        in_specs=[pl.BlockSpec((count, width), lambda i: (0, 0))]
        + [pl.BlockSpec((height, step), lambda i: (0, i))] * len(blocks),
        out_specs=pl.BlockSpec((width, step), lambda i: (0, i)),
        scratch_shapes=[pltpu.VMEM((count, step), jnp.bfloat16)],
        compiler_params=pltpu.CompilerParams(vmem_limit_bytes=16 << 20),
        cost_estimate=pl.CostEstimate(
            flops=2 * count * width * vocab,
            bytes_accessed=2 * (count * width + count * vocab + width * vocab),
            transcendentals=0,
        ),
    )(rows, *blocks)


def paired_body(states, head_weight, pair_order, row_example):
    micro_count, row_count, half_width = states.shape
    place = lax.axis_index("rep")
    replica, side = place // 2, place % 2
    parity = replica % 2
    pairs = pair_order.shape[1] // 2
    quarter = row_count // 4
    local = jnp.arange(row_count, dtype=jnp.int32)
    block = local // quarter
    by_core = (block >> 1, block & 1)
    by_chip = (block & 1, block >> 1)
    examples = lax.dynamic_index_in_dim(row_example, replica, 1, keepdims=False)

    def onehots(order):
        other_core, other_chip = order
        example_of = (
            (side ^ other_core) * (2 * quarter) + (parity ^ other_chip) * quarter + local % quarter
        )
        return (examples[:, None, :] == example_of[None, :, None]).astype(jnp.bfloat16)

    onehot_core, onehot_chip = onehots(by_core), onehots(by_chip)

    logits = []
    for m in range(micro_count):
        rows = jnp.dot(onehot_core[m], states[m], preferred_element_type=jnp.float32)
        rows = rows.astype(jnp.bfloat16)
        theirs = jnp.dot(rows[2 * quarter :], head_weight, preferred_element_type=jnp.float32)
        arrived = swap(theirs, "rep", 1)
        own = jnp.dot(rows[: 2 * quarter], head_weight, preferred_element_type=jnp.float32)
        far = (own[quarter:] + arrived[quarter:]).astype(jnp.bfloat16)
        home = (own[:quarter] + arrived[:quarter]).astype(jnp.bfloat16)
        logits.append((home, far))
    sib = swap(logits[0][1], "rep", 2)
    codes = routes(after(pair_order, *logits[-1]))
    chip_rows = jnp.einsum(
        "mei,miw->mew", onehot_chip, after(states, *logits[-1]), preferred_element_type=jnp.float32
    )
    chip_rows = chip_rows.astype(jnp.bfloat16)

    def settle(home, sib, first, second, to_home_first):
        grad_home = difference(home, jnp.where(to_home_first, first, second))
        grad_sib = difference(sib, jnp.where(to_home_first, second, first))
        return grad_home, grad_sib

    grads = []
    waiting = None
    for m in range(micro_count):
        home = logits[m][0]
        branch_first, branch_second, home_first, to_home_first = codes[m]
        sent_first = jnp.where(home_first, home, sib)
        sent_second = jnp.where(home_first, sib, home)
        nexts = [logits[m + 1][1]] if m + 1 < micro_count else []

        def beside_first(nexts, waiting):
            arriving = [swap(far, "rep", 2) for far in nexts]
            settled = []
            if waiting is not None:
                settled = settle(*waiting)
                settled = [*settled, swap(settled[0], "rep", 1)]
            return arriving, settled

        def beside_second(back):
            return [swap(grad, "rep", 2) for grad in back]

        first, arriving, settled = move_pairs(
            sent_first, branch_first, pairs, beside_first, nexts, waiting
        )
        back = [settled[1]] if settled else []
        second, *returned = move_pairs(
            after(sent_second, first), branch_second, pairs, beside_second, back
        )
        if settled:
            grads.append([settled[0], settled[2], returned[0]])
        waiting = (home, sib, first, second, to_home_first)
        sib = arriving[0] if arriving else None
    grad_home, grad_sib = settle(*waiting)
    grads.append([grad_home, swap(grad_home, "rep", 1), swap(grad_sib, "rep", 2)])
    for group in grads:
        group.append(swap(group[2], "rep", 1))

    def back(first, second):
        gradient = jnp.concatenate([first, second], axis=0)
        partial = jnp.einsum(
            "rv,wv->rw", gradient, head_weight, preferred_element_type=jnp.float32
        )
        return partial + swap(partial.astype(jnp.bfloat16), "voc", 1).astype(jnp.float32)

    state_parts = []
    for m in range(micro_count):
        near, far = back(*grads[m][:2]), back(*grads[m][2:])
        state_parts.append(
            jnp.einsum(
                "ei,ew->iw",
                onehot_chip[m],
                jnp.concatenate([near, far], axis=0).astype(jnp.bfloat16),
                preferred_element_type=jnp.float32,
            )
        )
    state_grad = jnp.stack(state_parts).astype(jnp.bfloat16)
    head_grad = head_gradient(
        chip_rows.reshape(micro_count * row_count, half_width), sum(grads, [])
    )
    return state_grad, head_grad


def spread_body(states, head_weight, pair_order, row_example):
    micro_count, row_count, half_width = states.shape
    devices = lax.axis_size("rep")
    place = lax.axis_index("rep")
    replica, side = place // 2, place % 2
    half = row_count // 2
    local = jnp.arange(row_count, dtype=jnp.int32)
    example_of = (side ^ (local // half)) * half + local % half
    examples = lax.dynamic_index_in_dim(row_example, replica, 1, keepdims=False)
    onehot = (examples[:, None, :] == example_of[None, :, None]).astype(jnp.bfloat16)
    ordered = jnp.einsum("mei,miw->mew", onehot, states, preferred_element_type=jnp.float32)
    ordered = ordered.astype(jnp.bfloat16)
    partner = partner_table(pair_order)
    sources = jnp.arange(devices, dtype=jnp.int32)
    partner_dev = 2 * jnp.repeat(partner, 2, axis=1) + sources % 2
    state_parts, gradients = [], []
    for m in range(micro_count):
        partial = jnp.dot(ordered[m], head_weight, preferred_element_type=jnp.float32)
        logits = (partial[:half] + swap(partial[half:], "rep", 1)).astype(jnp.bfloat16)
        tiles = logits.reshape(devices, half // devices, -1)
        tiles = lax.all_to_all(tiles, "rep", split_axis=0, concat_axis=0, tiled=True)
        mates = (partner_dev[m][:, None] == sources[None, :]).astype(jnp.bfloat16)
        mate_tiles = jnp.einsum("ds,srv->drv", mates, tiles, preferred_element_type=jnp.float32)
        graded = difference(tiles, mate_tiles)
        graded = lax.all_to_all(graded, "rep", split_axis=0, concat_axis=0, tiled=True)
        graded = graded.reshape(half, -1)
        gradient = jnp.concatenate([graded, swap(graded, "rep", 1)], axis=0)
        gradients.append(gradient)
        back = jnp.einsum("rv,wv->rw", gradient, head_weight, preferred_element_type=jnp.float32)
        state_canon = sum_over(back, "voc").astype(jnp.bfloat16)
        state_parts.append(
            jnp.einsum("ei,ew->iw", onehot[m], state_canon, preferred_element_type=jnp.float32)
        )
    state_grad = jnp.stack(state_parts).astype(jnp.bfloat16)
    head_grad = jnp.einsum(
        "mrw,mrv->wv", ordered, jnp.stack(gradients), preferred_element_type=jnp.float32
    )
    return state_grad, head_grad.astype(jnp.bfloat16)


def solution(mesh):
    replicas = mesh.shape["rep"] // 2
    few = replicas % 2 == 0 and math.factorial(replicas // 2) <= max_branches
    few = few and mesh.shape["voc"] == 2
    return jax.shard_map(
        paired_body if few else spread_body,
        mesh=mesh,
        in_specs=(P(None, None, "rep"), P("rep", "voc"), P(), P()),
        out_specs=(P(None, None, "rep"), P("rep", "voc")),
        check_vma=False,
    )
```

time: 108 us -> 83.6 us (0.77)
  starting transfers between devices: 33.1 us -> 18.5 us
  local copies, waits for them, and re-layouts: 11.4 us -> 3.16 us
  matrix products: 13.3 us -> 8.53 us
  waiting for transfers between devices: 32.5 us -> 36.7 us
  Pallas kernels: 1.69 us -> 5.73 us
  other arithmetic: 9.24 us -> 6.23 us
  between operations: 5.99 us -> 4.49 us
    ppermute x4, starting transfers between devices: 21.9 us -> 8.71 us  [one(): moved = lax.ppermute(moved, 'rep', route)]
    ppermute x4, waiting for transfers between devices: 19.8 us -> 29.2 us  [one(): moved = lax.ppermute(moved, 'rep', route)]
    unnamed x27 -> x14, local copies, waits for them, and re-layouts: 6.84 us -> 0.97 us
    ppermute x14, waiting for transfers between devices: 12.7 us -> 7.49 us  [swap(): return lax.ppermute(block, axis, [(i, i ^ bit) for i in range(count)])]
    pallas_call x1 -> x2, Pallas kernels: 1.69 us -> 5.73 us  [the longest x1 4.14 us: head_gradient(): pl.pallas_call(head_kernel, grid=(vocab // step,), out_shape=jax.ShapeDty...]
    dot_general x5, matrix products: 5.15 us -> 2.38 us  [the longest x2 1.46 us: paired_body(): jnp.dot(onehot_core[m], states[m], preferred_element_type=jnp.float32)]
    convert_element_type x6 -> x2, other arithmetic: 3.35 us -> 0.94 us  [paired_body(): far = (own[quarter:] + arrived[quarter:]).astype(jnp.bfloat16)]
    select_n x2, other arithmetic: 0.07 us -> 2.12 us  [paired_body(): sent_second = jnp.where(home_first, sib, home)]
  transfers between devices with their start and end apart: 18 -> 18, of which waited for: 9 -> 9; matrix products, arithmetic and copies ran while one was open for 25% -> 11% of each run, Pallas kernels for 2% -> 7%
where the time goes in v3:
time: 83.6 us; the launch traced here: 84.1 us
  waiting for transfers between devices  36.7 us (44%)
  starting transfers between devices  18.5 us (22%)
  matrix products  8.53 us (10%)
  other arithmetic  6.23 us (7%)
  Pallas kernels  5.73 us (7%)
  between operations  4.49 us (5%)
  local copies, waits for them, and re-layouts  3.16 us (4%)
    ppermute x4, waiting for transfers between devices, one(): moved = lax.ppermute(moved, 'rep', route)  29.2 us
    ppermute x14, starting transfers between devices, swap(): return lax.ppermute(block, axis, [(i, i ^ bit) for i in range(count)])  9.79 us
    ppermute x4, starting transfers between devices, one(): moved = lax.ppermute(moved, 'rep', route)  8.71 us
    ppermute x14, waiting for transfers between devices, swap(): return lax.ppermute(block, axis, [(i, i ^ bit) for i in range(count)])  7.49 us
    dot_general x4, matrix products, back(): jnp.einsum('rv,wv->rw', gradient, head_weight, preferred_element_type=jnp...  4.4 us
    pallas_call x1, Pallas kernels, head_gradient(): pl.pallas_call(head_kernel, grid=(vocab // step,), out_shape=jax.ShapeDty...  4.14 us
    select_n x2, other arithmetic, paired_body(): sent_second = jnp.where(home_first, sib, home)  2.12 us
    convert_element_type x2, other arithmetic, difference(): return (distill_weight * spread).astype(jnp.bfloat16)  2.05 us
  transfers between devices with their start and end apart: 18, of which 9 were waited for; matrix products, arithmetic and copies ran while one was open for 11% of the time, Pallas kernels for 7%

profile of v3, /device:TPU:0, one launch (start us, length us, event | category | flops | bytes accessed | tf_op | source)
XLA Modules:
  0.0 84.1 jit_solution(14744013411691766667)
XLA Ops:
  0.7 0.8 constant_dynamic-slice_fusion
  1.8 1.2 %convolution_convert_fusion.3 = bf16[256,384]{1,0:T(8,128)(2,1)S(1)} fusion(pred[2,256,256]{2,1,0:T(32,128)(4,1)S(1)} %get-tuple-element.875, bf16[2,256,384]{2,1,0:T(8,128)(2,1)} %param.100), kind=kOutput, calls=%fused_computation.51 | convolution fusion | flops 50429952 | bytes 458752 | tf_op jit(solution)/shard_map/dot_general | solution.py:167
  6.3 0.9 %copy-done.2 = f32[128,2048]{1,0:T(8,128)} copy-done((f32[128,2048]{1,0:T(8,128)}, f32[128,2048]{1,0:T(8,128)S(1)}, u32[]{:S(2)}) %copy-start.2) | copy-done | bytes 1048600
  7.2 2.9 %collective-permute-start.166 = (bf16[64,2048]{1,0:T(8,128)(2,1)S(1)}, bf16[64,2048]{1,0:T(8,128)(2,1)S(1)}, u32[]{:S(2)}, u32[]{:S(2)}) collective-permute-start(bf16[64,2048]{1,0:T(8,128)(2,1)S(1)} %fusion.2), channel_id=1, source_target_pairs={{0,4},{2,6},{4,0},{6,2},{8,12},{10,14},{12,8},{14,10},{16,20},{18,... | collective-permute-start | bytes 786440 | tf_op jit(solution)/shard_map/ppermute | solution.py:94
  10.1 0.9 %fusion.4 = (bf16[64,2048]{1,0:T(8,128)(2,1)}, bf16[64,2048]{1,0:T(8,128)(2,1)}) fusion(f32[128,2048]{1,0:T(8,128)S(1)} %collective-permute-done.164, f32[128,2048]{1,0:T(8,128)S(1)} %fusion.38), kind=kLoop, calls=%fused_computation.60 | loop fusion | flops 524288 | bytes 2621440 | tf_op jit(solution)/shard_map/convert_element_type | solution.py:172
  11.0 1.6 %shard_map.59 = s32[2]{0:T(128)} custom-call(s32[2,8]{1,0:T(2,128)} %order_ref), custom_call_target="tpu_custom_call" | custom-call | tf_op jit(solution)/shard_map/pallas_call | solution.py:64
  12.6 1.3 %fusion.49 = (s32[1]{0:T(128)}, s32[1]{0:T(128)}) fusion(s32[2]{0:T(128)} %shard_map.59), kind=kLoop, calls=%fused_computation.131 | loop fusion | bytes 16 | tf_op jit(solution)/shard_map/slice | solution.py:75
  17.5 1.1 %broadcast_select_fusion.2 = (bf16[64,2048]{1,0:T(8,128)(2,1)S(1)}, bf16[64,2048]{1,0:T(8,128)(2,1)S(1)}) fusion(bf16[64,2048]{1,0:T(8,128)(2,1)S(1)} %collective-permute-done.166, pred[]{:T(512)} %bitcast.8, f32[128,2048]{1,0:T(8,128)} %copy-done.2, f32[128,2048]{1,0:T(8,128)S(1)} %fusion.34), kind=kLoop, calls=%fused_computation.90 | loop fusion | flops 393216 | bytes 1835009 | tf_op jit(solution)/shard_map/jit(_where)/select_n | solution.py:193
  18.7 10.1 %conditional.6 = (bf16[64,2048]{1,0:T(8,128)(2,1)S(1)}, bf16[64,2048]{1,0:T(8,128)(2,1)}) conditional(s32[]{:T(128)} %bitcast.7, (bf16[64,2048]{1,0:T(8,128)(2,1)S(1)}, bf16[64,2048]{1,0:T(8,128)(2,1)S(1)}) %tuple.733, (bf16[64,2048]{1,0:T(8,128)(2,1)S(1)}, bf16[64,2048]{1,0:T(8,128)(2,1)S(1)}) %tuple.734, ...), branch_computations={%region_0.1_spmd, %region_1.2_spmd, %region_2.3_spmd, %region_3.4_... | conditional | bytes 2621536 | solution.py:89
  18.7 1.6 %collective-permute-start.17 = (bf16[64,2048]{1,0:T(8,128)(2,1)S(1)}, bf16[64,2048]{1,0:T(8,128)(2,1)S(1)}, u32[]{:S(2)}, u32[]{:S(2)}) collective-permute-start(bf16[64,2048]{1,0:T(8,128)(2,1)S(1)} %get-tuple-element.563), channel_id=1, source_target_pairs={{0,8},{2,10},{4,12},{6,14},{8,16},{10,18},{12,20},{14,22},{16,24},... | collective-permute-start | bytes 786440 | tf_op jit(solution)/shard_map/cond/branch_9_fun/ppermute | solution.py:85
  20.3 1.0 %collective-permute-start.18 = (bf16[64,2048]{1,0:T(8,128)(2,1)S(1)}, bf16[64,2048]{1,0:T(8,128)(2,1)}, u32[]{:S(2)}, u32[]{:S(2)}) collective-permute-start(bf16[64,2048]{1,0:T(8,128)(2,1)S(1)} %get-tuple-element.564), channel_id=1, source_target_pairs={{0,4},{2,6},{4,0},{6,2},{8,12},{10,14},{12,8},{14,10},{16,20},{18,... | collective-permute-start | bytes 786440 | tf_op jit(solution)/shard_map/cond/branch_9_fun/ppermute | solution.py:94
  21.3 7.4 %collective-permute-done.17 = bf16[64,2048]{1,0:T(8,128)(2,1)S(1)} collective-permute-done((bf16[64,2048]{1,0:T(8,128)(2,1)S(1)}, bf16[64,2048]{1,0:T(8,128)(2,1)S(1)}, u32[]{:S(2)}, u32[]{:S(2)}) %collective-permute-start.17) | collective-permute-done | bytes 262176 | tf_op jit(solution)/shard_map/cond/branch_9_fun/ppermute | solution.py:85
  28.8 10.3 %conditional.7 = (bf16[64,2048]{1,0:T(8,128)(2,1)S(1)}) conditional(s32[]{:T(128)} %bitcast.9, bf16[64,2048]{1,0:T(8,128)(2,1)S(1)} %get-tuple-element.801, bf16[64,2048]{1,0:T(8,128)(2,1)S(1)} %get-tuple-element.801, bf16[64,2048]{1,0:T(8,128)(2,1)S(1)} %get-tuple-element.801, ...), branch_computations={%region_24.25_spmd, %region_25.26_spmd, %region_26.27_spmd, %regio... | conditional | bytes 1572912 | solution.py:89
  28.8 3.0 %collective-permute-start.54 = (bf16[64,2048]{1,0:T(8,128)(2,1)S(1)}, bf16[64,2048]{1,0:T(8,128)(2,1)S(1)}, u32[]{:S(2)}, u32[]{:S(2)}) collective-permute-start(bf16[64,2048]{1,0:T(8,128)(2,1)S(1)} %param.32), channel_id=1, source_target_pairs={{0,8},{2,10},{4,12},{6,14},{8,16},{10,18},{12,20},{14,22},{16,0},{... | collective-permute-start | bytes 786440 | tf_op jit(solution)/shard_map/cond/branch_8_fun/ppermute | solution.py:85
  31.8 7.1 %collective-permute-done.54 = bf16[64,2048]{1,0:T(8,128)(2,1)S(1)} collective-permute-done((bf16[64,2048]{1,0:T(8,128)(2,1)S(1)}, bf16[64,2048]{1,0:T(8,128)(2,1)S(1)}, u32[]{:S(2)}, u32[]{:S(2)}) %collective-permute-start.54) | collective-permute-done | bytes 262176 | tf_op jit(solution)/shard_map/cond/branch_8_fun/ppermute | solution.py:85
  39.0 1.0 %broadcast_select_fusion = (bf16[64,2048]{1,0:T(8,128)(2,1)S(1)}, bf16[64,2048]{1,0:T(8,128)(2,1)S(1)}) fusion(bf16[64,2048]{1,0:T(8,128)(2,1)} %get-tuple-element.802, bf16[64,2048]{1,0:T(8,128)(2,1)S(1)} %copy-done.1, pred[]{:T(512)} %bitcast.10), kind=kLoop, calls=%fused_computation.88 | loop fusion | flops 262144 | bytes 1048577 | tf_op jit(solution)/shard_map/jit(_where)/select_n | solution.py:193
  40.0 8.6 %conditional.10 = (bf16[64,2048]{1,0:T(8,128)(2,1)S(1)}, bf16[64,2048]{1,0:T(8,128)(2,1)}, bf16[64,2048]{1,0:T(8,128)(2,1)}, bf16[64,2048]{1,0:T(8,128)(2,1)S(1)}) conditional(s32[]{:T(128)} %bitcast.3, (bf16[64,2048]{1,0:T(8,128)(2,1)S(1)}, pred[]{:T(512)}, bf16[64,2048]{1,0:T(8,128)(2,1)S(1)}, ...), branch_computations={%region_48.49_spmd, %region_49.50_spmd, %region_50.51_spmd, %regio... | conditional | flops 1572864 | bytes 4194417
  40.3 1.9 %collective-permute-start.154 = (bf16[64,2048]{1,0:T(8,128)(2,1)S(1)}, bf16[64,2048]{1,0:T(8,128)(2,1)S(1)}, u32[]{:S(2)}, u32[]{:S(2)}) collective-permute-start(bf16[64,2048]{1,0:T(8,128)(2,1)S(1)} %get-tuple-element.707), channel_id=1, source_target_pairs={{0,24},{2,26},{4,28},{6,30},{8,0},{10,2},{12,4},{14,6},{16,16},{18... | collective-permute-start | bytes 786440 | tf_op jit(solution)/shard_map/cond/branch_19_fun/ppermute | solution.py:85
  42.2 0.9 %multiply_convert_fusion.38 = (bf16[64,2048]{1,0:T(8,128)(2,1)S(1)}, bf16[64,2048]{1,0:T(8,128)(2,1)}) fusion(bf16[64,2048]{1,0:T(8,128)(2,1)S(1)} %get-tuple-element.712, bf16[64,2048]{1,0:T(8,128)(2,1)S(1)} %get-tuple-element.711, bf16[64,2048]{1,0:T(8,128)(2,1)S(1)} %get-tuple-element.710, pred[]{:T(512)} %get-tuple-element.709, ...), kind=kLoop, calls=%fused_computation.38 | loop fusion | flops 1572864 | bytes 1572865 | tf_op jit(solution)/shard_map/cond/branch_0_fun/convert_element_type | solution.py:99
  43.1 5.4 %collective-permute-done.154 = bf16[64,2048]{1,0:T(8,128)(2,1)S(1)} collective-permute-done((bf16[64,2048]{1,0:T(8,128)(2,1)S(1)}, bf16[64,2048]{1,0:T(8,128)(2,1)S(1)}, u32[]{:S(2)}, u32[]{:S(2)}) %collective-permute-start.154) | collective-permute-done | bytes 262176 | tf_op jit(solution)/shard_map/cond/branch_19_fun/ppermute | solution.py:85
  48.6 12.1 %conditional.9 = (bf16[64,2048]{1,0:T(8,128)(2,1)S(1)}, bf16[64,2048]{1,0:T(8,128)(2,1)}) conditional(s32[]{:T(128)} %bitcast.11, (bf16[64,2048]{1,0:T(8,128)(2,1)S(1)}, bf16[64,2048]{1,0:T(8,128)(2,1)S(1)}) %tuple.525, (bf16[64,2048]{1,0:T(8,128)(2,1)S(1)}, bf16[64,2048]{1,0:T(8,128)(2,1)S(1)}) %tuple.526, ...), branch_computations={%region_72.73_spmd, %region_73.74_spmd, %region_74.75_spmd, %regio... | conditional | bytes 2621536 | solution.py:89
  48.7 2.1 %collective-permute-start.113 = (bf16[64,2048]{1,0:T(8,128)(2,1)S(1)}, bf16[64,2048]{1,0:T(8,128)(2,1)S(1)}, u32[]{:S(2)}, u32[]{:S(2)}) collective-permute-start(bf16[64,2048]{1,0:T(8,128)(2,1)S(1)} %get-tuple-element.781), channel_id=1, source_target_pairs={{0,24},{2,26},{4,28},{6,30},{8,16},{10,18},{12,20},{14,22},{16,0},... | collective-permute-start | bytes 786440 | tf_op jit(solution)/shard_map/cond/branch_22_fun/ppermute | solution.py:85
  51.2 9.2 %collective-permute-done.113 = bf16[64,2048]{1,0:T(8,128)(2,1)S(1)} collective-permute-done((bf16[64,2048]{1,0:T(8,128)(2,1)S(1)}, bf16[64,2048]{1,0:T(8,128)(2,1)S(1)}, u32[]{:S(2)}, u32[]{:S(2)}) %collective-permute-start.113) | collective-permute-done | bytes 262176 | tf_op jit(solution)/shard_map/cond/branch_22_fun/ppermute | solution.py:85
  60.8 1.1 %multiply_convert_fusion.49 = (bf16[64,2048]{1,0:T(8,128)(2,1)S(1)}, bf16[64,2048]{1,0:T(8,128)(2,1)S(1)}) fusion(bf16[64,2048]{1,0:T(8,128)(2,1)S(1)} %copy-done.1, bf16[64,2048]{1,0:T(8,128)(2,1)S(1)} %get-tuple-element.806, bf16[64,2048]{1,0:T(8,128)(2,1)S(1)} %get-tuple-element.809, pred[]{:T(512)} %bitcast.14, bf16[64,2048]{1,0:T(8,128)(2,1)} %get-tuple-element.802), kind=kLoop, calls=%fused_computation.80 | loop fusion | flops 1572864 | bytes 1572865 | tf_op jit(solution)/shard_map/convert_element_type | solution.py:99
  62.0 1.7 %fusion.53 = (bf16[128,384]{1,0:T(8,128)(2,1)S(1)}, f32[128,384]{1,0:T(8,128)S(1)}) fusion(bf16[384,2048]{1,0:T(8,128)(2,1)S(1)} %copy-done, bf16[64,2048]{1,0:T(8,128)(2,1)} %get-tuple-element.804.refs_2_, bf16[64,2048]{1,0:T(8,128)(2,1)} %get-tuple-element.817.refs_1_), kind=kOutput, calls=%fused_computation.135 | convolution fusion | flops 202424320 | bytes 2392064 | tf_op jit(solution)/shard_map/rv,wv->rw/dot_general | solution.py:225
  63.7 1.6 %collective-permute-start.167 = (bf16[128,384]{1,0:T(8,128)(2,1)S(1)}, bf16[128,384]{1,0:T(8,128)(2,1)S(1)}, u32[]{:S(2)}, u32[]{:S(2)}) collective-permute-start(bf16[128,384]{1,0:T(8,128)(2,1)S(1)} %get-tuple-element.885), channel_id=1, source_target_pairs={{0,1},{1,0},{2,3},{3,2},{4,5},{5,4},{6,7},{7,6},{8,9},{9,8},{10,11... | collective-permute-start | bytes 294920 | tf_op jit(solution)/shard_map/ppermute | solution.py:94
  66.1 2.8 %collective-permute-done.167 = bf16[128,384]{1,0:T(8,128)(2,1)S(1)} collective-permute-done((bf16[128,384]{1,0:T(8,128)(2,1)S(1)}, bf16[128,384]{1,0:T(8,128)(2,1)S(1)}, u32[]{:S(2)}, u32[]{:S(2)}) %collective-permute-start.167) | collective-permute-done | bytes 98336 | tf_op jit(solution)/shard_map/ppermute | solution.py:94
  69.5 1.6 %collective-permute-start.171 = (bf16[128,384]{1,0:T(8,128)(2,1)S(1)}, bf16[128,384]{1,0:T(8,128)(2,1)S(1)}, u32[]{:S(2)}, u32[]{:S(2)}) collective-permute-start(bf16[128,384]{1,0:T(8,128)(2,1)S(1)} %get-tuple-element.881), channel_id=1, source_target_pairs={{0,1},{1,0},{2,3},{3,2},{4,5},{5,4},{6,7},{7,6},{8,9},{9,8},{10,11... | collective-permute-start | bytes 294920 | tf_op jit(solution)/shard_map/ppermute | solution.py:94
  71.1 1.5 %fusion.52 = (bf16[128,384]{1,0:T(8,128)(2,1)S(1)}, f32[128,384]{1,0:T(8,128)S(1)}) fusion(bf16[384,2048]{1,0:T(8,128)(2,1)S(1)} %copy-done, bf16[64,2048]{1,0:T(8,128)(2,1)S(1)} %collective-permute-done.168.refs_4_, bf16[64,2048]{1,0:T(8,128)(2,1)} %get-tuple-element.808.refs_3_), kind=kOutput, calls=%fused_computation.134 | convolution fusion | flops 202424320 | bytes 2392064 | tf_op jit(solution)/shard_map/rv,wv->rw/dot_general | solution.py:225
  73.2 0.8 collective-permute-done.172.refs_7_
  74.2 3.1 %collective-permute-done.169 = bf16[128,384]{1,0:T(8,128)(2,1)S(1)} collective-permute-done((bf16[128,384]{1,0:T(8,128)(2,1)S(1)}, bf16[128,384]{1,0:T(8,128)(2,1)S(1)}, u32[]{:S(2)}, u32[]{:S(2)}) %collective-permute-start.169) | collective-permute-done | bytes 98336 | tf_op jit(solution)/shard_map/ppermute | solution.py:94
  78.9 4.1 %shard_map.60 = bf16[384,2048]{1,0:T(8,128)(2,1)} custom-call(bf16[512,384]{1,0:T(8,128)(2,1)S(1)} %bitcast.43, bf16[64,2048]{1,0:T(8,128)(2,1)} %get-tuple-element.817.refs_1_, bf16[64,2048]{1,0:T(8,128)(2,1)} %get-tuple-element.804.refs_2_, bf16[64,2048]{1,0:T(8,128)(2,1)} %get-tuple-element.808.refs_3_, ...), custom_call_target="tpu_custom_call" | custom-call | flops 805306368 | bytes 4063232 | tf_op jit(solution)/shard_map/pallas_call | solution.py:126
  (56 shorter events, 9.0 us)
Async XLA Ops:
  0.6 2.4 %copy-start = (bf16[384,2048]{1,0:T(8,128)(2,1)S(1)}, bf16[384,2048]{1,0:T(8,128)(2,1)}, u32[]{:S(2)}) copy-start(bf16[384,2048]{1,0:T(8,128)(2,1)} %param.101) | copy-start | bytes 4718596
  1.8 2.2 %copy-start.3 = (bf16[2,256,384]{2,1,0:T(8,128)(2,1)S(1)}, bf16[2,256,384]{2,1,0:T(8,128)(2,1)}, u32[]{:S(2)}) copy-start(bf16[2,256,384]{2,1,0:T(8,128)(2,1)} %param.100) | copy-start | bytes 1179652
  3.5 2.8 %collective-permute-start.165 = (f32[128,2048]{1,0:T(8,128)S(1)}, f32[128,2048]{1,0:T(8,128)S(1)}, u32[]{:S(2)}, u32[]{:S(2)}) collective-permute-start(f32[128,2048]{1,0:T(8,128)S(1)} %fusion.32), channel_id=1, source_target_pairs={{0,2},{2,0},{4,6},{6,4},{8,10},{10,8},{12,14},{14,12},{16,18},{18,... | collective-permute-start | bytes 3145736 | tf_op jit(solution)/shard_map/ppermute | solution.py:94
  4.7 5.5 %collective-permute-start.164 = (f32[128,2048]{1,0:T(8,128)S(1)}, f32[128,2048]{1,0:T(8,128)S(1)}, u32[]{:S(2)}, u32[]{:S(2)}) collective-permute-start(f32[128,2048]{1,0:T(8,128)S(1)} %fusion.36), channel_id=1, source_target_pairs={{0,2},{2,0},{4,6},{6,4},{8,10},{10,8},{12,14},{14,12},{16,18},{18,... | collective-permute-start | bytes 3145736 | tf_op jit(solution)/shard_map/ppermute | solution.py:94
  6.3 1.0 %copy-start.2 = (f32[128,2048]{1,0:T(8,128)}, f32[128,2048]{1,0:T(8,128)S(1)}, u32[]{:S(2)}) copy-start(f32[128,2048]{1,0:T(8,128)S(1)} %collective-permute-done.165) | copy-start | bytes 3145732
  7.2 10.3 %collective-permute-start.166 = (bf16[64,2048]{1,0:T(8,128)(2,1)S(1)}, bf16[64,2048]{1,0:T(8,128)(2,1)S(1)}, u32[]{:S(2)}, u32[]{:S(2)}) collective-permute-start(bf16[64,2048]{1,0:T(8,128)(2,1)S(1)} %fusion.2), channel_id=1, source_target_pairs={{0,4},{2,6},{4,0},{6,2},{8,12},{10,14},{12,8},{14,10},{16,20},{18,... | collective-permute-start | bytes 786440 | tf_op jit(solution)/shard_map/ppermute | solution.py:94
  12.6 6.1 %copy-start.5 = (bf16[64,2048]{1,0:T(8,128)(2,1)S(1)}, bf16[64,2048]{1,0:T(8,128)(2,1)}, u32[]{:S(2)}) copy-start(bf16[64,2048]{1,0:T(8,128)(2,1)} %get-tuple-element.869) | copy-start | bytes 786436
  18.7 10.0 %collective-permute-start.17 = (bf16[64,2048]{1,0:T(8,128)(2,1)S(1)}, bf16[64,2048]{1,0:T(8,128)(2,1)S(1)}, u32[]{:S(2)}, u32[]{:S(2)}) collective-permute-start(bf16[64,2048]{1,0:T(8,128)(2,1)S(1)} %get-tuple-element.563), channel_id=1, source_target_pairs={{0,8},{2,10},{4,12},{6,14},{8,16},{10,18},{12,20},{14,22},{16,24},... | collective-permute-start | bytes 786440 | tf_op jit(solution)/shard_map/cond/branch_9_fun/ppermute | solution.py:85
  20.3 8.4 %collective-permute-start.18 = (bf16[64,2048]{1,0:T(8,128)(2,1)S(1)}, bf16[64,2048]{1,0:T(8,128)(2,1)}, u32[]{:S(2)}, u32[]{:S(2)}) collective-permute-start(bf16[64,2048]{1,0:T(8,128)(2,1)S(1)} %get-tuple-element.564), channel_id=1, source_target_pairs={{0,4},{2,6},{4,0},{6,2},{8,12},{10,14},{12,8},{14,10},{16,20},{18,... | collective-permute-start | bytes 786440 | tf_op jit(solution)/shard_map/cond/branch_9_fun/ppermute | solution.py:94
  28.7 10.3 %copy-start.1 = (bf16[64,2048]{1,0:T(8,128)(2,1)S(1)}, bf16[64,2048]{1,0:T(8,128)(2,1)}, u32[]{:S(2)}) copy-start(bf16[64,2048]{1,0:T(8,128)(2,1)} %get-tuple-element.870) | copy-start | bytes 786436
  28.8 10.2 %collective-permute-start.54 = (bf16[64,2048]{1,0:T(8,128)(2,1)S(1)}, bf16[64,2048]{1,0:T(8,128)(2,1)S(1)}, u32[]{:S(2)}, u32[]{:S(2)}) collective-permute-start(bf16[64,2048]{1,0:T(8,128)(2,1)S(1)} %param.32), channel_id=1, source_target_pairs={{0,8},{2,10},{4,12},{6,14},{8,16},{10,18},{12,20},{14,22},{16,0},{... | collective-permute-start | bytes 786440 | tf_op jit(solution)/shard_map/cond/branch_8_fun/ppermute | solution.py:85
  40.3 8.3 %collective-permute-start.154 = (bf16[64,2048]{1,0:T(8,128)(2,1)S(1)}, bf16[64,2048]{1,0:T(8,128)(2,1)S(1)}, u32[]{:S(2)}, u32[]{:S(2)}) collective-permute-start(bf16[64,2048]{1,0:T(8,128)(2,1)S(1)} %get-tuple-element.707), channel_id=1, source_target_pairs={{0,24},{2,26},{4,28},{6,30},{8,0},{10,2},{12,4},{14,6},{16,16},{18... | collective-permute-start | bytes 786440 | tf_op jit(solution)/shard_map/cond/branch_19_fun/ppermute | solution.py:85
  43.1 5.5 %collective-permute-start.155 = (bf16[64,2048]{1,0:T(8,128)(2,1)}, bf16[64,2048]{1,0:T(8,128)(2,1)}, u32[]{:S(2)}, u32[]{:S(2)}) collective-permute-start(bf16[64,2048]{1,0:T(8,128)(2,1)} %get-tuple-element.1015), channel_id=1, source_target_pairs={{0,2},{2,0},{4,6},{6,4},{8,10},{10,8},{12,14},{14,12},{16,18},{18,... | collective-permute-start | bytes 786440 | tf_op jit(solution)/shard_map/cond/branch_19_fun/ppermute | solution.py:94
  48.7 11.8 %collective-permute-start.113 = (bf16[64,2048]{1,0:T(8,128)(2,1)S(1)}, bf16[64,2048]{1,0:T(8,128)(2,1)S(1)}, u32[]{:S(2)}, u32[]{:S(2)}) collective-permute-start(bf16[64,2048]{1,0:T(8,128)(2,1)S(1)} %get-tuple-element.781), channel_id=1, source_target_pairs={{0,24},{2,26},{4,28},{6,30},{8,16},{10,18},{12,20},{14,22},{16,0},... | collective-permute-start | bytes 786440 | tf_op jit(solution)/shard_map/cond/branch_22_fun/ppermute | solution.py:85
  50.8 9.7 %collective-permute-start.114 = (bf16[64,2048]{1,0:T(8,128)(2,1)S(1)}, bf16[64,2048]{1,0:T(8,128)(2,1)}, u32[]{:S(2)}, u32[]{:S(2)}) collective-permute-start(bf16[64,2048]{1,0:T(8,128)(2,1)S(1)} %get-tuple-element.782), channel_id=1, source_target_pairs={{0,4},{2,6},{4,0},{6,2},{8,12},{10,14},{12,8},{14,10},{16,20},{18,... | collective-permute-start | bytes 786440 | tf_op jit(solution)/shard_map/cond/branch_22_fun/ppermute | solution.py:94
  61.9 3.3 %copy-start.4 = (bf16[2,256,384]{2,1,0:T(8,128)(2,1)S(1)}, bf16[2,256,384]{2,1,0:T(8,128)(2,1)}, u32[]{:S(2)}) copy-start(bf16[2,256,384]{2,1,0:T(8,128)(2,1)} %param.100) | copy-start | bytes 1179652
  61.9 7.0 %collective-permute-start.170 = (bf16[64,2048]{1,0:T(8,128)(2,1)S(1)}, bf16[64,2048]{1,0:T(8,128)(2,1)S(1)}, u32[]{:S(2)}, u32[]{:S(2)}) collective-permute-start(bf16[64,2048]{1,0:T(8,128)(2,1)S(1)} %get-tuple-element.871.refs_5_), channel_id=1, source_target_pairs={{0,2},{2,0},{4,6},{6,4},{8,10},{10,8},{12,14},{14,12},{16,18},{18,... | collective-permute-start | bytes 786440 | tf_op jit(solution)/shard_map/ppermute | solution.py:94
  63.7 5.2 %collective-permute-start.167 = (bf16[128,384]{1,0:T(8,128)(2,1)S(1)}, bf16[128,384]{1,0:T(8,128)(2,1)S(1)}, u32[]{:S(2)}, u32[]{:S(2)}) collective-permute-start(bf16[128,384]{1,0:T(8,128)(2,1)S(1)} %get-tuple-element.885), channel_id=1, source_target_pairs={{0,1},{1,0},{2,3},{3,2},{4,5},{5,4},{6,7},{7,6},{8,9},{9,8},{10,11... | collective-permute-start | bytes 294920 | tf_op jit(solution)/shard_map/ppermute | solution.py:94
  65.6 8.5 %collective-permute-start.172 = (bf16[64,2048]{1,0:T(8,128)(2,1)S(1)}, bf16[64,2048]{1,0:T(8,128)(2,1)S(1)}, u32[]{:S(2)}, u32[]{:S(2)}) collective-permute-start(bf16[64,2048]{1,0:T(8,128)(2,1)S(1)} %get-tuple-element.872), channel_id=1, source_target_pairs={{0,4},{2,6},{4,0},{6,2},{8,12},{10,14},{12,8},{14,10},{16,20},{18,... | collective-permute-start | bytes 786440 | tf_op jit(solution)/shard_map/ppermute | solution.py:94
  66.1 5.0 %collective-permute-start.168 = (bf16[64,2048]{1,0:T(8,128)(2,1)}, bf16[64,2048]{1,0:T(8,128)(2,1)S(1)}, u32[]{:S(2)}, u32[]{:S(2)}) collective-permute-start(bf16[64,2048]{1,0:T(8,128)(2,1)} %get-tuple-element.808.refs_3_), channel_id=1, source_target_pairs={{0,2},{2,0},{4,6},{6,4},{8,10},{10,8},{12,14},{14,12},{16,18},{18,... | collective-permute-start | bytes 786440 | tf_op jit(solution)/shard_map/ppermute | solution.py:94
  69.5 4.7 %collective-permute-start.171 = (bf16[128,384]{1,0:T(8,128)(2,1)S(1)}, bf16[128,384]{1,0:T(8,128)(2,1)S(1)}, u32[]{:S(2)}, u32[]{:S(2)}) collective-permute-start(bf16[128,384]{1,0:T(8,128)(2,1)S(1)} %get-tuple-element.881), channel_id=1, source_target_pairs={{0,1},{1,0},{2,3},{3,2},{4,5},{5,4},{6,7},{7,6},{8,9},{9,8},{10,11... | collective-permute-start | bytes 294920 | tf_op jit(solution)/shard_map/ppermute | solution.py:94
  72.7 4.7 %collective-permute-start.169 = (bf16[128,384]{1,0:T(8,128)(2,1)S(1)}, bf16[128,384]{1,0:T(8,128)(2,1)S(1)}, u32[]{:S(2)}, u32[]{:S(2)}) collective-permute-start(bf16[128,384]{1,0:T(8,128)(2,1)S(1)} %get-tuple-element.883), channel_id=1, source_target_pairs={{0,1},{1,0},{2,3},{3,2},{4,5},{5,4},{6,7},{7,6},{8,9},{9,8},{10,11... | collective-permute-start | bytes 294920 | tf_op jit(solution)/shard_map/ppermute | solution.py:94
  74.1 3.3 %collective-permute-start.173 = (bf16[64,2048]{1,0:T(8,128)(2,1)S(1)}, bf16[64,2048]{1,0:T(8,128)(2,1)S(1)}, u32[]{:S(2)}, u32[]{:S(2)}) collective-permute-start(bf16[64,2048]{1,0:T(8,128)(2,1)S(1)} %collective-permute-done.172.refs_7_), channel_id=1, source_target_pairs={{0,2},{2,0},{4,6},{6,4},{8,10},{10,8},{12,14},{14,12},{16,18},{18,... | collective-permute-start | bytes 786440 | tf_op jit(solution)/shard_map/ppermute | solution.py:94
  78.0 5.0 %collective-permute-start.174 = (bf16[128,384]{1,0:T(8,128)(2,1)S(1)}, bf16[128,384]{1,0:T(8,128)(2,1)S(1)}, u32[]{:S(2)}, u32[]{:S(2)}) collective-permute-start(bf16[128,384]{1,0:T(8,128)(2,1)S(1)} %get-tuple-element.879), channel_id=1, source_target_pairs={{0,1},{1,0},{2,3},{3,2},{4,5},{5,4},{6,7},{7,6},{8,9},{9,8},{10,11... | collective-permute-start | bytes 294920 | tf_op jit(solution)/shard_map/ppermute | solution.py:94

commit v4 on v3

--- a/solution.py
+++ b/solution.py
@@ -10,7 +10,7 @@
 from jax.sharding import PartitionSpec as P
 
 distill_weight = 0.0625
-max_branches = 24
+max_permutations = 24
 
 
 def partner_table(pair_order):
@@ -21,10 +21,10 @@
     return jnp.sum(jnp.where(matches, following[:, None, :], 0), axis=2)
 
 
-def route_kernel(order_ref, code_ref, dest, src, color):
+def route_kernel(order_ref, *refs):
+    *branch_refs, flags_ref, dest, src, color = refs
     micro_count, replicas = order_ref.shape
     pairs = replicas // 2
-    bits = branch_bits(pairs)
     replica = lax.axis_index("rep") // 2
     for m in range(micro_count):
         for k in range(replicas):
@@ -38,8 +38,7 @@
                 color[at] = 0
                 color[at ^ 1] = 1
                 at = src[dest[at ^ 1] ^ 1]
-        code = (1 - color[src[replica]]) * 2 + (1 - color[replica])
-        for c in (1, 0):
+        for c in range(2):
             sigma = []
             place = jnp.int32(0)
             for z in range(pairs):
@@ -50,32 +49,27 @@
                     smaller = smaller - jnp.where(earlier < to, 1, 0)
                 place = place * (pairs - z) + smaller
                 sigma.append(to)
-            code = (code << bits) + place
-        code_ref[m] = code
-
-
-def branch_bits(pairs):
-    return (math.factorial(pairs) - 1).bit_length()
+            branch_refs[2 * m + c][0] = place
+        for row, moved in enumerate((replica, src[replica])):
+            at = 2 * m + row
+            flags_ref[at : at + 1, :] = jnp.full((1, flags_ref.shape[1]), color[moved], jnp.int32)
 
 
 def routes(pair_order):
     micro_count, replicas = pair_order.shape
     smem = pl.BlockSpec(memory_space=pltpu.SMEM)
-    codes = pl.pallas_call(
+    *branches, flags = pl.pallas_call(
         route_kernel,
-        out_shape=jax.ShapeDtypeStruct((micro_count,), jnp.int32),
+        out_shape=[jax.ShapeDtypeStruct((1,), jnp.int32)] * (2 * micro_count)
+        + [jax.ShapeDtypeStruct((2 * micro_count, 128), jnp.int32)],
         in_specs=[smem],
-        out_specs=smem,
+        out_specs=[smem] * (2 * micro_count) + [pl.BlockSpec(memory_space=pltpu.VMEM)],
         scratch_shapes=[pltpu.SMEM((replicas,), jnp.int32)] * 3,
+        compiler_params=pltpu.CompilerParams(vmem_limit_bytes=1 << 20),
     )(pair_order)
-    bits = branch_bits(replicas // 2)
-    mask = (1 << bits) - 1
-    found = []
-    for m in range(micro_count):
-        code = codes[m]
-        flags = code >> (2 * bits)
-        found.append((code & mask, (code >> bits) & mask, (flags & 1) == 1, flags >= 2))
-    return found
+    branch = [number.reshape(()) for number in branches]
+    flag = [flags[at : at + 1, :1] == 0 for at in range(2 * micro_count)]
+    return [(branch[2 * m : 2 * m + 2], flag[2 * m : 2 * m + 2]) for m in range(micro_count)]
 
 
 def move_pairs(block, branch, pairs, beside, *given):
@@ -83,7 +77,7 @@
         if any(z != to for z, to in enumerate(sigma)):
             route = [(z * 4 + low, to * 4 + low) for z, to in enumerate(sigma) for low in range(4)]
             moved = lax.ppermute(moved, "rep", route)
-        return moved, *beside(*rest)
+        return moved, beside(*rest)
 
     every = [functools.partial(one, sigma) for sigma in itertools.permutations(range(pairs))]
     return lax.switch(branch, every, block, *given)
@@ -184,41 +178,44 @@
         grad_sib = difference(sib, jnp.where(to_home_first, second, first))
         return grad_home, grad_sib
 
-    grads = []
-    waiting = None
-    for m in range(micro_count):
-        home = logits[m][0]
-        branch_first, branch_second, home_first, to_home_first = codes[m]
-        sent_first = jnp.where(home_first, home, sib)
-        sent_second = jnp.where(home_first, sib, home)
-        nexts = [logits[m + 1][1]] if m + 1 < micro_count else []
-
-        def beside_first(nexts, waiting):
-            arriving = [swap(far, "rep", 2) for far in nexts]
-            settled = []
-            if waiting is not None:
-                settled = settle(*waiting)
-                settled = [*settled, swap(settled[0], "rep", 1)]
-            return arriving, settled
-
-        def beside_second(back):
-            return [swap(grad, "rep", 2) for grad in back]
-
-        first, arriving, settled = move_pairs(
-            sent_first, branch_first, pairs, beside_first, nexts, waiting
-        )
-        back = [settled[1]] if settled else []
-        second, *returned = move_pairs(
-            after(sent_second, first), branch_second, pairs, beside_second, back
-        )
-        if settled:
-            grads.append([settled[0], settled[2], returned[0]])
-        waiting = (home, sib, first, second, to_home_first)
-        sib = arriving[0] if arriving else None
-    grad_home, grad_sib = settle(*waiting)
-    grads.append([grad_home, swap(grad_home, "rep", 1), swap(grad_sib, "rep", 2)])
-    for group in grads:
-        group.append(swap(group[2], "rep", 1))
+    def leaving(home, sib, home_first):
+        return jnp.where(home_first, home, sib), jnp.where(home_first, sib, home)
+
+    def first_beside(far, waiting):
+        return [swap(block, "rep", 2) for block in far], [settle(*group) for group in waiting]
+
+    def second_beside(coming, settled):
+        sent = [leaving(*group) for group in coming]
+        returned = []
+        for grad_home, grad_sib in settled:
+            grad_far = swap(grad_sib, "rep", 2)
+            near = swap(grad_home, "rep", 1)
+            returned.append([grad_home, near, grad_far, swap(grad_far, "rep", 1)])
+        return sent, returned
+
+    grads, waiting = [], []
+    (branches, (home_first, to_home_first)) = codes[0]
+    home = logits[0][0]
+    sent = leaving(home, sib, home_first)
+    for m in range(micro_count):
+        last = m + 1 == micro_count
+        first, (arrived, settled) = move_pairs(
+            sent[0], branches[0], pairs, first_beside, [] if last else [logits[m + 1][1]], waiting
+        )
+        coming = [] if last else [(logits[m + 1][0], arrived[0], codes[m + 1][1][0])]
+        second, (sents, returned) = move_pairs(
+            after(sent[1], first), branches[1], pairs, second_beside, coming, settled
+        )
+        grads += returned
+        waiting = [(home, sib, first, second, to_home_first)]
+        if not last:
+            (branches, (home_first, to_home_first)) = codes[m + 1]
+            home, sib, sent = logits[m + 1][0], arrived[0], sents[0]
+    [(grad_home, grad_sib)] = [settle(*group) for group in waiting]
+    grad_far = swap(grad_sib, "rep", 2)
+    near = swap(grad_home, "rep", 1)
+    grads = [[after(block, near) for block in group] for group in grads]
+    grads.append([grad_home, near, grad_far, swap(grad_far, "rep", 1)])
 
     def back(first, second):
         gradient = jnp.concatenate([first, second], axis=0)
@@ -227,18 +224,13 @@
         )
         return partial + swap(partial.astype(jnp.bfloat16), "voc", 1).astype(jnp.float32)
 
-    state_parts = []
-    for m in range(micro_count):
-        near, far = back(*grads[m][:2]), back(*grads[m][2:])
-        state_parts.append(
-            jnp.einsum(
-                "ei,ew->iw",
-                onehot_chip[m],
-                jnp.concatenate([near, far], axis=0).astype(jnp.bfloat16),
-                preferred_element_type=jnp.float32,
-            )
-        )
-    state_grad = jnp.stack(state_parts).astype(jnp.bfloat16)
+    canon = []
+    for group in grads:
+        near, far = back(*group[:2]), back(*group[2:])
+        canon.append(jnp.concatenate([near, far], axis=0).astype(jnp.bfloat16))
+    state_grad = jnp.einsum(
+        "mei,mew->miw", onehot_chip, jnp.stack(canon), preferred_element_type=jnp.float32
+    ).astype(jnp.bfloat16)
     head_grad = head_gradient(
         chip_rows.reshape(micro_count * row_count, half_width), sum(grads, [])
     )
@@ -287,7 +279,7 @@
 
 def solution(mesh):
     replicas = mesh.shape["rep"] // 2
-    few = replicas % 2 == 0 and math.factorial(replicas // 2) <= max_branches
+    few = replicas % 2 == 0 and math.factorial(replicas // 2) <= max_permutations
     few = few and mesh.shape["voc"] == 2
     return jax.shard_map(
         paired_body if few else spread_body,

time: 83.6 us -> 81.6 us (0.976); the launches traced: 84.1 us -> 80.9 us
  waiting for transfers between devices: 36.7 us -> 26.3 us
  starting transfers between devices: 18.5 us -> 28.2 us
  other arithmetic: 6.23 us -> 2.98 us
  between operations: 4.49 us -> 5.97 us
  local copies, waits for them, and re-layouts: 3.16 us -> 2.32 us
    ppermute x4, waiting for transfers between devices: 29.2 us -> 16.4 us  [one(): moved = lax.ppermute(moved, 'rep', route)]
    ppermute x4, starting transfers between devices: 8.71 us -> 15.3 us  [one(): moved = lax.ppermute(moved, 'rep', route)]
    ppermute x14, starting transfers between devices: 9.79 us -> 13 us  [swap(): return lax.ppermute(block, axis, [(i, i ^ bit) for i in range(count)])]
    ppermute x14, waiting for transfers between devices: 7.49 us -> 9.94 us  [swap(): return lax.ppermute(block, axis, [(i, i ^ bit) for i in range(count)])]
    select_n x3, other arithmetic: 2.15 us -> 1.11 us  [leaving(): return (jnp.where(home_first, home, sib), jnp.where(home_first, sib, home))]
    another operation x5 -> x0, other arithmetic: 0.88 us -> none  [the longest x1 0.8 us: paired_body(): state_grad = jnp.stack(state_parts).astype(jnp.bfloat16)]
  transfers between devices with their start and end apart: 18 -> 18, of which waited for: 9 -> 9; matrix products, arithmetic and copies ran while one was open for 11% -> 9% of each run, Pallas kernels for 7% -> 7%
where the time goes in v4:
time: 81.6 us; the launch traced here: 80.9 us
  starting transfers between devices  28.2 us (35%)
  waiting for transfers between devices  26.3 us (32%)
  matrix products  9.09 us (11%)
  between operations  5.97 us (7%)
  Pallas kernels  5.6 us (7%)
  other arithmetic  2.98 us (4%)
  local copies, waits for them, and re-layouts  2.32 us (3%)
    ppermute x4, waiting for transfers between devices, one(): moved = lax.ppermute(moved, 'rep', route)  16.4 us
    ppermute x4, starting transfers between devices, one(): moved = lax.ppermute(moved, 'rep', route)  15.3 us
    ppermute x14, starting transfers between devices, swap(): return lax.ppermute(block, axis, [(i, i ^ bit) for i in range(count)])  13 us
    ppermute x14, waiting for transfers between devices, swap(): return lax.ppermute(block, axis, [(i, i ^ bit) for i in range(count)])  9.94 us
    dot_general x4, matrix products, back(): jnp.einsum('rv,wv->rw', gradient, head_weight, preferred_element_type=jnp...  4.36 us
    pallas_call x1, Pallas kernels, head_gradient(): pl.pallas_call(head_kernel, grid=(vocab // step,), out_shape=jax.ShapeDty...  4.16 us
  transfers between devices with their start and end apart: 18, of which 9 were waited for; matrix products, arithmetic and copies ran while one was open for 9% of the time, Pallas kernels for 7%

profile of v4, /device:TPU:0, one launch (start us, length us, event | category | flops | bytes accessed | tf_op | source)
XLA Modules:
  0.0 80.9 jit_solution(13481420701809456090)
XLA Ops:
  0.7 0.8 %constant_dynamic-slice_fusion = s32[2,1,256]{2,1,0:T(1,128)S(1)} fusion(s32[2,8,256]{2,1,0:T(8,128)} %param.103, s32[]{:T(128)S(6)} %select_n.266), kind=kLoop, calls=%fused_computation.126 | loop fusion | bytes 4100 | tf_op jit(solution)/shard_map/jit(dynamic_index_in_dim)/dynamic_slice | solution.py:148
  1.7 1.2 %convolution_convert_fusion.2 = bf16[256,384]{1,0:T(8,128)(2,1)S(1)} fusion(pred[2,256,256]{2,1,0:T(32,128)(4,1)S(1)} %broadcast_compare_fusion, bf16[2,256,384]{2,1,0:T(8,128)(2,1)} %param.100), kind=kOutput, calls=%fused_computation.50 | convolution fusion | flops 50429952 | bytes 458752 | tf_op jit(solution)/shard_map/dot_general | solution.py:161
  6.2 3.0 %collective-permute-start.190 = (bf16[64,2048]{1,0:T(8,128)(2,1)S(1)}, bf16[64,2048]{1,0:T(8,128)(2,1)S(1)}, u32[]{:S(2)}, u32[]{:S(2)}) collective-permute-start(bf16[64,2048]{1,0:T(8,128)(2,1)S(1)} %fusion.2), channel_id=1, source_target_pairs={{0,4},{2,6},{4,0},{6,2},{8,12},{10,14},{12,8},{14,10},{16,20},{18,... | collective-permute-start | bytes 786440 | tf_op jit(solution)/shard_map/ppermute | solution.py:88
  9.3 1.4 %shard_map.59 = (s32[1]{0:T(128)}, s32[1]{0:T(128)}, s32[1]{0:T(128)}, s32[1]{0:T(128)}, s32[4,128]{1,0:T(4,128)S(1)}) custom-call(s32[2,8]{1,0:T(2,128)S(1)} %copy-done.1), custom_call_target="tpu_custom_call" | custom-call | tf_op jit(solution)/shard_map/pallas_call | solution.py:61
  10.8 0.6 fusion.58
  16.6 9.0 %conditional.6 = (bf16[64,2048]{1,0:T(8,128)(2,1)S(1)}, bf16[64,2048]{1,0:T(8,128)(2,1)}) conditional(s32[]{:T(128)} %bitcast.53, (bf16[64,2048]{1,0:T(8,128)(2,1)S(1)}, bf16[64,2048]{1,0:T(8,128)(2,1)S(1)}) %tuple.572, (bf16[64,2048]{1,0:T(8,128)(2,1)S(1)}, bf16[64,2048]{1,0:T(8,128)(2,1)S(1)}) %tuple.573, ...), branch_computations={%region_0.1_spmd, %region_1.2_spmd, %region_2.3_spmd, %region_3.4_... | conditional | bytes 2621536 | solution.py:83
  16.6 0.7 collective-permute-start.5
  17.3 1.4 %collective-permute-start.6 = (bf16[64,2048]{1,0:T(8,128)(2,1)S(1)}, bf16[64,2048]{1,0:T(8,128)(2,1)}, u32[]{:S(2)}, u32[]{:S(2)}) collective-permute-start(bf16[64,2048]{1,0:T(8,128)(2,1)S(1)} %get-tuple-element.746), channel_id=1, source_target_pairs={{0,4},{2,6},{4,0},{6,2},{8,12},{10,14},{12,8},{14,10},{16,20},{18,... | collective-permute-start | bytes 786440 | tf_op jit(solution)/shard_map/cond/branch_3_fun/ppermute | solution.py:88
  18.7 6.8 %collective-permute-done.6 = bf16[64,2048]{1,0:T(8,128)(2,1)} collective-permute-done((bf16[64,2048]{1,0:T(8,128)(2,1)S(1)}, bf16[64,2048]{1,0:T(8,128)(2,1)}, u32[]{:S(2)}, u32[]{:S(2)}) %collective-permute-start.6) | collective-permute-done | bytes 262176 | tf_op jit(solution)/shard_map/cond/branch_3_fun/ppermute | solution.py:88
  25.5 12.7 %conditional.7 = (bf16[64,2048]{1,0:T(8,128)(2,1)S(1)}, pred[64,2048]{1,0:T(8,128)(4,1)S(1)}, pred[64,2048]{1,0:T(8,128)(4,1)S(1)}, bf16[64,2048]{1,0:T(8,128)(2,1)S(1)}, bf16[64,2048]{1,0:T(8,128)(2,1)}) conditional(s32[]{:T(128)} %bitcast.55, (pred[1,1]{1,0:T(4,128)(4,1)}, bf16[64,2048]{1,0:T(8,128)(2,1)S(1)}, ...), branch_computations={%region_24.25_spmd, %region_25.26_spmd, %region_26.27_spmd, %regio... | conditional | bytes 1835090 | solution.py:83
  25.5 6.1 %collective-permute-start.54 = (bf16[64,2048]{1,0:T(8,128)(2,1)S(1)}, bf16[64,2048]{1,0:T(8,128)(2,1)S(1)}, u32[]{:S(2)}, u32[]{:S(2)}) collective-permute-start(bf16[64,2048]{1,0:T(8,128)(2,1)S(1)} %get-tuple-element.819), channel_id=1, source_target_pairs={{0,8},{2,10},{4,12},{6,14},{8,16},{10,18},{12,20},{14,22},{16,0},{... | collective-permute-start | bytes 786440 | tf_op jit(solution)/shard_map/cond/branch_8_fun/ppermute | solution.py:79
  31.7 6.3 %collective-permute-done.54 = bf16[64,2048]{1,0:T(8,128)(2,1)S(1)} collective-permute-done((bf16[64,2048]{1,0:T(8,128)(2,1)S(1)}, bf16[64,2048]{1,0:T(8,128)(2,1)S(1)}, u32[]{:S(2)}, u32[]{:S(2)}) %collective-permute-start.54) | collective-permute-done | bytes 262176 | tf_op jit(solution)/shard_map/cond/branch_8_fun/ppermute | solution.py:79
  38.2 1.0 %fusion.57 = (bf16[64,2048]{1,0:T(8,128)(2,1)S(1)}, bf16[64,2048]{1,0:T(8,128)(2,1)S(1)}) fusion(pred[64,2048]{1,0:T(8,128)(4,1)S(1)} %get-tuple-element.1136, bf16[64,2048]{1,0:T(8,128)(2,1)} %get-tuple-element.1138, bf16[64,2048]{1,0:T(8,128)(2,1)S(1)} %get-tuple-element.1137), kind=kLoop, calls=%fused_computation.132 | loop fusion | flops 262144 | bytes 1179648 | tf_op jit(solution)/shard_map/cond/branch_0_fun/jit(_where)/select_n | solution.py:182
  39.2 8.4 %conditional.10 = (bf16[64,2048]{1,0:T(8,128)(2,1)S(1)}, bf16[64,2048]{1,0:T(8,128)(2,1)S(1)}, bf16[64,2048]{1,0:T(8,128)(2,1)S(1)}) conditional(s32[]{:T(128)} %bitcast.50, (bf16[64,2048]{1,0:T(8,128)(2,1)S(1)}, pred[1,1]{1,0:T(4,128)(4,1)}, bf16[64,2048]{1,0:T(8,128)(2,1)S(1)}, bf16[64,2048]{1,0:T(8,128)(2,1)S(1)}, ...), branch_computations={%region_48.49_spmd, %region_49.50_spmd, %region_50.51_spmd, %regio... | conditional | flops 1572864 | bytes 3145793
  39.3 1.8 %collective-permute-start.181 = (bf16[64,2048]{1,0:T(8,128)(2,1)S(1)}, bf16[64,2048]{1,0:T(8,128)(2,1)S(1)}, u32[]{:S(2)}, u32[]{:S(2)}) collective-permute-start(bf16[64,2048]{1,0:T(8,128)(2,1)S(1)} %get-tuple-element.985), channel_id=1, source_target_pairs={{0,16},{2,18},{4,20},{6,22},{8,24},{10,26},{12,28},{14,30},{16,8},... | collective-permute-start | bytes 786440 | tf_op jit(solution)/shard_map/cond/branch_17_fun/ppermute | solution.py:79
  41.3 6.4 %collective-permute-done.181 = bf16[64,2048]{1,0:T(8,128)(2,1)S(1)} collective-permute-done((bf16[64,2048]{1,0:T(8,128)(2,1)S(1)}, bf16[64,2048]{1,0:T(8,128)(2,1)S(1)}, u32[]{:S(2)}, u32[]{:S(2)}) %collective-permute-start.181) | collective-permute-done | bytes 262176 | tf_op jit(solution)/shard_map/cond/branch_17_fun/ppermute | solution.py:79
  47.7 0.7 copy-done.2
  48.4 12.9 %conditional.9 = (bf16[64,2048]{1,0:T(8,128)(2,1)S(1)}, bf16[64,2048]{1,0:T(8,128)(2,1)}, bf16[64,2048]{1,0:T(8,128)(2,1)}, bf16[64,2048]{1,0:T(8,128)(2,1)}) conditional(s32[]{:T(128)} %bitcast.57, (bf16[64,2048]{1,0:T(8,128)(2,1)S(1)}, bf16[64,2048]{1,0:T(8,128)(2,1)S(1)}, ...), branch_computations={%region_72.73_spmd, %region_73.74_spmd, %region_74.75_spmd, %regio... | conditional | bytes 4718784 | solution.py:83
  48.4 1.9 %collective-permute-start.155 = (bf16[64,2048]{1,0:T(8,128)(2,1)S(1)}, bf16[64,2048]{1,0:T(8,128)(2,1)}, u32[]{:S(2)}, u32[]{:S(2)}) collective-permute-start(bf16[64,2048]{1,0:T(8,128)(2,1)S(1)} %get-tuple-element.1092), channel_id=1, source_target_pairs={{0,4},{2,6},{4,0},{6,2},{8,12},{10,14},{12,8},{14,10},{16,20},{18,... | collective-permute-start | bytes 786440 | tf_op jit(solution)/shard_map/cond/branch_21_fun/ppermute | solution.py:88
  50.3 6.7 %collective-permute-start.153 = (bf16[64,2048]{1,0:T(8,128)(2,1)S(1)}, bf16[64,2048]{1,0:T(8,128)(2,1)S(1)}, u32[]{:S(2)}, u32[]{:S(2)}) collective-permute-start(bf16[64,2048]{1,0:T(8,128)(2,1)S(1)} %get-tuple-element.1090), channel_id=1, source_target_pairs={{0,24},{2,26},{4,28},{6,30},{8,8},{10,10},{12,12},{14,14},{16,16},... | collective-permute-start | bytes 786440 | tf_op jit(solution)/shard_map/cond/branch_21_fun/ppermute | solution.py:79
  57.5 3.8 %collective-permute-done.153 = bf16[64,2048]{1,0:T(8,128)(2,1)S(1)} collective-permute-done((bf16[64,2048]{1,0:T(8,128)(2,1)S(1)}, bf16[64,2048]{1,0:T(8,128)(2,1)S(1)}, u32[]{:S(2)}, u32[]{:S(2)}) %collective-permute-start.153) | collective-permute-done | bytes 262176 | tf_op jit(solution)/shard_map/cond/branch_21_fun/ppermute | solution.py:79
  61.3 1.3 %multiply_convert_fusion.49 = (bf16[64,2048]{1,0:T(8,128)(2,1)S(1)}, bf16[64,2048]{1,0:T(8,128)(2,1)S(1)}) fusion(bf16[64,2048]{1,0:T(8,128)(2,1)S(1)} %get-tuple-element.1137, bf16[64,2048]{1,0:T(8,128)(2,1)} %copy-done.2, bf16[64,2048]{1,0:T(8,128)(2,1)S(1)} %get-tuple-element.1144, pred[]{:T(512)} %bitcast.56, bf16[64,2048]{1,0:T(8,128)(2,1)} %get-tuple-element.1134), kind=kLoop, calls=%fused_computation.79 | loop fusion | flops 1572864 | bytes 1572865 | tf_op jit(solution)/shard_map/convert_element_type | solution.py:93
  63.3 0.9 %collective-permute-done.191.refs_6_ = bf16[64,2048]{1,0:T(8,128)(2,1)S(1)} collective-permute-done((bf16[64,2048]{1,0:T(8,128)(2,1)S(1)}, bf16[64,2048]{1,0:T(8,128)(2,1)S(1)}, u32[]{:S(2)}, u32[]{:S(2)}) %collective-permute-start.191) | collective-permute-done | bytes 262176 | tf_op jit(solution)/shard_map/ppermute | solution.py:88
  64.8 1.6 %collective-permute-start.194 = (bf16[128,384]{1,0:T(8,128)(2,1)S(1)}, bf16[128,384]{1,0:T(8,128)(2,1)S(1)}, u32[]{:S(2)}, u32[]{:S(2)}) collective-permute-start(bf16[128,384]{1,0:T(8,128)(2,1)S(1)} %get-tuple-element.1222), channel_id=1, source_target_pairs={{0,1},{1,0},{2,3},{3,2},{4,5},{5,4},{6,7},{7,6},{8,9},{9,8},{10,11... | collective-permute-start | bytes 294920 | tf_op jit(solution)/shard_map/ppermute | solution.py:88
  66.4 1.6 %fusion.61 = (bf16[128,384]{1,0:T(8,128)(2,1)S(1)}, f32[128,384]{1,0:T(8,128)S(1)}) fusion(bf16[384,2048]{1,0:T(8,128)(2,1)S(1)} %copy-done, bf16[64,2048]{1,0:T(8,128)(2,1)} %get-tuple-element.1151.refs_4_, bf16[64,2048]{1,0:T(8,128)(2,1)} %get-tuple-element.1149.refs_3_), kind=kOutput, calls=%fused_computation.136 | convolution fusion | flops 202424320 | bytes 2392064 | tf_op jit(solution)/shard_map/rv,wv->rw/dot_general | solution.py:222
  68.0 0.6 collective-permute-start.193
  68.6 1.5 %fusion.62 = (bf16[128,384]{1,0:T(8,128)(2,1)S(1)}, f32[128,384]{1,0:T(8,128)S(1)}) fusion(bf16[384,2048]{1,0:T(8,128)(2,1)S(1)} %copy-done, bf16[64,2048]{1,0:T(8,128)(2,1)} %get-tuple-element.1147.refs_2_, bf16[64,2048]{1,0:T(8,128)(2,1)S(1)} %get-tuple-element.1145.refs_1_), kind=kOutput, calls=%fused_computation.137 | convolution fusion | flops 202424320 | bytes 2392064 | tf_op jit(solution)/shard_map/rv,wv->rw/dot_general | solution.py:222
  70.2 1.6 %collective-permute-start.192 = (bf16[128,384]{1,0:T(8,128)(2,1)S(1)}, bf16[128,384]{1,0:T(8,128)(2,1)S(1)}, u32[]{:S(2)}, u32[]{:S(2)}) collective-permute-start(bf16[128,384]{1,0:T(8,128)(2,1)S(1)} %get-tuple-element.1226), channel_id=1, source_target_pairs={{0,1},{1,0},{2,3},{3,2},{4,5},{5,4},{6,7},{7,6},{8,9},{9,8},{10,11... | collective-permute-start | bytes 294920 | tf_op jit(solution)/shard_map/ppermute | solution.py:88
  71.9 1.1 %collective-permute-done.193 = bf16[128,384]{1,0:T(8,128)(2,1)S(1)} collective-permute-done((bf16[128,384]{1,0:T(8,128)(2,1)S(1)}, bf16[128,384]{1,0:T(8,128)(2,1)S(1)}, u32[]{:S(2)}, u32[]{:S(2)}) %collective-permute-start.193) | collective-permute-done | bytes 98336 | tf_op jit(solution)/shard_map/ppermute | solution.py:88
  74.0 1.6 %collective-permute-start.197 = (bf16[128,384]{1,0:T(8,128)(2,1)S(1)}, bf16[128,384]{1,0:T(8,128)(2,1)S(1)}, u32[]{:S(2)}, u32[]{:S(2)}) collective-permute-start(bf16[128,384]{1,0:T(8,128)(2,1)S(1)} %get-tuple-element.1220), channel_id=1, source_target_pairs={{0,1},{1,0},{2,3},{3,2},{4,5},{5,4},{6,7},{7,6},{8,9},{9,8},{10,11... | collective-permute-start | bytes 294920 | tf_op jit(solution)/shard_map/ppermute | solution.py:88
  75.6 4.2 %shard_map.60 = bf16[384,2048]{1,0:T(8,128)(2,1)} custom-call(bf16[512,384]{1,0:T(8,128)(2,1)S(1)} %bitcast.87, bf16[64,2048]{1,0:T(8,128)(2,1)S(1)} %get-tuple-element.1145.refs_1_, bf16[64,2048]{1,0:T(8,128)(2,1)} %get-tuple-element.1147.refs_2_, bf16[64,2048]{1,0:T(8,128)(2,1)} %get-tuple-element.1149.refs_3_, ...), custom_call_target="tpu_custom_call" | custom-call | flops 805306368 | bytes 4063232 | tf_op jit(solution)/shard_map/pallas_call | solution.py:120
  79.7 1.2 %convolution_convert_fusion.1 = bf16[2,256,384]{2,1,0:T(8,128)(2,1)} fusion(bf16[1,128,384]{2,1,0:T(8,128)(2,1)S(1)} %fusion.40, bf16[1,128,384]{2,1,0:T(8,128)(2,1)S(1)} %fusion.39, bf16[1,128,384]{2,1,0:T(8,128)(2,1)S(1)} %fusion.38, bf16[1,128,384]{2,1,0:T(8,128)(2,1)S(1)} %fusion.37, s32[2,256]{1,0:T(2,128)S(1)} %bitcast.90, s32[256]{0:T(256)S(1)} %add_add_fusion.1), kind=kOutput, calls=%fused_computation.49 | convolution fusion | flops 102563840 | bytes 789504 | tf_op jit(solution)/shard_map/mei,mew->miw/dot_general | solution.py:231
  (55 shorter events, 7.0 us)
Async XLA Ops:
  0.6 2.3 %copy-start = (bf16[384,2048]{1,0:T(8,128)(2,1)S(1)}, bf16[384,2048]{1,0:T(8,128)(2,1)}, u32[]{:S(2)}) copy-start(bf16[384,2048]{1,0:T(8,128)(2,1)} %param.101) | copy-start | bytes 4718596
  1.7 2.2 %copy-start.3 = (bf16[2,256,384]{2,1,0:T(8,128)(2,1)S(1)}, bf16[2,256,384]{2,1,0:T(8,128)(2,1)}, u32[]{:S(2)}) copy-start(bf16[2,256,384]{2,1,0:T(8,128)(2,1)} %param.100) | copy-start | bytes 1179652
  3.4 2.8 %collective-permute-start.189 = (f32[128,2048]{1,0:T(8,128)S(1)}, f32[128,2048]{1,0:T(8,128)S(1)}, u32[]{:S(2)}, u32[]{:S(2)}) collective-permute-start(f32[128,2048]{1,0:T(8,128)S(1)} %fusion.41), channel_id=1, source_target_pairs={{0,2},{2,0},{4,6},{6,4},{8,10},{10,8},{12,14},{14,12},{16,18},{18,... | collective-permute-start | bytes 3145736 | tf_op jit(solution)/shard_map/ppermute | solution.py:88
  4.6 4.6 %collective-permute-start.188 = (f32[128,2048]{1,0:T(8,128)S(1)}, f32[128,2048]{1,0:T(8,128)S(1)}, u32[]{:S(2)}, u32[]{:S(2)}) collective-permute-start(f32[128,2048]{1,0:T(8,128)S(1)} %fusion.45), channel_id=1, source_target_pairs={{0,2},{2,0},{4,6},{6,4},{8,10},{10,8},{12,14},{14,12},{16,18},{18,... | collective-permute-start | bytes 3145736 | tf_op jit(solution)/shard_map/ppermute | solution.py:88
  6.2 3.1 %copy-start.1 = (s32[2,8]{1,0:T(2,128)S(1)}, s32[2,8]{1,0:T(2,128)}, u32[]{:S(2)}) copy-start(s32[2,8]{1,0:T(2,128)} %order_ref) | copy-start | bytes 196
  6.2 10.2 %collective-permute-start.190 = (bf16[64,2048]{1,0:T(8,128)(2,1)S(1)}, bf16[64,2048]{1,0:T(8,128)(2,1)S(1)}, u32[]{:S(2)}, u32[]{:S(2)}) collective-permute-start(bf16[64,2048]{1,0:T(8,128)(2,1)S(1)} %fusion.2), channel_id=1, source_target_pairs={{0,4},{2,6},{4,0},{6,2},{8,12},{10,14},{12,8},{14,10},{16,20},{18,... | collective-permute-start | bytes 786440 | tf_op jit(solution)/shard_map/ppermute | solution.py:88
  16.6 2.1 %collective-permute-start.5 = (bf16[64,2048]{1,0:T(8,128)(2,1)S(1)}, bf16[64,2048]{1,0:T(8,128)(2,1)S(1)}, u32[]{:S(2)}, u32[]{:S(2)}) collective-permute-start(bf16[64,2048]{1,0:T(8,128)(2,1)S(1)} %get-tuple-element.745), channel_id=1, source_target_pairs={{0,0},{2,2},{4,4},{6,6},{8,16},{10,18},{12,20},{14,22},{16,24},{18... | collective-permute-start | bytes 786440 | tf_op jit(solution)/shard_map/cond/branch_3_fun/ppermute | solution.py:79
  17.3 8.2 %collective-permute-start.6 = (bf16[64,2048]{1,0:T(8,128)(2,1)S(1)}, bf16[64,2048]{1,0:T(8,128)(2,1)}, u32[]{:S(2)}, u32[]{:S(2)}) collective-permute-start(bf16[64,2048]{1,0:T(8,128)(2,1)S(1)} %get-tuple-element.746), channel_id=1, source_target_pairs={{0,4},{2,6},{4,0},{6,2},{8,12},{10,14},{12,8},{14,10},{16,20},{18,... | collective-permute-start | bytes 786440 | tf_op jit(solution)/shard_map/cond/branch_3_fun/ppermute | solution.py:88
  25.5 12.4 %collective-permute-start.54 = (bf16[64,2048]{1,0:T(8,128)(2,1)S(1)}, bf16[64,2048]{1,0:T(8,128)(2,1)S(1)}, u32[]{:S(2)}, u32[]{:S(2)}) collective-permute-start(bf16[64,2048]{1,0:T(8,128)(2,1)S(1)} %get-tuple-element.819), channel_id=1, source_target_pairs={{0,8},{2,10},{4,12},{6,14},{8,16},{10,18},{12,20},{14,22},{16,0},{... | collective-permute-start | bytes 786440 | tf_op jit(solution)/shard_map/cond/branch_8_fun/ppermute | solution.py:79
  39.3 8.3 %collective-permute-start.181 = (bf16[64,2048]{1,0:T(8,128)(2,1)S(1)}, bf16[64,2048]{1,0:T(8,128)(2,1)S(1)}, u32[]{:S(2)}, u32[]{:S(2)}) collective-permute-start(bf16[64,2048]{1,0:T(8,128)(2,1)S(1)} %get-tuple-element.985), channel_id=1, source_target_pairs={{0,16},{2,18},{4,20},{6,22},{8,24},{10,26},{12,28},{14,30},{16,8},... | collective-permute-start | bytes 786440 | tf_op jit(solution)/shard_map/cond/branch_17_fun/ppermute | solution.py:79
  47.7 0.7 copy-start.2
  48.4 8.6 %collective-permute-start.155 = (bf16[64,2048]{1,0:T(8,128)(2,1)S(1)}, bf16[64,2048]{1,0:T(8,128)(2,1)}, u32[]{:S(2)}, u32[]{:S(2)}) collective-permute-start(bf16[64,2048]{1,0:T(8,128)(2,1)S(1)} %get-tuple-element.1092), channel_id=1, source_target_pairs={{0,4},{2,6},{4,0},{6,2},{8,12},{10,14},{12,8},{14,10},{16,20},{18,... | collective-permute-start | bytes 786440 | tf_op jit(solution)/shard_map/cond/branch_21_fun/ppermute | solution.py:88
  50.3 11.0 %collective-permute-start.153 = (bf16[64,2048]{1,0:T(8,128)(2,1)S(1)}, bf16[64,2048]{1,0:T(8,128)(2,1)S(1)}, u32[]{:S(2)}, u32[]{:S(2)}) collective-permute-start(bf16[64,2048]{1,0:T(8,128)(2,1)S(1)} %get-tuple-element.1090), channel_id=1, source_target_pairs={{0,24},{2,26},{4,28},{6,30},{8,8},{10,10},{12,12},{14,14},{16,16},... | collective-permute-start | bytes 786440 | tf_op jit(solution)/shard_map/cond/branch_21_fun/ppermute | solution.py:79
  56.9 4.4 %collective-permute-start.154 = (bf16[64,2048]{1,0:T(8,128)(2,1)S(1)}, bf16[64,2048]{1,0:T(8,128)(2,1)}, u32[]{:S(2)}, u32[]{:S(2)}) collective-permute-start(bf16[64,2048]{1,0:T(8,128)(2,1)S(1)} %get-tuple-element.1091), channel_id=1, source_target_pairs={{0,2},{2,0},{4,6},{6,4},{8,10},{10,8},{12,14},{14,12},{16,18},{18,... | collective-permute-start | bytes 786440 | tf_op jit(solution)/shard_map/cond/branch_21_fun/ppermute | solution.py:88
  57.0 4.3 %collective-permute-start.156 = (bf16[64,2048]{1,0:T(8,128)(2,1)}, bf16[64,2048]{1,0:T(8,128)(2,1)}, u32[]{:S(2)}, u32[]{:S(2)}) collective-permute-start(bf16[64,2048]{1,0:T(8,128)(2,1)} %collective-permute-done.155), channel_id=1, source_target_pairs={{0,2},{2,0},{4,6},{6,4},{8,10},{10,8},{12,14},{14,12},{16,18},{18,... | collective-permute-start | bytes 786440 | tf_op jit(solution)/shard_map/cond/branch_21_fun/ppermute | solution.py:88
  61.3 1.4 %copy-start.4 = (bf16[2,256,384]{2,1,0:T(8,128)(2,1)S(1)}, bf16[2,256,384]{2,1,0:T(8,128)(2,1)}, u32[]{:S(2)}) copy-start(bf16[2,256,384]{2,1,0:T(8,128)(2,1)} %param.100) | copy-start | bytes 1179652
  62.6 1.6 %collective-permute-start.191 = (bf16[64,2048]{1,0:T(8,128)(2,1)S(1)}, bf16[64,2048]{1,0:T(8,128)(2,1)S(1)}, u32[]{:S(2)}, u32[]{:S(2)}) collective-permute-start(bf16[64,2048]{1,0:T(8,128)(2,1)S(1)} %get-tuple-element.1214.refs_5_), channel_id=1, source_target_pairs={{0,2},{2,0},{4,6},{6,4},{8,10},{10,8},{12,14},{14,12},{16,18},{18,... | collective-permute-start | bytes 786440 | tf_op jit(solution)/shard_map/ppermute | solution.py:88
  63.1 8.8 %collective-permute-start.195 = (bf16[64,2048]{1,0:T(8,128)(2,1)S(1)}, bf16[64,2048]{1,0:T(8,128)(2,1)S(1)}, u32[]{:S(2)}, u32[]{:S(2)}) collective-permute-start(bf16[64,2048]{1,0:T(8,128)(2,1)S(1)} %get-tuple-element.1215), channel_id=1, source_target_pairs={{0,4},{2,6},{4,0},{6,2},{8,12},{10,14},{12,8},{14,10},{16,20},{18,... | collective-permute-start | bytes 786440 | tf_op jit(solution)/shard_map/ppermute | solution.py:88
  64.8 7.0 %collective-permute-start.194 = (bf16[128,384]{1,0:T(8,128)(2,1)S(1)}, bf16[128,384]{1,0:T(8,128)(2,1)S(1)}, u32[]{:S(2)}, u32[]{:S(2)}) collective-permute-start(bf16[128,384]{1,0:T(8,128)(2,1)S(1)} %get-tuple-element.1222), channel_id=1, source_target_pairs={{0,1},{1,0},{2,3},{3,2},{4,5},{5,4},{6,7},{7,6},{8,9},{9,8},{10,11... | collective-permute-start | bytes 294920 | tf_op jit(solution)/shard_map/ppermute | solution.py:88
  68.0 5.0 %collective-permute-start.193 = (bf16[128,384]{1,0:T(8,128)(2,1)S(1)}, bf16[128,384]{1,0:T(8,128)(2,1)S(1)}, u32[]{:S(2)}, u32[]{:S(2)}) collective-permute-start(bf16[128,384]{1,0:T(8,128)(2,1)S(1)} %get-tuple-element.1224), channel_id=1, source_target_pairs={{0,1},{1,0},{2,3},{3,2},{4,5},{5,4},{6,7},{7,6},{8,9},{9,8},{10,11... | collective-permute-start | bytes 294920 | tf_op jit(solution)/shard_map/ppermute | solution.py:88
  70.2 5.4 %collective-permute-start.192 = (bf16[128,384]{1,0:T(8,128)(2,1)S(1)}, bf16[128,384]{1,0:T(8,128)(2,1)S(1)}, u32[]{:S(2)}, u32[]{:S(2)}) collective-permute-start(bf16[128,384]{1,0:T(8,128)(2,1)S(1)} %get-tuple-element.1226), channel_id=1, source_target_pairs={{0,1},{1,0},{2,3},{3,2},{4,5},{5,4},{6,7},{7,6},{8,9},{9,8},{10,11... | collective-permute-start | bytes 294920 | tf_op jit(solution)/shard_map/ppermute | solution.py:88
  71.8 1.5 %collective-permute-start.196 = (bf16[64,2048]{1,0:T(8,128)(2,1)S(1)}, bf16[64,2048]{1,0:T(8,128)(2,1)S(1)}, u32[]{:S(2)}, u32[]{:S(2)}) collective-permute-start(bf16[64,2048]{1,0:T(8,128)(2,1)S(1)} %collective-permute-done.195.refs_7_), channel_id=1, source_target_pairs={{0,2},{2,0},{4,6},{6,4},{8,10},{10,8},{12,14},{14,12},{16,18},{18,... | collective-permute-start | bytes 786440 | tf_op jit(solution)/shard_map/ppermute | solution.py:88
  74.0 5.7 %collective-permute-start.197 = (bf16[128,384]{1,0:T(8,128)(2,1)S(1)}, bf16[128,384]{1,0:T(8,128)(2,1)S(1)}, u32[]{:S(2)}, u32[]{:S(2)}) collective-permute-start(bf16[128,384]{1,0:T(8,128)(2,1)S(1)} %get-tuple-element.1220), channel_id=1, source_target_pairs={{0,1},{1,0},{2,3},{3,2},{4,5},{5,4},{6,7},{7,6},{8,9},{9,8},{10,11... | collective-permute-start | bytes 294920 | tf_op jit(solution)/shard_map/ppermute | solution.py:88

commit v5 on v4

--- a/solution.py
+++ b/solution.py
@@ -55,20 +55,20 @@
             flags_ref[at : at + 1, :] = jnp.full((1, flags_ref.shape[1]), color[moved], jnp.int32)
 
 
-def routes(pair_order):
+def routes(pair_order, width):
     micro_count, replicas = pair_order.shape
     smem = pl.BlockSpec(memory_space=pltpu.SMEM)
     *branches, flags = pl.pallas_call(
         route_kernel,
         out_shape=[jax.ShapeDtypeStruct((1,), jnp.int32)] * (2 * micro_count)
-        + [jax.ShapeDtypeStruct((2 * micro_count, 128), jnp.int32)],
+        + [jax.ShapeDtypeStruct((2 * micro_count, width), jnp.int32)],
         in_specs=[smem],
         out_specs=[smem] * (2 * micro_count) + [pl.BlockSpec(memory_space=pltpu.VMEM)],
         scratch_shapes=[pltpu.SMEM((replicas,), jnp.int32)] * 3,
         compiler_params=pltpu.CompilerParams(vmem_limit_bytes=1 << 20),
     )(pair_order)
     branch = [number.reshape(()) for number in branches]
-    flag = [flags[at : at + 1, :1] == 0 for at in range(2 * micro_count)]
+    flag = [flags[at : at + 1] == 0 for at in range(2 * micro_count)]
     return [(branch[2 * m : 2 * m + 2], flag[2 * m : 2 * m + 2]) for m in range(micro_count)]
 
 
@@ -167,12 +167,7 @@
         home = (own[:quarter] + arrived[:quarter]).astype(jnp.bfloat16)
         logits.append((home, far))
     sib = swap(logits[0][1], "rep", 2)
-    codes = routes(after(pair_order, *logits[-1]))
-    chip_rows = jnp.einsum(
-        "mei,miw->mew", onehot_chip, after(states, *logits[-1]), preferred_element_type=jnp.float32
-    )
-    chip_rows = chip_rows.astype(jnp.bfloat16)
-
+    codes = routes(after(pair_order, *logits[-1]), head_weight.shape[1])
     def settle(home, sib, first, second, to_home_first):
         grad_home = difference(home, jnp.where(to_home_first, first, second))
         grad_sib = difference(sib, jnp.where(to_home_first, second, first))
@@ -215,6 +210,10 @@
     grad_far = swap(grad_sib, "rep", 2)
     near = swap(grad_home, "rep", 1)
     grads = [[after(block, near) for block in group] for group in grads]
+    chip_rows = jnp.einsum(
+        "mei,miw->mew", onehot_chip, after(states, near), preferred_element_type=jnp.float32
+    )
+    chip_rows = chip_rows.astype(jnp.bfloat16)
     grads.append([grad_home, near, grad_far, swap(grad_far, "rep", 1)])
 
     def back(first, second):

time: 81.6 us -> 79 us (0.968)
  starting transfers between devices: 28.2 us -> 24.9 us
  between operations: 5.97 us -> 3.46 us
  waiting for transfers between devices: 26.3 us -> 27.4 us
    ppermute x4, waiting for transfers between devices: 16.4 us -> 20.8 us  [one(): moved = lax.ppermute(moved, 'rep', route)]
    ppermute x14, waiting for transfers between devices: 9.94 us -> 6.6 us  [swap(): return lax.ppermute(block, axis, [(i, i ^ bit) for i in range(count)])]
    ppermute x4, starting transfers between devices: 15.3 us -> 13.1 us  [one(): moved = lax.ppermute(moved, 'rep', route)]
    ppermute x14, starting transfers between devices: 13 us -> 11.8 us  [swap(): return lax.ppermute(block, axis, [(i, i ^ bit) for i in range(count)])]
    unnamed x12, local copies, waits for them, and re-layouts: 0.75 us -> 1.71 us
where the time goes in v5:
time: 79 us; the launch traced here: 77.5 us
  waiting for transfers between devices  27.4 us (35%)
  starting transfers between devices  24.9 us (32%)
  matrix products  9.09 us (12%)
  Pallas kernels  5.6 us (7%)
  other arithmetic  3.72 us (5%)
  between operations  3.46 us (4%)
  local copies, waits for them, and re-layouts  2.68 us (3%)
    ppermute x4, waiting for transfers between devices, one(): moved = lax.ppermute(moved, 'rep', route)  20.8 us
    ppermute x4, starting transfers between devices, one(): moved = lax.ppermute(moved, 'rep', route)  13.1 us
    ppermute x14, starting transfers between devices, swap(): return lax.ppermute(block, axis, [(i, i ^ bit) for i in range(count)])  11.8 us
    ppermute x14, waiting for transfers between devices, swap(): return lax.ppermute(block, axis, [(i, i ^ bit) for i in range(count)])  6.6 us
    dot_general x4, matrix products, back(): jnp.einsum('rv,wv->rw', gradient, head_weight, preferred_element_type=jnp...  4.36 us
    pallas_call x1, Pallas kernels, head_gradient(): pl.pallas_call(head_kernel, grid=(vocab // step,), out_shape=jax.ShapeDty...  4.16 us
    select_n x3, other arithmetic, leaving(): return (jnp.where(home_first, home, sib), jnp.where(home_first, sib, home))  1.82 us
    unnamed x12, local copies, waits for them, and re-layouts  1.71 us
  transfers between devices with their start and end apart: 18, of which 9 were waited for; matrix products, arithmetic and copies ran while one was open for 9% of the time, Pallas kernels for 7%

profile of v5, /device:TPU:0, one launch (start us, length us, event | category | flops | bytes accessed | tf_op | source)
XLA Modules:
  0.0 77.5 jit_solution(8579630377128675108)
XLA Ops:
  0.7 0.8 %constant_dynamic-slice_fusion = s32[2,1,256]{2,1,0:T(1,128)S(1)} fusion(s32[2,8,256]{2,1,0:T(8,128)} %param.103, s32[]{:T(128)S(6)} %select_n.266), kind=kLoop, calls=%fused_computation.130 | loop fusion | bytes 4100 | tf_op jit(solution)/shard_map/jit(dynamic_index_in_dim)/dynamic_slice | solution.py:148
  1.7 1.2 %convolution_convert_fusion.2 = bf16[256,384]{1,0:T(8,128)(2,1)S(1)} fusion(pred[2,256,256]{2,1,0:T(32,128)(4,1)S(1)} %broadcast_compare_fusion, bf16[2,256,384]{2,1,0:T(8,128)(2,1)} %param.100), kind=kOutput, calls=%fused_computation.50 | convolution fusion | flops 50429952 | bytes 458752 | tf_op jit(solution)/shard_map/dot_general | solution.py:161
  6.2 3.0 %collective-permute-start.190 = (bf16[64,2048]{1,0:T(8,128)(2,1)S(1)}, bf16[64,2048]{1,0:T(8,128)(2,1)S(1)}, u32[]{:S(2)}, u32[]{:S(2)}) collective-permute-start(bf16[64,2048]{1,0:T(8,128)(2,1)S(1)} %fusion.2), channel_id=1, source_target_pairs={{0,4},{2,6},{4,0},{6,2},{8,12},{10,14},{12,8},{14,10},{16,20},{18,... | collective-permute-start | bytes 786440 | tf_op jit(solution)/shard_map/ppermute | solution.py:88
  9.3 1.4 %shard_map.59 = (s32[1]{0:T(128)}, s32[1]{0:T(128)}, s32[1]{0:T(128)}, s32[1]{0:T(128)}, s32[4,2048]{1,0:T(4,128)S(1)}) custom-call(s32[2,8]{1,0:T(2,128)S(1)} %copy-done.1), custom_call_target="tpu_custom_call" | custom-call | tf_op jit(solution)/shard_map/pallas_call | solution.py:61
  13.4 2.4 %collective-permute-done.190 = bf16[64,2048]{1,0:T(8,128)(2,1)S(1)} collective-permute-done((bf16[64,2048]{1,0:T(8,128)(2,1)S(1)}, bf16[64,2048]{1,0:T(8,128)(2,1)S(1)}, u32[]{:S(2)}, u32[]{:S(2)}) %collective-permute-start.190) | collective-permute-done | bytes 262176 | tf_op jit(solution)/shard_map/ppermute | solution.py:88
  16.0 9.8 %conditional.6 = (bf16[64,2048]{1,0:T(8,128)(2,1)S(1)}, bf16[64,2048]{1,0:T(8,128)(2,1)}) conditional(s32[]{:T(128)} %bitcast.5, (bf16[64,2048]{1,0:T(8,128)(2,1)S(1)}, bf16[64,2048]{1,0:T(8,128)(2,1)S(1)}) %tuple.572, (bf16[64,2048]{1,0:T(8,128)(2,1)S(1)}, bf16[64,2048]{1,0:T(8,128)(2,1)S(1)}) %tuple.573, ...), branch_computations={%region_0.1_spmd, %region_1.2_spmd, %region_2.3_spmd, %region_3.4_... | conditional | bytes 2621536 | solution.py:83
  16.0 1.9 %collective-permute-start.17 = (bf16[64,2048]{1,0:T(8,128)(2,1)S(1)}, bf16[64,2048]{1,0:T(8,128)(2,1)S(1)}, u32[]{:S(2)}, u32[]{:S(2)}) collective-permute-start(bf16[64,2048]{1,0:T(8,128)(2,1)S(1)} %get-tuple-element.757), channel_id=1, source_target_pairs={{0,8},{2,10},{4,12},{6,14},{8,16},{10,18},{12,20},{14,22},{16,24},... | collective-permute-start | bytes 786440 | tf_op jit(solution)/shard_map/cond/branch_9_fun/ppermute | solution.py:79
  17.8 1.5 %collective-permute-start.18 = (bf16[64,2048]{1,0:T(8,128)(2,1)S(1)}, bf16[64,2048]{1,0:T(8,128)(2,1)}, u32[]{:S(2)}, u32[]{:S(2)}) collective-permute-start(bf16[64,2048]{1,0:T(8,128)(2,1)S(1)} %get-tuple-element.758), channel_id=1, source_target_pairs={{0,4},{2,6},{4,0},{6,2},{8,12},{10,14},{12,8},{14,10},{16,20},{18,... | collective-permute-start | bytes 786440 | tf_op jit(solution)/shard_map/cond/branch_9_fun/ppermute | solution.py:88
  19.4 6.3 %collective-permute-done.17 = bf16[64,2048]{1,0:T(8,128)(2,1)S(1)} collective-permute-done((bf16[64,2048]{1,0:T(8,128)(2,1)S(1)}, bf16[64,2048]{1,0:T(8,128)(2,1)S(1)}, u32[]{:S(2)}, u32[]{:S(2)}) %collective-permute-start.17) | collective-permute-done | bytes 262176 | tf_op jit(solution)/shard_map/cond/branch_9_fun/ppermute | solution.py:79
  25.7 13.6 %conditional.7 = (bf16[64,2048]{1,0:T(8,128)(2,1)S(1)}, pred[64,2048]{1,0:T(8,128)(4,1)S(1)}, pred[64,2048]{1,0:T(8,128)(4,1)S(1)}, bf16[64,2048]{1,0:T(8,128)(2,1)S(1)}, bf16[64,2048]{1,0:T(8,128)(2,1)}) conditional(s32[]{:T(128)} %bitcast.6, (pred[1,2048]{1,0:T(4,128)(4,1)S(1)}, bf16[64,2048]{1,0:T(8,128)(2,1)S(1)}, ...), branch_computations={%region_24.25_spmd, %region_25.26_spmd, %region_26.27_spmd, %regio... | conditional | bytes 1843281 | solution.py:83
  25.8 2.0 %collective-permute-start.157 = (bf16[64,2048]{1,0:T(8,128)(2,1)S(1)}, bf16[64,2048]{1,0:T(8,128)(2,1)S(1)}, u32[]{:S(2)}, u32[]{:S(2)}) collective-permute-start(bf16[64,2048]{1,0:T(8,128)(2,1)S(1)} %get-tuple-element.851), channel_id=1, source_target_pairs={{0,16},{2,18},{4,20},{6,22},{8,24},{10,26},{12,28},{14,30},{16,0},... | collective-permute-start | bytes 786440 | tf_op jit(solution)/shard_map/cond/branch_16_fun/ppermute | solution.py:79
  27.8 11.2 %collective-permute-done.157 = bf16[64,2048]{1,0:T(8,128)(2,1)S(1)} collective-permute-done((bf16[64,2048]{1,0:T(8,128)(2,1)S(1)}, bf16[64,2048]{1,0:T(8,128)(2,1)S(1)}, u32[]{:S(2)}, u32[]{:S(2)}) %collective-permute-start.157) | collective-permute-done | bytes 262176 | tf_op jit(solution)/shard_map/cond/branch_16_fun/ppermute | solution.py:79
  39.4 1.7 %fusion.57 = (bf16[64,2048]{1,0:T(8,128)(2,1)S(1)}, bf16[64,2048]{1,0:T(8,128)(2,1)}) fusion(pred[64,2048]{1,0:T(8,128)(4,1)S(1)} %get-tuple-element.1136, bf16[64,2048]{1,0:T(8,128)(2,1)} %get-tuple-element.1138, bf16[64,2048]{1,0:T(8,128)(2,1)S(1)} %get-tuple-element.1137), kind=kLoop, calls=%fused_computation.136 | loop fusion | flops 262144 | bytes 1179648 | tf_op jit(solution)/shard_map/cond/branch_0_fun/jit(_where)/select_n | solution.py:177
  41.0 5.5 %conditional.10 = (bf16[64,2048]{1,0:T(8,128)(2,1)}, bf16[64,2048]{1,0:T(8,128)(2,1)S(1)}, bf16[64,2048]{1,0:T(8,128)(2,1)S(1)}) conditional(s32[]{:T(128)} %bitcast.2, (bf16[64,2048]{1,0:T(8,128)(2,1)S(1)}, pred[1,2048]{1,0:T(4,128)(4,1)S(1)}, bf16[64,2048]{1,0:T(8,128)(2,1)S(1)}, bf16[64,2048]{1,0:T(8,128)(2,1)S(1)}, ...), branch_computations={%region_48.49_spmd, %region_49.50_spmd, %region_50.51_spmd, %regio... | conditional | flops 1572864 | bytes 3151937
  41.0 3.6 %collective-permute-start.168 = (bf16[64,2048]{1,0:T(8,128)(2,1)}, bf16[64,2048]{1,0:T(8,128)(2,1)}, u32[]{:S(2)}, u32[]{:S(2)}) collective-permute-start(bf16[64,2048]{1,0:T(8,128)(2,1)} %get-tuple-element.907), channel_id=1, source_target_pairs={{0,0},{2,2},{4,4},{6,6},{8,24},{10,26},{12,28},{14,30},{16,8},{18,... | collective-permute-start | bytes 786440 | tf_op jit(solution)/shard_map/cond/branch_4_fun/ppermute | solution.py:79
  44.9 1.7 %copy.144 = bf16[64,2048]{1,0:T(8,128)(2,1)} copy(bf16[64,2048]{1,0:T(8,128)(2,1)} %collective-permute-done.168) | data formatting | bytes 524288
  46.5 11.9 %conditional.9 = (bf16[64,2048]{1,0:T(8,128)(2,1)S(1)}, bf16[64,2048]{1,0:T(8,128)(2,1)}, bf16[64,2048]{1,0:T(8,128)(2,1)}, bf16[64,2048]{1,0:T(8,128)(2,1)}) conditional(s32[]{:T(128)} %bitcast.7, (bf16[64,2048]{1,0:T(8,128)(2,1)S(1)}, bf16[64,2048]{1,0:T(8,128)(2,1)S(1)}, ...), branch_computations={%region_72.73_spmd, %region_73.74_spmd, %region_74.75_spmd, %regio... | conditional | bytes 4718784 | solution.py:83
  46.5 1.5 %collective-permute-start.76 = (bf16[64,2048]{1,0:T(8,128)(2,1)S(1)}, bf16[64,2048]{1,0:T(8,128)(2,1)}, u32[]{:S(2)}, u32[]{:S(2)}) collective-permute-start(bf16[64,2048]{1,0:T(8,128)(2,1)S(1)} %get-tuple-element.1050), channel_id=1, source_target_pairs={{0,4},{2,6},{4,0},{6,2},{8,12},{10,14},{12,8},{14,10},{16,20},{18,... | collective-permute-start | bytes 786440 | tf_op jit(solution)/shard_map/cond/branch_7_fun/ppermute | solution.py:88
  48.0 5.7 %collective-permute-start.74 = (bf16[64,2048]{1,0:T(8,128)(2,1)S(1)}, bf16[64,2048]{1,0:T(8,128)(2,1)S(1)}, u32[]{:S(2)}, u32[]{:S(2)}) collective-permute-start(bf16[64,2048]{1,0:T(8,128)(2,1)S(1)} %get-tuple-element.1048), channel_id=1, source_target_pairs={{0,8},{2,10},{4,12},{6,14},{8,0},{10,2},{12,4},{14,6},{16,24},{18,... | collective-permute-start | bytes 786440 | tf_op jit(solution)/shard_map/cond/branch_7_fun/ppermute | solution.py:79
  53.7 1.2 %collective-permute-done.76 = bf16[64,2048]{1,0:T(8,128)(2,1)} collective-permute-done((bf16[64,2048]{1,0:T(8,128)(2,1)S(1)}, bf16[64,2048]{1,0:T(8,128)(2,1)}, u32[]{:S(2)}, u32[]{:S(2)}) %collective-permute-start.76) | collective-permute-done | bytes 262176 | tf_op jit(solution)/shard_map/cond/branch_7_fun/ppermute | solution.py:88
  54.9 3.3 %collective-permute-done.74 = bf16[64,2048]{1,0:T(8,128)(2,1)S(1)} collective-permute-done((bf16[64,2048]{1,0:T(8,128)(2,1)S(1)}, bf16[64,2048]{1,0:T(8,128)(2,1)S(1)}, u32[]{:S(2)}, u32[]{:S(2)}) %collective-permute-start.74) | collective-permute-done | bytes 262176 | tf_op jit(solution)/shard_map/cond/branch_7_fun/ppermute | solution.py:79
  58.5 1.1 %multiply_convert_fusion.49 = (bf16[64,2048]{1,0:T(8,128)(2,1)S(1)}, bf16[64,2048]{1,0:T(8,128)(2,1)S(1)}) fusion(bf16[64,2048]{1,0:T(8,128)(2,1)S(1)} %get-tuple-element.1137, bf16[64,2048]{1,0:T(8,128)(2,1)S(1)} %copy-done.2, bf16[64,2048]{1,0:T(8,128)(2,1)S(1)} %get-tuple-element.1144, pred[2048]{0:T(1024)(128)(4,1)S(1)} %get-tuple-element.1160, ...), kind=kLoop, calls=%fused_computation.79 | loop fusion | flops 1572864 | bytes 1574912 | tf_op jit(solution)/shard_map/convert_element_type | solution.py:93
  60.3 0.9 %collective-permute-done.191.refs_6_ = bf16[64,2048]{1,0:T(8,128)(2,1)S(1)} collective-permute-done((bf16[64,2048]{1,0:T(8,128)(2,1)S(1)}, bf16[64,2048]{1,0:T(8,128)(2,1)S(1)}, u32[]{:S(2)}, u32[]{:S(2)}) %collective-permute-start.191) | collective-permute-done | bytes 262176 | tf_op jit(solution)/shard_map/ppermute | solution.py:88
  61.8 1.6 %collective-permute-start.194 = (bf16[128,384]{1,0:T(8,128)(2,1)S(1)}, bf16[128,384]{1,0:T(8,128)(2,1)S(1)}, u32[]{:S(2)}, u32[]{:S(2)}) collective-permute-start(bf16[128,384]{1,0:T(8,128)(2,1)S(1)} %get-tuple-element.1222), channel_id=1, source_target_pairs={{0,1},{1,0},{2,3},{3,2},{4,5},{5,4},{6,7},{7,6},{8,9},{9,8},{10,11... | collective-permute-start | bytes 294920 | tf_op jit(solution)/shard_map/ppermute | solution.py:88
  63.4 1.6 %fusion.60 = (bf16[128,384]{1,0:T(8,128)(2,1)S(1)}, f32[128,384]{1,0:T(8,128)S(1)}) fusion(bf16[384,2048]{1,0:T(8,128)(2,1)S(1)} %copy-done, bf16[64,2048]{1,0:T(8,128)(2,1)} %get-tuple-element.1151.refs_4_, bf16[64,2048]{1,0:T(8,128)(2,1)} %get-tuple-element.1149.refs_3_), kind=kOutput, calls=%fused_computation.139 | convolution fusion | flops 202424320 | bytes 2392064 | tf_op jit(solution)/shard_map/rv,wv->rw/dot_general | solution.py:221
  65.6 1.5 %fusion.61 = (bf16[128,384]{1,0:T(8,128)(2,1)S(1)}, f32[128,384]{1,0:T(8,128)S(1)}) fusion(bf16[384,2048]{1,0:T(8,128)(2,1)S(1)} %copy-done, bf16[64,2048]{1,0:T(8,128)(2,1)} %get-tuple-element.1147.refs_2_, bf16[64,2048]{1,0:T(8,128)(2,1)S(1)} %get-tuple-element.1145.refs_1_), kind=kOutput, calls=%fused_computation.140 | convolution fusion | flops 202424320 | bytes 2392064 | tf_op jit(solution)/shard_map/rv,wv->rw/dot_general | solution.py:221
  67.2 1.6 %collective-permute-start.192 = (bf16[128,384]{1,0:T(8,128)(2,1)S(1)}, bf16[128,384]{1,0:T(8,128)(2,1)S(1)}, u32[]{:S(2)}, u32[]{:S(2)}) collective-permute-start(bf16[128,384]{1,0:T(8,128)(2,1)S(1)} %get-tuple-element.1226), channel_id=1, source_target_pairs={{0,1},{1,0},{2,3},{3,2},{4,5},{5,4},{6,7},{7,6},{8,9},{9,8},{10,11... | collective-permute-start | bytes 294920 | tf_op jit(solution)/shard_map/ppermute | solution.py:88
  69.2 0.8 %collective-permute-done.193 = bf16[128,384]{1,0:T(8,128)(2,1)S(1)} collective-permute-done((bf16[128,384]{1,0:T(8,128)(2,1)S(1)}, bf16[128,384]{1,0:T(8,128)(2,1)S(1)}, u32[]{:S(2)}, u32[]{:S(2)}) %collective-permute-start.193) | collective-permute-done | bytes 98336 | tf_op jit(solution)/shard_map/ppermute | solution.py:88
  70.1 0.6 collective-permute-done.196.refs_8_
  71.3 0.8 %collective-permute-start.197 = (bf16[128,384]{1,0:T(8,128)(2,1)S(1)}, bf16[128,384]{1,0:T(8,128)(2,1)S(1)}, u32[]{:S(2)}, u32[]{:S(2)}) collective-permute-start(bf16[128,384]{1,0:T(8,128)(2,1)S(1)} %get-tuple-element.1220), channel_id=1, source_target_pairs={{0,1},{1,0},{2,3},{3,2},{4,5},{5,4},{6,7},{7,6},{8,9},{9,8},{10,11... | collective-permute-start | bytes 294920 | tf_op jit(solution)/shard_map/ppermute | solution.py:88
  72.2 4.2 %shard_map.60 = bf16[384,2048]{1,0:T(8,128)(2,1)} custom-call(bf16[512,384]{1,0:T(8,128)(2,1)S(1)} %bitcast.37, bf16[64,2048]{1,0:T(8,128)(2,1)S(1)} %get-tuple-element.1145.refs_1_, bf16[64,2048]{1,0:T(8,128)(2,1)} %get-tuple-element.1147.refs_2_, bf16[64,2048]{1,0:T(8,128)(2,1)} %get-tuple-element.1149.refs_3_, ...), custom_call_target="tpu_custom_call" | custom-call | flops 805306368 | bytes 4063232 | tf_op jit(solution)/shard_map/pallas_call | solution.py:120
  76.3 1.2 %convolution_convert_fusion.1 = bf16[2,256,384]{2,1,0:T(8,128)(2,1)} fusion(bf16[1,128,384]{2,1,0:T(8,128)(2,1)S(1)} %fusion.40, bf16[1,128,384]{2,1,0:T(8,128)(2,1)S(1)} %fusion.39, bf16[1,128,384]{2,1,0:T(8,128)(2,1)S(1)} %fusion.38, bf16[1,128,384]{2,1,0:T(8,128)(2,1)S(1)} %fusion.37, s32[2,256]{1,0:T(2,128)S(1)} %bitcast.40, s32[256]{0:T(256)S(1)} %add_add_fusion.1), kind=kOutput, calls=%fused_computation.49 | convolution fusion | flops 102563840 | bytes 789504 | tf_op jit(solution)/shard_map/mei,mew->miw/dot_general | solution.py:230
  (57 shorter events, 7.1 us)
Async XLA Ops:
  0.6 2.3 %copy-start = (bf16[384,2048]{1,0:T(8,128)(2,1)S(1)}, bf16[384,2048]{1,0:T(8,128)(2,1)}, u32[]{:S(2)}) copy-start(bf16[384,2048]{1,0:T(8,128)(2,1)} %param.101) | copy-start | bytes 4718596
  1.7 2.2 %copy-start.3 = (bf16[2,256,384]{2,1,0:T(8,128)(2,1)S(1)}, bf16[2,256,384]{2,1,0:T(8,128)(2,1)}, u32[]{:S(2)}) copy-start(bf16[2,256,384]{2,1,0:T(8,128)(2,1)} %param.100) | copy-start | bytes 1179652
  3.4 2.8 %collective-permute-start.189 = (f32[128,2048]{1,0:T(8,128)S(1)}, f32[128,2048]{1,0:T(8,128)S(1)}, u32[]{:S(2)}, u32[]{:S(2)}) collective-permute-start(f32[128,2048]{1,0:T(8,128)S(1)} %fusion.41), channel_id=1, source_target_pairs={{0,2},{2,0},{4,6},{6,4},{8,10},{10,8},{12,14},{14,12},{16,18},{18,... | collective-permute-start | bytes 3145736 | tf_op jit(solution)/shard_map/ppermute | solution.py:88
  4.6 4.6 %collective-permute-start.188 = (f32[128,2048]{1,0:T(8,128)S(1)}, f32[128,2048]{1,0:T(8,128)S(1)}, u32[]{:S(2)}, u32[]{:S(2)}) collective-permute-start(f32[128,2048]{1,0:T(8,128)S(1)} %fusion.45), channel_id=1, source_target_pairs={{0,2},{2,0},{4,6},{6,4},{8,10},{10,8},{12,14},{14,12},{16,18},{18,... | collective-permute-start | bytes 3145736 | tf_op jit(solution)/shard_map/ppermute | solution.py:88
  6.2 3.1 %copy-start.1 = (s32[2,8]{1,0:T(2,128)S(1)}, s32[2,8]{1,0:T(2,128)}, u32[]{:S(2)}) copy-start(s32[2,8]{1,0:T(2,128)} %order_ref) | copy-start | bytes 196
  6.2 9.6 %collective-permute-start.190 = (bf16[64,2048]{1,0:T(8,128)(2,1)S(1)}, bf16[64,2048]{1,0:T(8,128)(2,1)S(1)}, u32[]{:S(2)}, u32[]{:S(2)}) collective-permute-start(bf16[64,2048]{1,0:T(8,128)(2,1)S(1)} %fusion.2), channel_id=1, source_target_pairs={{0,4},{2,6},{4,0},{6,2},{8,12},{10,14},{12,8},{14,10},{16,20},{18,... | collective-permute-start | bytes 786440 | tf_op jit(solution)/shard_map/ppermute | solution.py:88
  16.0 9.7 %collective-permute-start.17 = (bf16[64,2048]{1,0:T(8,128)(2,1)S(1)}, bf16[64,2048]{1,0:T(8,128)(2,1)S(1)}, u32[]{:S(2)}, u32[]{:S(2)}) collective-permute-start(bf16[64,2048]{1,0:T(8,128)(2,1)S(1)} %get-tuple-element.757), channel_id=1, source_target_pairs={{0,8},{2,10},{4,12},{6,14},{8,16},{10,18},{12,20},{14,22},{16,24},... | collective-permute-start | bytes 786440 | tf_op jit(solution)/shard_map/cond/branch_9_fun/ppermute | solution.py:79
  17.8 7.9 %collective-permute-start.18 = (bf16[64,2048]{1,0:T(8,128)(2,1)S(1)}, bf16[64,2048]{1,0:T(8,128)(2,1)}, u32[]{:S(2)}, u32[]{:S(2)}) collective-permute-start(bf16[64,2048]{1,0:T(8,128)(2,1)S(1)} %get-tuple-element.758), channel_id=1, source_target_pairs={{0,4},{2,6},{4,0},{6,2},{8,12},{10,14},{12,8},{14,10},{16,20},{18,... | collective-permute-start | bytes 786440 | tf_op jit(solution)/shard_map/cond/branch_9_fun/ppermute | solution.py:88
  25.8 13.2 %collective-permute-start.157 = (bf16[64,2048]{1,0:T(8,128)(2,1)S(1)}, bf16[64,2048]{1,0:T(8,128)(2,1)S(1)}, u32[]{:S(2)}, u32[]{:S(2)}) collective-permute-start(bf16[64,2048]{1,0:T(8,128)(2,1)S(1)} %get-tuple-element.851), channel_id=1, source_target_pairs={{0,16},{2,18},{4,20},{6,22},{8,24},{10,26},{12,28},{14,30},{16,0},... | collective-permute-start | bytes 786440 | tf_op jit(solution)/shard_map/cond/branch_16_fun/ppermute | solution.py:79
  41.0 3.8 %collective-permute-start.168 = (bf16[64,2048]{1,0:T(8,128)(2,1)}, bf16[64,2048]{1,0:T(8,128)(2,1)}, u32[]{:S(2)}, u32[]{:S(2)}) collective-permute-start(bf16[64,2048]{1,0:T(8,128)(2,1)} %get-tuple-element.907), channel_id=1, source_target_pairs={{0,0},{2,2},{4,4},{6,6},{8,24},{10,26},{12,28},{14,30},{16,8},{18,... | collective-permute-start | bytes 786440 | tf_op jit(solution)/shard_map/cond/branch_4_fun/ppermute | solution.py:79
  46.5 11.9 %copy-start.2 = (bf16[64,2048]{1,0:T(8,128)(2,1)S(1)}, bf16[64,2048]{1,0:T(8,128)(2,1)}, u32[]{:S(2)}) copy-start(bf16[64,2048]{1,0:T(8,128)(2,1)} %get-tuple-element.1140) | copy-start | bytes 786436
  46.5 8.3 %collective-permute-start.76 = (bf16[64,2048]{1,0:T(8,128)(2,1)S(1)}, bf16[64,2048]{1,0:T(8,128)(2,1)}, u32[]{:S(2)}, u32[]{:S(2)}) collective-permute-start(bf16[64,2048]{1,0:T(8,128)(2,1)S(1)} %get-tuple-element.1050), channel_id=1, source_target_pairs={{0,4},{2,6},{4,0},{6,2},{8,12},{10,14},{12,8},{14,10},{16,20},{18,... | collective-permute-start | bytes 786440 | tf_op jit(solution)/shard_map/cond/branch_7_fun/ppermute | solution.py:88
  48.0 10.1 %collective-permute-start.74 = (bf16[64,2048]{1,0:T(8,128)(2,1)S(1)}, bf16[64,2048]{1,0:T(8,128)(2,1)S(1)}, u32[]{:S(2)}, u32[]{:S(2)}) collective-permute-start(bf16[64,2048]{1,0:T(8,128)(2,1)S(1)} %get-tuple-element.1048), channel_id=1, source_target_pairs={{0,8},{2,10},{4,12},{6,14},{8,0},{10,2},{12,4},{14,6},{16,24},{18,... | collective-permute-start | bytes 786440 | tf_op jit(solution)/shard_map/cond/branch_7_fun/ppermute | solution.py:79
  53.7 4.5 %collective-permute-start.75 = (bf16[64,2048]{1,0:T(8,128)(2,1)S(1)}, bf16[64,2048]{1,0:T(8,128)(2,1)}, u32[]{:S(2)}, u32[]{:S(2)}) collective-permute-start(bf16[64,2048]{1,0:T(8,128)(2,1)S(1)} %get-tuple-element.1049), channel_id=1, source_target_pairs={{0,2},{2,0},{4,6},{6,4},{8,10},{10,8},{12,14},{14,12},{16,18},{18,... | collective-permute-start | bytes 786440 | tf_op jit(solution)/shard_map/cond/branch_7_fun/ppermute | solution.py:88
  54.9 3.3 %collective-permute-start.77 = (bf16[64,2048]{1,0:T(8,128)(2,1)}, bf16[64,2048]{1,0:T(8,128)(2,1)}, u32[]{:S(2)}, u32[]{:S(2)}) collective-permute-start(bf16[64,2048]{1,0:T(8,128)(2,1)} %collective-permute-done.76), channel_id=1, source_target_pairs={{0,2},{2,0},{4,6},{6,4},{8,10},{10,8},{12,14},{14,12},{16,18},{18,... | collective-permute-start | bytes 786440 | tf_op jit(solution)/shard_map/cond/branch_7_fun/ppermute | solution.py:88
  59.6 1.6 %collective-permute-start.191 = (bf16[64,2048]{1,0:T(8,128)(2,1)S(1)}, bf16[64,2048]{1,0:T(8,128)(2,1)S(1)}, u32[]{:S(2)}, u32[]{:S(2)}) collective-permute-start(bf16[64,2048]{1,0:T(8,128)(2,1)S(1)} %get-tuple-element.1216.refs_5_), channel_id=1, source_target_pairs={{0,2},{2,0},{4,6},{6,4},{8,10},{10,8},{12,14},{14,12},{16,18},{18,... | collective-permute-start | bytes 786440 | tf_op jit(solution)/shard_map/ppermute | solution.py:88
  59.7 9.4 %collective-permute-start.195 = (bf16[64,2048]{1,0:T(8,128)(2,1)S(1)}, bf16[64,2048]{1,0:T(8,128)(2,1)S(1)}, u32[]{:S(2)}, u32[]{:S(2)}) collective-permute-start(bf16[64,2048]{1,0:T(8,128)(2,1)S(1)} %get-tuple-element.1217), channel_id=1, source_target_pairs={{0,4},{2,6},{4,0},{6,2},{8,12},{10,14},{12,8},{14,10},{16,20},{18,... | collective-permute-start | bytes 786440 | tf_op jit(solution)/shard_map/ppermute | solution.py:88
  61.8 7.4 %collective-permute-start.194 = (bf16[128,384]{1,0:T(8,128)(2,1)S(1)}, bf16[128,384]{1,0:T(8,128)(2,1)S(1)}, u32[]{:S(2)}, u32[]{:S(2)}) collective-permute-start(bf16[128,384]{1,0:T(8,128)(2,1)S(1)} %get-tuple-element.1222), channel_id=1, source_target_pairs={{0,1},{1,0},{2,3},{3,2},{4,5},{5,4},{6,7},{7,6},{8,9},{9,8},{10,11... | collective-permute-start | bytes 294920 | tf_op jit(solution)/shard_map/ppermute | solution.py:88
  65.0 3.7 %copy-start.4 = (bf16[2,256,384]{2,1,0:T(8,128)(2,1)S(1)}, bf16[2,256,384]{2,1,0:T(8,128)(2,1)}, u32[]{:S(2)}) copy-start(bf16[2,256,384]{2,1,0:T(8,128)(2,1)} %param.100) | copy-start | bytes 1179652
  65.0 5.0 %collective-permute-start.193 = (bf16[128,384]{1,0:T(8,128)(2,1)S(1)}, bf16[128,384]{1,0:T(8,128)(2,1)S(1)}, u32[]{:S(2)}, u32[]{:S(2)}) collective-permute-start(bf16[128,384]{1,0:T(8,128)(2,1)S(1)} %get-tuple-element.1224), channel_id=1, source_target_pairs={{0,1},{1,0},{2,3},{3,2},{4,5},{5,4},{6,7},{7,6},{8,9},{9,8},{10,11... | collective-permute-start | bytes 294920 | tf_op jit(solution)/shard_map/ppermute | solution.py:88
  67.2 5.0 %collective-permute-start.192 = (bf16[128,384]{1,0:T(8,128)(2,1)S(1)}, bf16[128,384]{1,0:T(8,128)(2,1)S(1)}, u32[]{:S(2)}, u32[]{:S(2)}) collective-permute-start(bf16[128,384]{1,0:T(8,128)(2,1)S(1)} %get-tuple-element.1226), channel_id=1, source_target_pairs={{0,1},{1,0},{2,3},{3,2},{4,5},{5,4},{6,7},{7,6},{8,9},{9,8},{10,11... | collective-permute-start | bytes 294920 | tf_op jit(solution)/shard_map/ppermute | solution.py:88
  69.1 1.6 %collective-permute-start.196 = (bf16[64,2048]{1,0:T(8,128)(2,1)S(1)}, bf16[64,2048]{1,0:T(8,128)(2,1)S(1)}, u32[]{:S(2)}, u32[]{:S(2)}) collective-permute-start(bf16[64,2048]{1,0:T(8,128)(2,1)S(1)} %collective-permute-done.195.refs_7_), channel_id=1, source_target_pairs={{0,2},{2,0},{4,6},{6,4},{8,10},{10,8},{12,14},{14,12},{16,18},{18,... | collective-permute-start | bytes 786440 | tf_op jit(solution)/shard_map/ppermute | solution.py:88
  71.3 5.0 %collective-permute-start.197 = (bf16[128,384]{1,0:T(8,128)(2,1)S(1)}, bf16[128,384]{1,0:T(8,128)(2,1)S(1)}, u32[]{:S(2)}, u32[]{:S(2)}) collective-permute-start(bf16[128,384]{1,0:T(8,128)(2,1)S(1)} %get-tuple-element.1220), channel_id=1, source_target_pairs={{0,1},{1,0},{2,3},{3,2},{4,5},{5,4},{6,7},{7,6},{8,9},{9,8},{10,11... | collective-permute-start | bytes 294920 | tf_op jit(solution)/shard_map/ppermute | solution.py:88

commit v6 on v5

--- a/solution.py
+++ b/solution.py
@@ -176,37 +176,34 @@
     def leaving(home, sib, home_first):
         return jnp.where(home_first, home, sib), jnp.where(home_first, sib, home)
 
-    def first_beside(far, waiting):
-        return [swap(block, "rep", 2) for block in far], [settle(*group) for group in waiting]
-
-    def second_beside(coming, settled):
-        sent = [leaving(*group) for group in coming]
-        returned = []
-        for grad_home, grad_sib in settled:
-            grad_far = swap(grad_sib, "rep", 2)
-            near = swap(grad_home, "rep", 1)
-            returned.append([grad_home, near, grad_far, swap(grad_far, "rep", 1)])
-        return sent, returned
-
-    grads, waiting = [], []
-    (branches, (home_first, to_home_first)) = codes[0]
-    home = logits[0][0]
-    sent = leaving(home, sib, home_first)
-    for m in range(micro_count):
-        last = m + 1 == micro_count
-        first, (arrived, settled) = move_pairs(
-            sent[0], branches[0], pairs, first_beside, [] if last else [logits[m + 1][1]], waiting
-        )
-        coming = [] if last else [(logits[m + 1][0], arrived[0], codes[m + 1][1][0])]
-        second, (sents, returned) = move_pairs(
-            after(sent[1], first), branches[1], pairs, second_beside, coming, settled
-        )
-        grads += returned
-        waiting = [(home, sib, first, second, to_home_first)]
-        if not last:
-            (branches, (home_first, to_home_first)) = codes[m + 1]
-            home, sib, sent = logits[m + 1][0], arrived[0], sents[0]
-    [(grad_home, grad_sib)] = [settle(*group) for group in waiting]
+    def beside(nexts, settled):
+        arriving = [swap(far, "rep", 2) for far in nexts]
+        return arriving, [swap(grad_sib, "rep", 2) for _, grad_sib in settled]
+
+    def second_beside(returned):
+        return [(swap(home, "rep", 1), swap(far, "rep", 1)) for home, far in returned]
+
+    early, settled = [], []
+    for m in range(micro_count):
+        home = logits[m][0]
+        branches, (home_first, to_home_first) = codes[m]
+        sent = leaving(home, sib, home_first)
+        nexts = [] if m + 1 == micro_count else [logits[m + 1][1]]
+        if m > 0:
+            sent = [after(block, *settled[0]) for block in sent]
+        first, (arriving, returned) = move_pairs(
+            sent[0], branches[0], pairs, beside, nexts, settled
+        )
+        returned = [(group[0], far) for group, far in zip(settled, returned)]
+        second, swapped = move_pairs(
+            after(sent[1], first), branches[1], pairs, second_beside, returned
+        )
+        for (grad_home, far), (near, farther) in zip(returned, swapped):
+            early.append((grad_home, near, far, farther))
+        settled = [settle(home, sib, first, second, to_home_first)]
+        sib = arriving[0] if arriving else None
+    [(grad_home, grad_sib)] = settled
+    grads = [list(group) for group in early]
     grad_far = swap(grad_sib, "rep", 2)
     near = swap(grad_home, "rep", 1)
     grads = [[after(block, near) for block in group] for group in grads]

time: 79 us -> 77.4 us (0.980)
  the two profiles are of different devices: /device:TPU:0 before, /device:TPU:9 now
where the time goes in v6:
time: 77.4 us; the launch traced here: 76.8 us
  waiting for transfers between devices  32.3 us (42%)
  starting transfers between devices  20.9 us (27%)
  matrix products  9.09 us (12%)
  Pallas kernels  5.6 us (7%)
  between operations  3.48 us (4%)
  other arithmetic  3.06 us (4%)
  local copies, waits for them, and re-layouts  1.64 us (2%)
    ppermute x4, waiting for transfers between devices, one(): moved = lax.ppermute(moved, 'rep', route)  28.6 us
    ppermute x14, starting transfers between devices, swap(): return lax.ppermute(block, axis, [(i, i ^ bit) for i in range(count)])  16.6 us
    dot_general x4, matrix products, back(): jnp.einsum('rv,wv->rw', gradient, head_weight, preferred_element_type=jnp...  4.36 us
    ppermute x4, starting transfers between devices, one(): moved = lax.ppermute(moved, 'rep', route)  4.31 us
    pallas_call x1, Pallas kernels, head_gradient(): pl.pallas_call(head_kernel, grid=(vocab // step,), out_shape=jax.ShapeDty...  4.16 us
    ppermute x14, waiting for transfers between devices, swap(): return lax.ppermute(block, axis, [(i, i ^ bit) for i in range(count)])  3.79 us
  transfers between devices with their start and end apart: 18, of which 7 were waited for; matrix products, arithmetic and copies ran while one was open for 9% of the time, Pallas kernels for 7%

profile of v6, /device:TPU:9, one launch (start us, length us, event | category | flops | bytes accessed | tf_op | source)
XLA Modules:
  0.0 76.8 jit_solution(1404440877955927558)
XLA Ops:
  0.7 0.8 %constant_dynamic-slice_fusion = s32[2,1,256]{2,1,0:T(1,128)S(1)} fusion(s32[2,8,256]{2,1,0:T(8,128)} %param.103, s32[]{:T(128)S(6)} %select_n.80), kind=kLoop, calls=%fused_computation.86 | loop fusion | bytes 4100 | tf_op jit(solution)/shard_map/jit(dynamic_index_in_dim)/dynamic_slice | solution.py:148
  1.7 1.2 %convolution_convert_fusion.3 = bf16[256,384]{1,0:T(8,128)(2,1)S(1)} fusion(pred[2,256,256]{2,1,0:T(32,128)(4,1)S(1)} %broadcast_compare_fusion, bf16[2,256,384]{2,1,0:T(8,128)(2,1)} %param.100), kind=kOutput, calls=%fused_computation.3 | convolution fusion | flops 50429952 | bytes 458752 | tf_op jit(solution)/shard_map/dot_general | solution.py:161
  3.4 0.7 collective-permute-start.188
  6.5 1.3 %collective-permute-start.190 = (bf16[64,2048]{1,0:T(8,128)(2,1)S(1)}, bf16[64,2048]{1,0:T(8,128)(2,1)S(1)}, u32[]{:S(2)}, u32[]{:S(2)}) collective-permute-start(bf16[64,2048]{1,0:T(8,128)(2,1)S(1)} %fusion.2), channel_id=1, source_target_pairs={{0,4},{2,6},{4,0},{6,2},{8,12},{10,14},{12,8},{14,10},{16,20},{18,... | collective-permute-start | bytes 786440 | tf_op jit(solution)/shard_map/ppermute | solution.py:88
  8.0 1.4 %shard_map.59 = (s32[1]{0:T(128)}, s32[1]{0:T(128)}, s32[1]{0:T(128)}, s32[1]{0:T(128)}, s32[4,2048]{1,0:T(4,128)S(1)}) custom-call(s32[2,8]{1,0:T(2,128)S(1)} %copy-done.1), custom_call_target="tpu_custom_call" | custom-call | tf_op jit(solution)/shard_map/pallas_call | solution.py:61
  12.1 1.9 %collective-permute-done.190 = bf16[64,2048]{1,0:T(8,128)(2,1)S(1)} collective-permute-done((bf16[64,2048]{1,0:T(8,128)(2,1)S(1)}, bf16[64,2048]{1,0:T(8,128)(2,1)S(1)}, u32[]{:S(2)}, u32[]{:S(2)}) %collective-permute-start.190) | collective-permute-done | bytes 262176 | tf_op jit(solution)/shard_map/ppermute | solution.py:88
  14.2 11.5 %conditional.4 = (bf16[64,2048]{1,0:T(8,128)(2,1)S(1)}, bf16[64,2048]{1,0:T(8,128)(2,1)}) conditional(s32[]{:T(128)} %bitcast.4, (bf16[64,2048]{1,0:T(8,128)(2,1)S(1)}, bf16[64,2048]{1,0:T(8,128)(2,1)S(1)}) %tuple.379, (bf16[64,2048]{1,0:T(8,128)(2,1)S(1)}, bf16[64,2048]{1,0:T(8,128)(2,1)S(1)}) %tuple.380, ...), branch_computations={%region_0.1_spmd, %region_1.2_spmd, %region_2.3_spmd, %region_3.4_... | conditional | bytes 2621536 | solution.py:83
  14.3 1.3 %collective-permute-start.43 = (bf16[64,2048]{1,0:T(8,128)(2,1)S(1)}, bf16[64,2048]{1,0:T(8,128)(2,1)S(1)}, u32[]{:S(2)}, u32[]{:S(2)}) collective-permute-start(bf16[64,2048]{1,0:T(8,128)(2,1)S(1)} %get-tuple-element.429), channel_id=1, source_target_pairs={{0,24},{2,26},{4,28},{6,30},{8,16},{10,18},{12,20},{14,22},{16,0},... | collective-permute-start | bytes 786440 | tf_op jit(solution)/shard_map/cond/branch_22_fun/ppermute | solution.py:79
  15.6 1.2 %collective-permute-start.44 = (bf16[64,2048]{1,0:T(8,128)(2,1)S(1)}, bf16[64,2048]{1,0:T(8,128)(2,1)}, u32[]{:S(2)}, u32[]{:S(2)}) collective-permute-start(bf16[64,2048]{1,0:T(8,128)(2,1)S(1)} %get-tuple-element.430), channel_id=1, source_target_pairs={{0,4},{2,6},{4,0},{6,2},{8,12},{10,14},{12,8},{14,10},{16,20},{18,... | collective-permute-start | bytes 786440 | tf_op jit(solution)/shard_map/cond/branch_22_fun/ppermute | solution.py:88
  16.9 8.8 %collective-permute-done.43 = bf16[64,2048]{1,0:T(8,128)(2,1)S(1)} collective-permute-done((bf16[64,2048]{1,0:T(8,128)(2,1)S(1)}, bf16[64,2048]{1,0:T(8,128)(2,1)S(1)}, u32[]{:S(2)}, u32[]{:S(2)}) %collective-permute-start.43) | collective-permute-done | bytes 262176 | tf_op jit(solution)/shard_map/cond/branch_22_fun/ppermute | solution.py:79
  25.7 0.8 %conditional.5 = (bf16[64,2048]{1,0:T(8,128)(2,1)S(1)}) conditional(s32[]{:T(128)} %bitcast.5, bf16[64,2048]{1,0:T(8,128)(2,1)S(1)} %get-tuple-element.582, bf16[64,2048]{1,0:T(8,128)(2,1)S(1)} %get-tuple-element.582, bf16[64,2048]{1,0:T(8,128)(2,1)S(1)} %get-tuple-element.582, ...), branch_computations={%region_24.25_spmd, %region_25.26_spmd, %region_26.27_spmd, %regio... | conditional | bytes 1572912 | solution.py:83
  25.7 0.7 collective-permute-start.60
  26.5 1.0 %broadcast_select_fusion = (bf16[64,2048]{1,0:T(8,128)(2,1)S(1)}, bf16[64,2048]{1,0:T(8,128)(2,1)S(1)}) fusion(bf16[64,2048]{1,0:T(8,128)(2,1)} %get-tuple-element.584, bf16[64,2048]{1,0:T(8,128)(2,1)S(1)} %get-tuple-element.606, pred[2048]{0:T(1024)(128)(4,1)S(1)} %get-tuple-element.600), kind=kLoop, calls=%fused_computation.48 | loop fusion | flops 262144 | bytes 1050624 | tf_op jit(solution)/shard_map/jit(_where)/select_n | solution.py:177
  27.7 15.7 %conditional.6 = (bf16[64,2048]{1,0:T(8,128)(2,1)S(1)}, bf16[64,2048]{1,0:T(8,128)(2,1)}) conditional(s32[]{:T(128)} %bitcast.6, (bf16[64,2048]{1,0:T(8,128)(2,1)S(1)}, bf16[64,2048]{1,0:T(8,128)(2,1)S(1)}) %tuple.383, (bf16[64,2048]{1,0:T(8,128)(2,1)S(1)}, bf16[64,2048]{1,0:T(8,128)(2,1)S(1)}) %tuple.384, ...), branch_computations={%region_48.49_spmd, %region_49.50_spmd, %region_50.51_spmd, %regio... | conditional | bytes 2621536 | solution.py:83
  27.8 1.3 %collective-permute-start.90 = (bf16[64,2048]{1,0:T(8,128)(2,1)S(1)}, bf16[64,2048]{1,0:T(8,128)(2,1)}, u32[]{:S(2)}, u32[]{:S(2)}) collective-permute-start(bf16[64,2048]{1,0:T(8,128)(2,1)S(1)} %get-tuple-element.454), channel_id=1, source_target_pairs={{0,4},{2,6},{4,0},{6,2},{8,12},{10,14},{12,8},{14,10},{16,20},{18,... | collective-permute-start | bytes 786440 | tf_op jit(solution)/shard_map/cond/branch_10_fun/ppermute | solution.py:88
  29.1 14.1 %collective-permute-done.89 = bf16[64,2048]{1,0:T(8,128)(2,1)S(1)} collective-permute-done((bf16[64,2048]{1,0:T(8,128)(2,1)S(1)}, bf16[64,2048]{1,0:T(8,128)(2,1)S(1)}, u32[]{:S(2)}, u32[]{:S(2)}) %collective-permute-start.89) | collective-permute-done | bytes 262176 | tf_op jit(solution)/shard_map/cond/branch_10_fun/ppermute | solution.py:79
  43.4 0.7 copy-done.2
  44.1 12.1 %conditional.7 = (bf16[64,2048]{1,0:T(8,128)(2,1)S(1)}, bf16[64,2048]{1,0:T(8,128)(2,1)}, bf16[64,2048]{1,0:T(8,128)(2,1)}) conditional(s32[]{:T(128)} %bitcast.7, (bf16[64,2048]{1,0:T(8,128)(2,1)S(1)}, bf16[64,2048]{1,0:T(8,128)(2,1)}, bf16[64,2048]{1,0:T(8,128)(2,1)S(1)}) %tuple.387, ...), branch_computations={%region_72.73_spmd, %region_73.74_spmd, %region_74.75_spmd, %regio... | conditional | bytes 3670160 | solution.py:83
  44.1 2.2 %collective-permute-start.182 = (bf16[64,2048]{1,0:T(8,128)(2,1)S(1)}, bf16[64,2048]{1,0:T(8,128)(2,1)S(1)}, u32[]{:S(2)}, u32[]{:S(2)}) collective-permute-start(bf16[64,2048]{1,0:T(8,128)(2,1)S(1)} %get-tuple-element.547), channel_id=1, source_target_pairs={{0,24},{2,26},{4,28},{6,30},{8,16},{10,18},{12,20},{14,22},{16,0},... | collective-permute-start | bytes 786440 | tf_op jit(solution)/shard_map/cond/branch_22_fun/ppermute | solution.py:79
  46.4 3.9 %collective-permute-start.183 = (bf16[64,2048]{1,0:T(8,128)(2,1)S(1)}, bf16[64,2048]{1,0:T(8,128)(2,1)}, u32[]{:S(2)}, u32[]{:S(2)}) collective-permute-start(bf16[64,2048]{1,0:T(8,128)(2,1)S(1)} %get-tuple-element.548), channel_id=1, source_target_pairs={{0,2},{2,0},{4,6},{6,4},{8,10},{10,8},{12,14},{14,12},{16,18},{18,... | collective-permute-start | bytes 786440 | tf_op jit(solution)/shard_map/cond/branch_22_fun/ppermute | solution.py:88
  50.3 5.7 %collective-permute-done.182 = bf16[64,2048]{1,0:T(8,128)(2,1)S(1)} collective-permute-done((bf16[64,2048]{1,0:T(8,128)(2,1)S(1)}, bf16[64,2048]{1,0:T(8,128)(2,1)S(1)}, u32[]{:S(2)}, u32[]{:S(2)}) %collective-permute-start.182) | collective-permute-done | bytes 262176 | tf_op jit(solution)/shard_map/cond/branch_22_fun/ppermute | solution.py:79
  56.2 1.2 %multiply_convert_fusion.1 = (bf16[64,2048]{1,0:T(8,128)(2,1)S(1)}, bf16[64,2048]{1,0:T(8,128)(2,1)S(1)}) fusion(bf16[64,2048]{1,0:T(8,128)(2,1)S(1)} %get-tuple-element.606, bf16[64,2048]{1,0:T(8,128)(2,1)} %copy-done.2, bf16[64,2048]{1,0:T(8,128)(2,1)S(1)} %get-tuple-element.591, pred[2048]{0:T(1024)(128)(4,1)S(1)} %get-tuple-element.599, ...), kind=kLoop, calls=%fused_computation.31 | loop fusion | flops 1572864 | bytes 1574912 | tf_op jit(solution)/shard_map/convert_element_type | solution.py:93
  57.5 2.2 %collective-permute-start.191 = (bf16[64,2048]{1,0:T(8,128)(2,1)S(1)}, bf16[64,2048]{1,0:T(8,128)(2,1)S(1)}, u32[]{:S(2)}, u32[]{:S(2)}) collective-permute-start(bf16[64,2048]{1,0:T(8,128)(2,1)S(1)} %get-tuple-element.607.refs_5_), channel_id=1, source_target_pairs={{0,2},{2,0},{4,6},{6,4},{8,10},{10,8},{12,14},{14,12},{16,18},{18,... | collective-permute-start | bytes 786440 | tf_op jit(solution)/shard_map/ppermute | solution.py:88
  59.7 1.3 %collective-permute-start.195 = (bf16[64,2048]{1,0:T(8,128)(2,1)S(1)}, bf16[64,2048]{1,0:T(8,128)(2,1)S(1)}, u32[]{:S(2)}, u32[]{:S(2)}) collective-permute-start(bf16[64,2048]{1,0:T(8,128)(2,1)S(1)} %get-tuple-element.608), channel_id=1, source_target_pairs={{0,4},{2,6},{4,0},{6,2},{8,12},{10,14},{12,8},{14,10},{16,20},{18,... | collective-permute-start | bytes 786440 | tf_op jit(solution)/shard_map/ppermute | solution.py:88
  61.5 1.3 %collective-permute-start.194 = (bf16[128,384]{1,0:T(8,128)(2,1)S(1)}, bf16[128,384]{1,0:T(8,128)(2,1)S(1)}, u32[]{:S(2)}, u32[]{:S(2)}) collective-permute-start(bf16[128,384]{1,0:T(8,128)(2,1)S(1)} %get-tuple-element.615), channel_id=1, source_target_pairs={{0,1},{1,0},{2,3},{3,2},{4,5},{5,4},{6,7},{7,6},{8,9},{9,8},{10,11... | collective-permute-start | bytes 294920 | tf_op jit(solution)/shard_map/ppermute | solution.py:88
  62.8 1.6 %fusion.59 = (bf16[128,384]{1,0:T(8,128)(2,1)S(1)}, f32[128,384]{1,0:T(8,128)S(1)}) fusion(bf16[384,2048]{1,0:T(8,128)(2,1)S(1)} %copy-done, bf16[64,2048]{1,0:T(8,128)(2,1)} %get-tuple-element.597.refs_4_, bf16[64,2048]{1,0:T(8,128)(2,1)} %get-tuple-element.595.refs_3_), kind=kOutput, calls=%fused_computation.94 | convolution fusion | flops 202424320 | bytes 2392064 | tf_op jit(solution)/shard_map/rv,wv->rw/dot_general | solution.py:218
  64.8 1.5 %fusion.60 = (bf16[128,384]{1,0:T(8,128)(2,1)S(1)}, f32[128,384]{1,0:T(8,128)S(1)}) fusion(bf16[384,2048]{1,0:T(8,128)(2,1)S(1)} %copy-done, bf16[64,2048]{1,0:T(8,128)(2,1)} %get-tuple-element.594.refs_2_, bf16[64,2048]{1,0:T(8,128)(2,1)S(1)} %get-tuple-element.592.refs_1_), kind=kOutput, calls=%fused_computation.95 | convolution fusion | flops 202424320 | bytes 2392064 | tf_op jit(solution)/shard_map/rv,wv->rw/dot_general | solution.py:218
  66.3 1.3 %collective-permute-start.192 = (bf16[128,384]{1,0:T(8,128)(2,1)S(1)}, bf16[128,384]{1,0:T(8,128)(2,1)S(1)}, u32[]{:S(2)}, u32[]{:S(2)}) collective-permute-start(bf16[128,384]{1,0:T(8,128)(2,1)S(1)} %get-tuple-element.619), channel_id=1, source_target_pairs={{0,1},{1,0},{2,3},{3,2},{4,5},{5,4},{6,7},{7,6},{8,9},{9,8},{10,11... | collective-permute-start | bytes 294920 | tf_op jit(solution)/shard_map/ppermute | solution.py:88
  68.0 1.3 %collective-permute-start.196 = (bf16[64,2048]{1,0:T(8,128)(2,1)S(1)}, bf16[64,2048]{1,0:T(8,128)(2,1)S(1)}, u32[]{:S(2)}, u32[]{:S(2)}) collective-permute-start(bf16[64,2048]{1,0:T(8,128)(2,1)S(1)} %collective-permute-done.195.refs_7_), channel_id=1, source_target_pairs={{0,2},{2,0},{4,6},{6,4},{8,10},{10,8},{12,14},{14,12},{16,18},{18,... | collective-permute-start | bytes 786440 | tf_op jit(solution)/shard_map/ppermute | solution.py:88
  69.3 1.1 %collective-permute-done.196.refs_8_ = bf16[64,2048]{1,0:T(8,128)(2,1)S(1)} collective-permute-done((bf16[64,2048]{1,0:T(8,128)(2,1)S(1)}, bf16[64,2048]{1,0:T(8,128)(2,1)S(1)}, u32[]{:S(2)}, u32[]{:S(2)}) %collective-permute-start.196) | collective-permute-done | bytes 262176 | tf_op jit(solution)/shard_map/ppermute | solution.py:88
  71.5 4.2 %shard_map.60 = bf16[384,2048]{1,0:T(8,128)(2,1)} custom-call(bf16[512,384]{1,0:T(8,128)(2,1)S(1)} %bitcast.37, bf16[64,2048]{1,0:T(8,128)(2,1)S(1)} %get-tuple-element.592.refs_1_, bf16[64,2048]{1,0:T(8,128)(2,1)} %get-tuple-element.594.refs_2_, bf16[64,2048]{1,0:T(8,128)(2,1)} %get-tuple-element.595.refs_3_, bf16[64,2048]{1,0:T(8,128)(2,1)} %get-tuple-element.597.refs_4_, ...), custom_call_target="tpu_custom_call" | custom-call | flops 805306368 | bytes 4063232 | tf_op jit(solution)/shard_map/pallas_call | solution.py:120
  75.7 1.2 %convolution_convert_fusion.1 = bf16[2,256,384]{2,1,0:T(8,128)(2,1)} fusion(bf16[1,128,384]{2,1,0:T(8,128)(2,1)S(1)} %fusion.40, bf16[1,128,384]{2,1,0:T(8,128)(2,1)S(1)} %fusion.39, bf16[1,128,384]{2,1,0:T(8,128)(2,1)S(1)} %fusion.38, bf16[1,128,384]{2,1,0:T(8,128)(2,1)S(1)} %fusion.37, s32[2,256]{1,0:T(2,128)S(1)} %bitcast.40, s32[256]{0:T(256)S(1)} %add_add_fusion.1), kind=kOutput, calls=%fused_computation.1 | convolution fusion | flops 102563840 | bytes 789504 | tf_op jit(solution)/shard_map/mei,mew->miw/dot_general | solution.py:227
  (53 shorter events, 6.2 us)
Async XLA Ops:
  0.6 2.3 %copy-start = (bf16[384,2048]{1,0:T(8,128)(2,1)S(1)}, bf16[384,2048]{1,0:T(8,128)(2,1)}, u32[]{:S(2)}) copy-start(bf16[384,2048]{1,0:T(8,128)(2,1)} %param.101) | copy-start | bytes 4718596
  1.7 2.4 %copy-start.3 = (bf16[2,256,384]{2,1,0:T(8,128)(2,1)S(1)}, bf16[2,256,384]{2,1,0:T(8,128)(2,1)}, u32[]{:S(2)}) copy-start(bf16[2,256,384]{2,1,0:T(8,128)(2,1)} %param.100) | copy-start | bytes 1179652
  3.4 3.0 %collective-permute-start.188 = (f32[128,2048]{1,0:T(8,128)S(1)}, f32[128,2048]{1,0:T(8,128)S(1)}, u32[]{:S(2)}, u32[]{:S(2)}) collective-permute-start(f32[128,2048]{1,0:T(8,128)S(1)} %fusion.45), channel_id=1, source_target_pairs={{0,2},{2,0},{4,6},{6,4},{8,10},{10,8},{12,14},{14,12},{16,18},{18,... | collective-permute-start | bytes 3145736 | tf_op jit(solution)/shard_map/ppermute | solution.py:88
  4.8 3.1 %collective-permute-start.189 = (f32[128,2048]{1,0:T(8,128)S(1)}, f32[128,2048]{1,0:T(8,128)S(1)}, u32[]{:S(2)}, u32[]{:S(2)}) collective-permute-start(f32[128,2048]{1,0:T(8,128)S(1)} %fusion.41), channel_id=1, source_target_pairs={{0,2},{2,0},{4,6},{6,4},{8,10},{10,8},{12,14},{14,12},{16,18},{18,... | collective-permute-start | bytes 3145736 | tf_op jit(solution)/shard_map/ppermute | solution.py:88
  6.5 1.6 %copy-start.1 = (s32[2,8]{1,0:T(2,128)S(1)}, s32[2,8]{1,0:T(2,128)}, u32[]{:S(2)}) copy-start(s32[2,8]{1,0:T(2,128)} %order_ref) | copy-start | bytes 196
  6.5 7.6 %collective-permute-start.190 = (bf16[64,2048]{1,0:T(8,128)(2,1)S(1)}, bf16[64,2048]{1,0:T(8,128)(2,1)S(1)}, u32[]{:S(2)}, u32[]{:S(2)}) collective-permute-start(bf16[64,2048]{1,0:T(8,128)(2,1)S(1)} %fusion.2), channel_id=1, source_target_pairs={{0,4},{2,6},{4,0},{6,2},{8,12},{10,14},{12,8},{14,10},{16,20},{18,... | collective-permute-start | bytes 786440 | tf_op jit(solution)/shard_map/ppermute | solution.py:88
  14.3 11.4 %collective-permute-start.43 = (bf16[64,2048]{1,0:T(8,128)(2,1)S(1)}, bf16[64,2048]{1,0:T(8,128)(2,1)S(1)}, u32[]{:S(2)}, u32[]{:S(2)}) collective-permute-start(bf16[64,2048]{1,0:T(8,128)(2,1)S(1)} %get-tuple-element.429), channel_id=1, source_target_pairs={{0,24},{2,26},{4,28},{6,30},{8,16},{10,18},{12,20},{14,22},{16,0},... | collective-permute-start | bytes 786440 | tf_op jit(solution)/shard_map/cond/branch_22_fun/ppermute | solution.py:79
  15.6 10.0 %collective-permute-start.44 = (bf16[64,2048]{1,0:T(8,128)(2,1)S(1)}, bf16[64,2048]{1,0:T(8,128)(2,1)}, u32[]{:S(2)}, u32[]{:S(2)}) collective-permute-start(bf16[64,2048]{1,0:T(8,128)(2,1)S(1)} %get-tuple-element.430), channel_id=1, source_target_pairs={{0,4},{2,6},{4,0},{6,2},{8,12},{10,14},{12,8},{14,10},{16,20},{18,... | collective-permute-start | bytes 786440 | tf_op jit(solution)/shard_map/cond/branch_22_fun/ppermute | solution.py:88
  25.7 0.7 collective-permute-start.60
  27.7 15.5 %collective-permute-start.89 = (bf16[64,2048]{1,0:T(8,128)(2,1)S(1)}, bf16[64,2048]{1,0:T(8,128)(2,1)S(1)}, u32[]{:S(2)}, u32[]{:S(2)}) collective-permute-start(bf16[64,2048]{1,0:T(8,128)(2,1)S(1)} %get-tuple-element.453), channel_id=1, source_target_pairs={{0,8},{2,10},{4,12},{6,14},{8,24},{10,26},{12,28},{14,30},{16,0},{... | collective-permute-start | bytes 786440 | tf_op jit(solution)/shard_map/cond/branch_10_fun/ppermute | solution.py:79
  27.8 15.4 %collective-permute-start.90 = (bf16[64,2048]{1,0:T(8,128)(2,1)S(1)}, bf16[64,2048]{1,0:T(8,128)(2,1)}, u32[]{:S(2)}, u32[]{:S(2)}) collective-permute-start(bf16[64,2048]{1,0:T(8,128)(2,1)S(1)} %get-tuple-element.454), channel_id=1, source_target_pairs={{0,4},{2,6},{4,0},{6,2},{8,12},{10,14},{12,8},{14,10},{16,20},{18,... | collective-permute-start | bytes 786440 | tf_op jit(solution)/shard_map/cond/branch_10_fun/ppermute | solution.py:88
  43.4 0.7 copy-start.2
  44.1 11.8 %collective-permute-start.182 = (bf16[64,2048]{1,0:T(8,128)(2,1)S(1)}, bf16[64,2048]{1,0:T(8,128)(2,1)S(1)}, u32[]{:S(2)}, u32[]{:S(2)}) collective-permute-start(bf16[64,2048]{1,0:T(8,128)(2,1)S(1)} %get-tuple-element.547), channel_id=1, source_target_pairs={{0,24},{2,26},{4,28},{6,30},{8,16},{10,18},{12,20},{14,22},{16,0},... | collective-permute-start | bytes 786440 | tf_op jit(solution)/shard_map/cond/branch_22_fun/ppermute | solution.py:79
  46.4 9.6 %collective-permute-start.183 = (bf16[64,2048]{1,0:T(8,128)(2,1)S(1)}, bf16[64,2048]{1,0:T(8,128)(2,1)}, u32[]{:S(2)}, u32[]{:S(2)}) collective-permute-start(bf16[64,2048]{1,0:T(8,128)(2,1)S(1)} %get-tuple-element.548), channel_id=1, source_target_pairs={{0,2},{2,0},{4,6},{6,4},{8,10},{10,8},{12,14},{14,12},{16,18},{18,... | collective-permute-start | bytes 786440 | tf_op jit(solution)/shard_map/cond/branch_22_fun/ppermute | solution.py:88
  50.3 5.7 %collective-permute-start.184 = (bf16[64,2048]{1,0:T(8,128)(2,1)}, bf16[64,2048]{1,0:T(8,128)(2,1)}, u32[]{:S(2)}, u32[]{:S(2)}) collective-permute-start(bf16[64,2048]{1,0:T(8,128)(2,1)} %get-tuple-element.549), channel_id=1, source_target_pairs={{0,2},{2,0},{4,6},{6,4},{8,10},{10,8},{12,14},{14,12},{16,18},{18,... | collective-permute-start | bytes 786440 | tf_op jit(solution)/shard_map/cond/branch_22_fun/ppermute | solution.py:88
  57.5 3.5 %collective-permute-start.191 = (bf16[64,2048]{1,0:T(8,128)(2,1)S(1)}, bf16[64,2048]{1,0:T(8,128)(2,1)S(1)}, u32[]{:S(2)}, u32[]{:S(2)}) collective-permute-start(bf16[64,2048]{1,0:T(8,128)(2,1)S(1)} %get-tuple-element.607.refs_5_), channel_id=1, source_target_pairs={{0,2},{2,0},{4,6},{6,4},{8,10},{10,8},{12,14},{14,12},{16,18},{18,... | collective-permute-start | bytes 786440 | tf_op jit(solution)/shard_map/ppermute | solution.py:88
  59.7 8.3 %collective-permute-start.195 = (bf16[64,2048]{1,0:T(8,128)(2,1)S(1)}, bf16[64,2048]{1,0:T(8,128)(2,1)S(1)}, u32[]{:S(2)}, u32[]{:S(2)}) collective-permute-start(bf16[64,2048]{1,0:T(8,128)(2,1)S(1)} %get-tuple-element.608), channel_id=1, source_target_pairs={{0,4},{2,6},{4,0},{6,2},{8,12},{10,14},{12,8},{14,10},{16,20},{18,... | collective-permute-start | bytes 786440 | tf_op jit(solution)/shard_map/ppermute | solution.py:88
  61.5 7.7 %collective-permute-start.194 = (bf16[128,384]{1,0:T(8,128)(2,1)S(1)}, bf16[128,384]{1,0:T(8,128)(2,1)S(1)}, u32[]{:S(2)}, u32[]{:S(2)}) collective-permute-start(bf16[128,384]{1,0:T(8,128)(2,1)S(1)} %get-tuple-element.615), channel_id=1, source_target_pairs={{0,1},{1,0},{2,3},{3,2},{4,5},{5,4},{6,7},{7,6},{8,9},{9,8},{10,11... | collective-permute-start | bytes 294920 | tf_op jit(solution)/shard_map/ppermute | solution.py:88
  64.4 3.2 %copy-start.4 = (bf16[2,256,384]{2,1,0:T(8,128)(2,1)S(1)}, bf16[2,256,384]{2,1,0:T(8,128)(2,1)}, u32[]{:S(2)}) copy-start(bf16[2,256,384]{2,1,0:T(8,128)(2,1)} %param.100) | copy-start | bytes 1179652
  64.5 4.8 %collective-permute-start.193 = (bf16[128,384]{1,0:T(8,128)(2,1)S(1)}, bf16[128,384]{1,0:T(8,128)(2,1)S(1)}, u32[]{:S(2)}, u32[]{:S(2)}) collective-permute-start(bf16[128,384]{1,0:T(8,128)(2,1)S(1)} %get-tuple-element.617), channel_id=1, source_target_pairs={{0,1},{1,0},{2,3},{3,2},{4,5},{5,4},{6,7},{7,6},{8,9},{9,8},{10,11... | collective-permute-start | bytes 294920 | tf_op jit(solution)/shard_map/ppermute | solution.py:88
  66.3 5.1 %collective-permute-start.192 = (bf16[128,384]{1,0:T(8,128)(2,1)S(1)}, bf16[128,384]{1,0:T(8,128)(2,1)S(1)}, u32[]{:S(2)}, u32[]{:S(2)}) collective-permute-start(bf16[128,384]{1,0:T(8,128)(2,1)S(1)} %get-tuple-element.619), channel_id=1, source_target_pairs={{0,1},{1,0},{2,3},{3,2},{4,5},{5,4},{6,7},{7,6},{8,9},{9,8},{10,11... | collective-permute-start | bytes 294920 | tf_op jit(solution)/shard_map/ppermute | solution.py:88
  68.0 2.4 %collective-permute-start.196 = (bf16[64,2048]{1,0:T(8,128)(2,1)S(1)}, bf16[64,2048]{1,0:T(8,128)(2,1)S(1)}, u32[]{:S(2)}, u32[]{:S(2)}) collective-permute-start(bf16[64,2048]{1,0:T(8,128)(2,1)S(1)} %collective-permute-done.195.refs_7_), channel_id=1, source_target_pairs={{0,2},{2,0},{4,6},{6,4},{8,10},{10,8},{12,14},{14,12},{16,18},{18,... | collective-permute-start | bytes 786440 | tf_op jit(solution)/shard_map/ppermute | solution.py:88
  71.0 4.6 %collective-permute-start.197 = (bf16[128,384]{1,0:T(8,128)(2,1)S(1)}, bf16[128,384]{1,0:T(8,128)(2,1)S(1)}, u32[]{:S(2)}, u32[]{:S(2)}) collective-permute-start(bf16[128,384]{1,0:T(8,128)(2,1)S(1)} %get-tuple-element.613), channel_id=1, source_target_pairs={{0,1},{1,0},{2,3},{3,2},{4,5},{5,4},{6,7},{7,6},{8,9},{9,8},{10,11... | collective-permute-start | bytes 294920 | tf_op jit(solution)/shard_map/ppermute | solution.py:88

commit v7 on v6

--- a/solution.py
+++ b/solution.py
@@ -38,6 +38,7 @@
                 color[at] = 0
                 color[at ^ 1] = 1
                 at = src[dest[at ^ 1] ^ 1]
+        places, loads = [], []
         for c in range(2):
             sigma = []
             place = jnp.int32(0)
@@ -49,10 +50,22 @@
                     smaller = smaller - jnp.where(earlier < to, 1, 0)
                 place = place * (pairs - z) + smaller
                 sigma.append(to)
-            branch_refs[2 * m + c][0] = place
+            load = jnp.int32(0)
+            for cut in range(1, pairs):
+                over = jnp.int32(0)
+                for to in sigma[:cut]:
+                    over = over + jnp.where(to >= cut, 1, 0)
+                load = jnp.maximum(load, over)
+            places.append(place)
+            loads.append(load)
+        turned = loads[1] > loads[0] if m + 1 < micro_count else loads[1] < loads[0]
+        first = jnp.where(turned, 1, 0)
+        branch_refs[2 * m][0] = jnp.where(first == 0, places[0], places[1])
+        branch_refs[2 * m + 1][0] = jnp.where(first == 0, places[1], places[0])
         for row, moved in enumerate((replica, src[replica])):
             at = 2 * m + row
-            flags_ref[at : at + 1, :] = jnp.full((1, flags_ref.shape[1]), color[moved], jnp.int32)
+            flag = jnp.where(color[moved] == first, 0, 1)
+            flags_ref[at : at + 1, :] = jnp.full((1, flags_ref.shape[1]), flag, jnp.int32)
 
 
 def routes(pair_order, width):

time: 77.4 us -> 75.1 us (0.970)
  the two profiles are of different devices: /device:TPU:9 before, /device:TPU:0 now
where the time goes in v7:
time: 75.1 us; the launch traced here: 76.4 us
  waiting for transfers between devices  29.3 us (39%)
  starting transfers between devices  23.5 us (31%)
  matrix products  9.08 us (12%)
  Pallas kernels  5.66 us (8%)
  between operations  3.49 us (5%)
  other arithmetic  3.06 us (4%)
  local copies, waits for them, and re-layouts  1.64 us (2%)
    ppermute x4, waiting for transfers between devices, one(): moved = lax.ppermute(moved, 'rep', route)  23.4 us
    ppermute x14, starting transfers between devices, swap(): return lax.ppermute(block, axis, [(i, i ^ bit) for i in range(count)])  13.5 us
    ppermute x4, starting transfers between devices, one(): moved = lax.ppermute(moved, 'rep', route)  10 us
    ppermute x14, waiting for transfers between devices, swap(): return lax.ppermute(block, axis, [(i, i ^ bit) for i in range(count)])  5.96 us
    dot_general x4, matrix products, back(): jnp.einsum('rv,wv->rw', gradient, head_weight, preferred_element_type=jnp...  4.36 us
    pallas_call x1, Pallas kernels, head_gradient(): pl.pallas_call(head_kernel, grid=(vocab // step,), out_shape=jax.ShapeDty...  4.16 us
    pallas_call x1, Pallas kernels, routes(): pl.pallas_call(route_kernel, out_shape=[jax.ShapeDtypeStruct((1,), jnp.in...  1.51 us
  transfers between devices with their start and end apart: 18, of which 9 were waited for; matrix products, arithmetic and copies ran while one was open for 9% of the time, Pallas kernels for 7%

profile of v7, /device:TPU:0, one launch (start us, length us, event | category | flops | bytes accessed | tf_op | source)
XLA Modules:
  0.0 76.4 jit_solution(7804856302702204728)
XLA Ops:
  0.7 0.8 %constant_dynamic-slice_fusion = s32[2,1,256]{2,1,0:T(1,128)S(1)} fusion(s32[2,8,256]{2,1,0:T(8,128)} %param.103, s32[]{:T(128)S(6)} %select_n.80), kind=kLoop, calls=%fused_computation.86 | loop fusion | bytes 4100 | tf_op jit(solution)/shard_map/jit(dynamic_index_in_dim)/dynamic_slice | solution.py:161
  1.7 1.2 %convolution_convert_fusion.3 = bf16[256,384]{1,0:T(8,128)(2,1)S(1)} fusion(pred[2,256,256]{2,1,0:T(32,128)(4,1)S(1)} %broadcast_compare_fusion, bf16[2,256,384]{2,1,0:T(8,128)(2,1)} %param.100), kind=kOutput, calls=%fused_computation.3 | convolution fusion | flops 50429952 | bytes 458752 | tf_op jit(solution)/shard_map/dot_general | solution.py:174
  6.2 3.0 %collective-permute-start.190 = (bf16[64,2048]{1,0:T(8,128)(2,1)S(1)}, bf16[64,2048]{1,0:T(8,128)(2,1)S(1)}, u32[]{:S(2)}, u32[]{:S(2)}) collective-permute-start(bf16[64,2048]{1,0:T(8,128)(2,1)S(1)} %fusion.2), channel_id=1, source_target_pairs={{0,4},{2,6},{4,0},{6,2},{8,12},{10,14},{12,8},{14,10},{16,20},{18,... | collective-permute-start | bytes 786440 | tf_op jit(solution)/shard_map/ppermute | solution.py:101
  9.3 1.5 %shard_map.59 = (s32[1]{0:T(128)}, s32[1]{0:T(128)}, s32[1]{0:T(128)}, s32[1]{0:T(128)}, s32[4,2048]{1,0:T(4,128)S(1)}) custom-call(s32[2,8]{1,0:T(2,128)S(1)} %copy-done.1), custom_call_target="tpu_custom_call" | custom-call | tf_op jit(solution)/shard_map/pallas_call | solution.py:74
  13.5 2.3 %collective-permute-done.190 = bf16[64,2048]{1,0:T(8,128)(2,1)S(1)} collective-permute-done((bf16[64,2048]{1,0:T(8,128)(2,1)S(1)}, bf16[64,2048]{1,0:T(8,128)(2,1)S(1)}, u32[]{:S(2)}, u32[]{:S(2)}) %collective-permute-start.190) | collective-permute-done | bytes 262176 | tf_op jit(solution)/shard_map/ppermute | solution.py:101
  16.0 13.2 %conditional.4 = (bf16[64,2048]{1,0:T(8,128)(2,1)S(1)}, bf16[64,2048]{1,0:T(8,128)(2,1)}) conditional(s32[]{:T(128)} %bitcast.4, (bf16[64,2048]{1,0:T(8,128)(2,1)S(1)}, bf16[64,2048]{1,0:T(8,128)(2,1)S(1)}) %tuple.379, (bf16[64,2048]{1,0:T(8,128)(2,1)S(1)}, bf16[64,2048]{1,0:T(8,128)(2,1)S(1)}) %tuple.380, ...), branch_computations={%region_0.1_spmd, %region_1.2_spmd, %region_2.3_spmd, %region_3.4_... | conditional | bytes 2621536 | solution.py:96
  16.0 5.7 %collective-permute-start.41 = (bf16[64,2048]{1,0:T(8,128)(2,1)S(1)}, bf16[64,2048]{1,0:T(8,128)(2,1)S(1)}, u32[]{:S(2)}, u32[]{:S(2)}) collective-permute-start(bf16[64,2048]{1,0:T(8,128)(2,1)S(1)} %get-tuple-element.427), channel_id=1, source_target_pairs={{0,24},{2,26},{4,28},{6,30},{8,8},{10,10},{12,12},{14,14},{16,16},... | collective-permute-start | bytes 786440 | tf_op jit(solution)/shard_map/cond/branch_21_fun/ppermute | solution.py:92
  21.7 1.6 %collective-permute-start.42 = (bf16[64,2048]{1,0:T(8,128)(2,1)S(1)}, bf16[64,2048]{1,0:T(8,128)(2,1)}, u32[]{:S(2)}, u32[]{:S(2)}) collective-permute-start(bf16[64,2048]{1,0:T(8,128)(2,1)S(1)} %get-tuple-element.428), channel_id=1, source_target_pairs={{0,4},{2,6},{4,0},{6,2},{8,12},{10,14},{12,8},{14,10},{16,20},{18,... | collective-permute-start | bytes 786440 | tf_op jit(solution)/shard_map/cond/branch_21_fun/ppermute | solution.py:101
  23.3 4.2 %collective-permute-done.41 = bf16[64,2048]{1,0:T(8,128)(2,1)S(1)} collective-permute-done((bf16[64,2048]{1,0:T(8,128)(2,1)S(1)}, bf16[64,2048]{1,0:T(8,128)(2,1)S(1)}, u32[]{:S(2)}, u32[]{:S(2)}) %collective-permute-start.41) | collective-permute-done | bytes 262176 | tf_op jit(solution)/shard_map/cond/branch_21_fun/ppermute | solution.py:92
  27.6 1.6 %collective-permute-done.42 = bf16[64,2048]{1,0:T(8,128)(2,1)} collective-permute-done((bf16[64,2048]{1,0:T(8,128)(2,1)S(1)}, bf16[64,2048]{1,0:T(8,128)(2,1)}, u32[]{:S(2)}, u32[]{:S(2)}) %collective-permute-start.42) | collective-permute-done | bytes 262176 | tf_op jit(solution)/shard_map/cond/branch_21_fun/ppermute | solution.py:101
  29.2 8.2 %conditional.5 = (bf16[64,2048]{1,0:T(8,128)(2,1)S(1)}) conditional(s32[]{:T(128)} %bitcast.5, bf16[64,2048]{1,0:T(8,128)(2,1)S(1)} %get-tuple-element.582, bf16[64,2048]{1,0:T(8,128)(2,1)S(1)} %get-tuple-element.582, bf16[64,2048]{1,0:T(8,128)(2,1)S(1)} %get-tuple-element.582, ...), branch_computations={%region_24.25_spmd, %region_25.26_spmd, %region_26.27_spmd, %regio... | conditional | bytes 1572912 | solution.py:96
  29.2 8.2 %collective-permute-done.55 = bf16[64,2048]{1,0:T(8,128)(2,1)S(1)} collective-permute-done((bf16[64,2048]{1,0:T(8,128)(2,1)S(1)}, bf16[64,2048]{1,0:T(8,128)(2,1)S(1)}, u32[]{:S(2)}, u32[]{:S(2)}) %collective-permute-start.55) | collective-permute-done | bytes 262176 | tf_op jit(solution)/shard_map/cond/branch_9_fun/ppermute | solution.py:92
  37.4 1.0 %broadcast_select_fusion = (bf16[64,2048]{1,0:T(8,128)(2,1)S(1)}, bf16[64,2048]{1,0:T(8,128)(2,1)S(1)}) fusion(bf16[64,2048]{1,0:T(8,128)(2,1)} %get-tuple-element.584, bf16[64,2048]{1,0:T(8,128)(2,1)S(1)} %get-tuple-element.606, pred[2048]{0:T(1024)(128)(4,1)S(1)} %get-tuple-element.600), kind=kLoop, calls=%fused_computation.48 | loop fusion | flops 262144 | bytes 1050624 | tf_op jit(solution)/shard_map/jit(_where)/select_n | solution.py:190
  38.6 9.4 %conditional.6 = (bf16[64,2048]{1,0:T(8,128)(2,1)S(1)}, bf16[64,2048]{1,0:T(8,128)(2,1)}) conditional(s32[]{:T(128)} %bitcast.6, (bf16[64,2048]{1,0:T(8,128)(2,1)S(1)}, bf16[64,2048]{1,0:T(8,128)(2,1)S(1)}) %tuple.383, (bf16[64,2048]{1,0:T(8,128)(2,1)S(1)}, bf16[64,2048]{1,0:T(8,128)(2,1)S(1)}) %tuple.384, ...), branch_computations={%region_48.49_spmd, %region_49.50_spmd, %region_50.51_spmd, %regio... | conditional | bytes 2621536 | solution.py:96
  38.8 2.4 %collective-permute-start.109 = (bf16[64,2048]{1,0:T(8,128)(2,1)S(1)}, bf16[64,2048]{1,0:T(8,128)(2,1)S(1)}, u32[]{:S(2)}, u32[]{:S(2)}) collective-permute-start(bf16[64,2048]{1,0:T(8,128)(2,1)S(1)} %get-tuple-element.473), channel_id=1, source_target_pairs={{0,24},{2,26},{4,28},{6,30},{8,8},{10,10},{12,12},{14,14},{16,0},{... | collective-permute-start | bytes 786440 | tf_op jit(solution)/shard_map/cond/branch_20_fun/ppermute | solution.py:92
  41.2 1.6 %collective-permute-start.110 = (bf16[64,2048]{1,0:T(8,128)(2,1)S(1)}, bf16[64,2048]{1,0:T(8,128)(2,1)}, u32[]{:S(2)}, u32[]{:S(2)}) collective-permute-start(bf16[64,2048]{1,0:T(8,128)(2,1)S(1)} %get-tuple-element.474), channel_id=1, source_target_pairs={{0,4},{2,6},{4,0},{6,2},{8,12},{10,14},{12,8},{14,10},{16,20},{18,... | collective-permute-start | bytes 786440 | tf_op jit(solution)/shard_map/cond/branch_20_fun/ppermute | solution.py:101
  42.8 5.2 %collective-permute-done.109 = bf16[64,2048]{1,0:T(8,128)(2,1)S(1)} collective-permute-done((bf16[64,2048]{1,0:T(8,128)(2,1)S(1)}, bf16[64,2048]{1,0:T(8,128)(2,1)S(1)}, u32[]{:S(2)}, u32[]{:S(2)}) %collective-permute-start.109) | collective-permute-done | bytes 262176 | tf_op jit(solution)/shard_map/cond/branch_20_fun/ppermute | solution.py:92
  48.0 0.7 copy-done.2
  48.7 8.5 %conditional.7 = (bf16[64,2048]{1,0:T(8,128)(2,1)S(1)}, bf16[64,2048]{1,0:T(8,128)(2,1)}, bf16[64,2048]{1,0:T(8,128)(2,1)}) conditional(s32[]{:T(128)} %bitcast.7, (bf16[64,2048]{1,0:T(8,128)(2,1)S(1)}, bf16[64,2048]{1,0:T(8,128)(2,1)}, bf16[64,2048]{1,0:T(8,128)(2,1)S(1)}) %tuple.387, ...), branch_computations={%region_72.73_spmd, %region_73.74_spmd, %region_74.75_spmd, %regio... | conditional | bytes 3670160 | solution.py:96
  48.7 1.9 %collective-permute-start.134 = (bf16[64,2048]{1,0:T(8,128)(2,1)S(1)}, bf16[64,2048]{1,0:T(8,128)(2,1)S(1)}, u32[]{:S(2)}, u32[]{:S(2)}) collective-permute-start(bf16[64,2048]{1,0:T(8,128)(2,1)S(1)} %get-tuple-element.499), channel_id=1, source_target_pairs={{0,8},{2,10},{4,12},{6,14},{8,0},{10,2},{12,4},{14,6},{16,16},{18,... | collective-permute-start | bytes 786440 | tf_op jit(solution)/shard_map/cond/branch_6_fun/ppermute | solution.py:92
  51.2 5.8 %collective-permute-done.134 = bf16[64,2048]{1,0:T(8,128)(2,1)S(1)} collective-permute-done((bf16[64,2048]{1,0:T(8,128)(2,1)S(1)}, bf16[64,2048]{1,0:T(8,128)(2,1)S(1)}, u32[]{:S(2)}, u32[]{:S(2)}) %collective-permute-start.134) | collective-permute-done | bytes 262176 | tf_op jit(solution)/shard_map/cond/branch_6_fun/ppermute | solution.py:92
  57.3 1.2 %multiply_convert_fusion.1 = (bf16[64,2048]{1,0:T(8,128)(2,1)S(1)}, bf16[64,2048]{1,0:T(8,128)(2,1)S(1)}) fusion(bf16[64,2048]{1,0:T(8,128)(2,1)S(1)} %get-tuple-element.606, bf16[64,2048]{1,0:T(8,128)(2,1)} %copy-done.2, bf16[64,2048]{1,0:T(8,128)(2,1)S(1)} %get-tuple-element.591, pred[2048]{0:T(1024)(128)(4,1)S(1)} %get-tuple-element.599, ...), kind=kLoop, calls=%fused_computation.31 | loop fusion | flops 1572864 | bytes 1574912 | tf_op jit(solution)/shard_map/convert_element_type | solution.py:106
  58.6 1.6 %collective-permute-start.195 = (bf16[64,2048]{1,0:T(8,128)(2,1)S(1)}, bf16[64,2048]{1,0:T(8,128)(2,1)S(1)}, u32[]{:S(2)}, u32[]{:S(2)}) collective-permute-start(bf16[64,2048]{1,0:T(8,128)(2,1)S(1)} %get-tuple-element.608), channel_id=1, source_target_pairs={{0,4},{2,6},{4,0},{6,2},{8,12},{10,14},{12,8},{14,10},{16,20},{18,... | collective-permute-start | bytes 786440 | tf_op jit(solution)/shard_map/ppermute | solution.py:101
  60.8 1.6 %collective-permute-start.194 = (bf16[128,384]{1,0:T(8,128)(2,1)S(1)}, bf16[128,384]{1,0:T(8,128)(2,1)S(1)}, u32[]{:S(2)}, u32[]{:S(2)}) collective-permute-start(bf16[128,384]{1,0:T(8,128)(2,1)S(1)} %get-tuple-element.615), channel_id=1, source_target_pairs={{0,1},{1,0},{2,3},{3,2},{4,5},{5,4},{6,7},{7,6},{8,9},{9,8},{10,11... | collective-permute-start | bytes 294920 | tf_op jit(solution)/shard_map/ppermute | solution.py:101
  62.3 1.6 %fusion.59 = (bf16[128,384]{1,0:T(8,128)(2,1)S(1)}, f32[128,384]{1,0:T(8,128)S(1)}) fusion(bf16[384,2048]{1,0:T(8,128)(2,1)S(1)} %copy-done, bf16[64,2048]{1,0:T(8,128)(2,1)} %get-tuple-element.597.refs_4_, bf16[64,2048]{1,0:T(8,128)(2,1)} %get-tuple-element.595.refs_3_), kind=kOutput, calls=%fused_computation.94 | convolution fusion | flops 202424320 | bytes 2392064 | tf_op jit(solution)/shard_map/rv,wv->rw/dot_general | solution.py:231
  64.6 1.5 %fusion.60 = (bf16[128,384]{1,0:T(8,128)(2,1)S(1)}, f32[128,384]{1,0:T(8,128)S(1)}) fusion(bf16[384,2048]{1,0:T(8,128)(2,1)S(1)} %copy-done, bf16[64,2048]{1,0:T(8,128)(2,1)} %get-tuple-element.594.refs_2_, bf16[64,2048]{1,0:T(8,128)(2,1)S(1)} %get-tuple-element.592.refs_1_), kind=kOutput, calls=%fused_computation.95 | convolution fusion | flops 202424320 | bytes 2392064 | tf_op jit(solution)/shard_map/rv,wv->rw/dot_general | solution.py:231
  66.1 1.6 %collective-permute-start.192 = (bf16[128,384]{1,0:T(8,128)(2,1)S(1)}, bf16[128,384]{1,0:T(8,128)(2,1)S(1)}, u32[]{:S(2)}, u32[]{:S(2)}) collective-permute-start(bf16[128,384]{1,0:T(8,128)(2,1)S(1)} %get-tuple-element.619), channel_id=1, source_target_pairs={{0,1},{1,0},{2,3},{3,2},{4,5},{5,4},{6,7},{7,6},{8,9},{9,8},{10,11... | collective-permute-start | bytes 294920 | tf_op jit(solution)/shard_map/ppermute | solution.py:101
  68.2 0.8 %collective-permute-done.193 = bf16[128,384]{1,0:T(8,128)(2,1)S(1)} collective-permute-done((bf16[128,384]{1,0:T(8,128)(2,1)S(1)}, bf16[128,384]{1,0:T(8,128)(2,1)S(1)}, u32[]{:S(2)}, u32[]{:S(2)}) %collective-permute-start.193) | collective-permute-done | bytes 98336 | tf_op jit(solution)/shard_map/ppermute | solution.py:101
  69.0 0.7 collective-permute-done.196.refs_8_
  70.3 0.7 collective-permute-start.197
  71.0 4.2 %shard_map.60 = bf16[384,2048]{1,0:T(8,128)(2,1)} custom-call(bf16[512,384]{1,0:T(8,128)(2,1)S(1)} %bitcast.37, bf16[64,2048]{1,0:T(8,128)(2,1)S(1)} %get-tuple-element.592.refs_1_, bf16[64,2048]{1,0:T(8,128)(2,1)} %get-tuple-element.594.refs_2_, bf16[64,2048]{1,0:T(8,128)(2,1)} %get-tuple-element.595.refs_3_, bf16[64,2048]{1,0:T(8,128)(2,1)} %get-tuple-element.597.refs_4_, ...), custom_call_target="tpu_custom_call" | custom-call | flops 805306368 | bytes 4063232 | tf_op jit(solution)/shard_map/pallas_call | solution.py:133
  75.2 1.2 %convolution_convert_fusion.1 = bf16[2,256,384]{2,1,0:T(8,128)(2,1)} fusion(bf16[1,128,384]{2,1,0:T(8,128)(2,1)S(1)} %fusion.40, bf16[1,128,384]{2,1,0:T(8,128)(2,1)S(1)} %fusion.39, bf16[1,128,384]{2,1,0:T(8,128)(2,1)S(1)} %fusion.38, bf16[1,128,384]{2,1,0:T(8,128)(2,1)S(1)} %fusion.37, s32[2,256]{1,0:T(2,128)S(1)} %bitcast.40, s32[256]{0:T(256)S(1)} %add_add_fusion.1), kind=kOutput, calls=%fused_computation.1 | convolution fusion | flops 102563840 | bytes 789504 | tf_op jit(solution)/shard_map/mei,mew->miw/dot_general | solution.py:240
  (53 shorter events, 7.0 us)
Async XLA Ops:
  0.6 2.3 %copy-start = (bf16[384,2048]{1,0:T(8,128)(2,1)S(1)}, bf16[384,2048]{1,0:T(8,128)(2,1)}, u32[]{:S(2)}) copy-start(bf16[384,2048]{1,0:T(8,128)(2,1)} %param.101) | copy-start | bytes 4718596
  1.7 2.2 %copy-start.3 = (bf16[2,256,384]{2,1,0:T(8,128)(2,1)S(1)}, bf16[2,256,384]{2,1,0:T(8,128)(2,1)}, u32[]{:S(2)}) copy-start(bf16[2,256,384]{2,1,0:T(8,128)(2,1)} %param.100) | copy-start | bytes 1179652
  3.4 2.8 %collective-permute-start.188 = (f32[128,2048]{1,0:T(8,128)S(1)}, f32[128,2048]{1,0:T(8,128)S(1)}, u32[]{:S(2)}, u32[]{:S(2)}) collective-permute-start(f32[128,2048]{1,0:T(8,128)S(1)} %fusion.45), channel_id=1, source_target_pairs={{0,2},{2,0},{4,6},{6,4},{8,10},{10,8},{12,14},{14,12},{16,18},{18,... | collective-permute-start | bytes 3145736 | tf_op jit(solution)/shard_map/ppermute | solution.py:101
  4.6 4.6 %collective-permute-start.189 = (f32[128,2048]{1,0:T(8,128)S(1)}, f32[128,2048]{1,0:T(8,128)S(1)}, u32[]{:S(2)}, u32[]{:S(2)}) collective-permute-start(f32[128,2048]{1,0:T(8,128)S(1)} %fusion.41), channel_id=1, source_target_pairs={{0,2},{2,0},{4,6},{6,4},{8,10},{10,8},{12,14},{14,12},{16,18},{18,... | collective-permute-start | bytes 3145736 | tf_op jit(solution)/shard_map/ppermute | solution.py:101
  6.2 3.1 %copy-start.1 = (s32[2,8]{1,0:T(2,128)S(1)}, s32[2,8]{1,0:T(2,128)}, u32[]{:S(2)}) copy-start(s32[2,8]{1,0:T(2,128)} %order_ref) | copy-start | bytes 196
  6.2 9.6 %collective-permute-start.190 = (bf16[64,2048]{1,0:T(8,128)(2,1)S(1)}, bf16[64,2048]{1,0:T(8,128)(2,1)S(1)}, u32[]{:S(2)}, u32[]{:S(2)}) collective-permute-start(bf16[64,2048]{1,0:T(8,128)(2,1)S(1)} %fusion.2), channel_id=1, source_target_pairs={{0,4},{2,6},{4,0},{6,2},{8,12},{10,14},{12,8},{14,10},{16,20},{18,... | collective-permute-start | bytes 786440 | tf_op jit(solution)/shard_map/ppermute | solution.py:101
  16.0 11.5 %collective-permute-start.41 = (bf16[64,2048]{1,0:T(8,128)(2,1)S(1)}, bf16[64,2048]{1,0:T(8,128)(2,1)S(1)}, u32[]{:S(2)}, u32[]{:S(2)}) collective-permute-start(bf16[64,2048]{1,0:T(8,128)(2,1)S(1)} %get-tuple-element.427), channel_id=1, source_target_pairs={{0,24},{2,26},{4,28},{6,30},{8,8},{10,10},{12,12},{14,14},{16,16},... | collective-permute-start | bytes 786440 | tf_op jit(solution)/shard_map/cond/branch_21_fun/ppermute | solution.py:92
  21.7 7.4 %collective-permute-start.42 = (bf16[64,2048]{1,0:T(8,128)(2,1)S(1)}, bf16[64,2048]{1,0:T(8,128)(2,1)}, u32[]{:S(2)}, u32[]{:S(2)}) collective-permute-start(bf16[64,2048]{1,0:T(8,128)(2,1)S(1)} %get-tuple-element.428), channel_id=1, source_target_pairs={{0,4},{2,6},{4,0},{6,2},{8,12},{10,14},{12,8},{14,10},{16,20},{18,... | collective-permute-start | bytes 786440 | tf_op jit(solution)/shard_map/cond/branch_21_fun/ppermute | solution.py:101
  29.2 8.2 %collective-permute-start.55 = (bf16[64,2048]{1,0:T(8,128)(2,1)S(1)}, bf16[64,2048]{1,0:T(8,128)(2,1)S(1)}, u32[]{:S(2)}, u32[]{:S(2)}) collective-permute-start(bf16[64,2048]{1,0:T(8,128)(2,1)S(1)} %param.33), channel_id=1, source_target_pairs={{0,8},{2,10},{4,12},{6,14},{8,16},{10,18},{12,20},{14,22},{16,24},... | collective-permute-start | bytes 786440 | tf_op jit(solution)/shard_map/cond/branch_9_fun/ppermute | solution.py:92
  38.8 9.2 %collective-permute-start.109 = (bf16[64,2048]{1,0:T(8,128)(2,1)S(1)}, bf16[64,2048]{1,0:T(8,128)(2,1)S(1)}, u32[]{:S(2)}, u32[]{:S(2)}) collective-permute-start(bf16[64,2048]{1,0:T(8,128)(2,1)S(1)} %get-tuple-element.473), channel_id=1, source_target_pairs={{0,24},{2,26},{4,28},{6,30},{8,8},{10,10},{12,12},{14,14},{16,0},{... | collective-permute-start | bytes 786440 | tf_op jit(solution)/shard_map/cond/branch_20_fun/ppermute | solution.py:92
  41.2 6.8 %collective-permute-start.110 = (bf16[64,2048]{1,0:T(8,128)(2,1)S(1)}, bf16[64,2048]{1,0:T(8,128)(2,1)}, u32[]{:S(2)}, u32[]{:S(2)}) collective-permute-start(bf16[64,2048]{1,0:T(8,128)(2,1)S(1)} %get-tuple-element.474), channel_id=1, source_target_pairs={{0,4},{2,6},{4,0},{6,2},{8,12},{10,14},{12,8},{14,10},{16,20},{18,... | collective-permute-start | bytes 786440 | tf_op jit(solution)/shard_map/cond/branch_20_fun/ppermute | solution.py:101
  48.0 0.7 copy-start.2
  48.7 8.3 %collective-permute-start.134 = (bf16[64,2048]{1,0:T(8,128)(2,1)S(1)}, bf16[64,2048]{1,0:T(8,128)(2,1)S(1)}, u32[]{:S(2)}, u32[]{:S(2)}) collective-permute-start(bf16[64,2048]{1,0:T(8,128)(2,1)S(1)} %get-tuple-element.499), channel_id=1, source_target_pairs={{0,8},{2,10},{4,12},{6,14},{8,0},{10,2},{12,4},{14,6},{16,16},{18,... | collective-permute-start | bytes 786440 | tf_op jit(solution)/shard_map/cond/branch_6_fun/ppermute | solution.py:92
  50.6 6.4 %collective-permute-start.135 = (bf16[64,2048]{1,0:T(8,128)(2,1)S(1)}, bf16[64,2048]{1,0:T(8,128)(2,1)}, u32[]{:S(2)}, u32[]{:S(2)}) collective-permute-start(bf16[64,2048]{1,0:T(8,128)(2,1)S(1)} %get-tuple-element.500), channel_id=1, source_target_pairs={{0,2},{2,0},{4,6},{6,4},{8,10},{10,8},{12,14},{14,12},{16,18},{18,... | collective-permute-start | bytes 786440 | tf_op jit(solution)/shard_map/cond/branch_6_fun/ppermute | solution.py:101
  50.7 6.3 %collective-permute-start.136 = (bf16[64,2048]{1,0:T(8,128)(2,1)}, bf16[64,2048]{1,0:T(8,128)(2,1)}, u32[]{:S(2)}, u32[]{:S(2)}) collective-permute-start(bf16[64,2048]{1,0:T(8,128)(2,1)} %get-tuple-element.501), channel_id=1, source_target_pairs={{0,2},{2,0},{4,6},{6,4},{8,10},{10,8},{12,14},{14,12},{16,18},{18,... | collective-permute-start | bytes 786440 | tf_op jit(solution)/shard_map/cond/branch_6_fun/ppermute | solution.py:101
  58.5 1.7 %collective-permute-start.191 = (bf16[64,2048]{1,0:T(8,128)(2,1)S(1)}, bf16[64,2048]{1,0:T(8,128)(2,1)S(1)}, u32[]{:S(2)}, u32[]{:S(2)}) collective-permute-start(bf16[64,2048]{1,0:T(8,128)(2,1)S(1)} %get-tuple-element.607.refs_5_), channel_id=1, source_target_pairs={{0,2},{2,0},{4,6},{6,4},{8,10},{10,8},{12,14},{14,12},{16,18},{18,... | collective-permute-start | bytes 786440 | tf_op jit(solution)/shard_map/ppermute | solution.py:101
  58.6 9.5 %collective-permute-start.195 = (bf16[64,2048]{1,0:T(8,128)(2,1)S(1)}, bf16[64,2048]{1,0:T(8,128)(2,1)S(1)}, u32[]{:S(2)}, u32[]{:S(2)}) collective-permute-start(bf16[64,2048]{1,0:T(8,128)(2,1)S(1)} %get-tuple-element.608), channel_id=1, source_target_pairs={{0,4},{2,6},{4,0},{6,2},{8,12},{10,14},{12,8},{14,10},{16,20},{18,... | collective-permute-start | bytes 786440 | tf_op jit(solution)/shard_map/ppermute | solution.py:101
  60.8 7.4 %collective-permute-start.194 = (bf16[128,384]{1,0:T(8,128)(2,1)S(1)}, bf16[128,384]{1,0:T(8,128)(2,1)S(1)}, u32[]{:S(2)}, u32[]{:S(2)}) collective-permute-start(bf16[128,384]{1,0:T(8,128)(2,1)S(1)} %get-tuple-element.615), channel_id=1, source_target_pairs={{0,1},{1,0},{2,3},{3,2},{4,5},{5,4},{6,7},{7,6},{8,9},{9,8},{10,11... | collective-permute-start | bytes 294920 | tf_op jit(solution)/shard_map/ppermute | solution.py:101
  64.0 3.7 %copy-start.4 = (bf16[2,256,384]{2,1,0:T(8,128)(2,1)S(1)}, bf16[2,256,384]{2,1,0:T(8,128)(2,1)}, u32[]{:S(2)}) copy-start(bf16[2,256,384]{2,1,0:T(8,128)(2,1)} %param.100) | copy-start | bytes 1179652
  64.0 5.0 %collective-permute-start.193 = (bf16[128,384]{1,0:T(8,128)(2,1)S(1)}, bf16[128,384]{1,0:T(8,128)(2,1)S(1)}, u32[]{:S(2)}, u32[]{:S(2)}) collective-permute-start(bf16[128,384]{1,0:T(8,128)(2,1)S(1)} %get-tuple-element.617), channel_id=1, source_target_pairs={{0,1},{1,0},{2,3},{3,2},{4,5},{5,4},{6,7},{7,6},{8,9},{9,8},{10,11... | collective-permute-start | bytes 294920 | tf_op jit(solution)/shard_map/ppermute | solution.py:101
  66.1 4.9 %collective-permute-start.192 = (bf16[128,384]{1,0:T(8,128)(2,1)S(1)}, bf16[128,384]{1,0:T(8,128)(2,1)S(1)}, u32[]{:S(2)}, u32[]{:S(2)}) collective-permute-start(bf16[128,384]{1,0:T(8,128)(2,1)S(1)} %get-tuple-element.619), channel_id=1, source_target_pairs={{0,1},{1,0},{2,3},{3,2},{4,5},{5,4},{6,7},{7,6},{8,9},{9,8},{10,11... | collective-permute-start | bytes 294920 | tf_op jit(solution)/shard_map/ppermute | solution.py:101
  68.1 1.6 %collective-permute-start.196 = (bf16[64,2048]{1,0:T(8,128)(2,1)S(1)}, bf16[64,2048]{1,0:T(8,128)(2,1)S(1)}, u32[]{:S(2)}, u32[]{:S(2)}) collective-permute-start(bf16[64,2048]{1,0:T(8,128)(2,1)S(1)} %collective-permute-done.195.refs_7_), channel_id=1, source_target_pairs={{0,2},{2,0},{4,6},{6,4},{8,10},{10,8},{12,14},{14,12},{16,18},{18,... | collective-permute-start | bytes 786440 | tf_op jit(solution)/shard_map/ppermute | solution.py:101
  70.3 4.9 %collective-permute-start.197 = (bf16[128,384]{1,0:T(8,128)(2,1)S(1)}, bf16[128,384]{1,0:T(8,128)(2,1)S(1)}, u32[]{:S(2)}, u32[]{:S(2)}) collective-permute-start(bf16[128,384]{1,0:T(8,128)(2,1)S(1)} %get-tuple-element.613), channel_id=1, source_target_pairs={{0,1},{1,0},{2,3},{3,2},{4,5},{5,4},{6,7},{7,6},{8,9},{9,8},{10,11... | collective-permute-start | bytes 294920 | tf_op jit(solution)/shard_map/ppermute | solution.py:101

commit v8 on v7

--- a/solution.py
+++ b/solution.py
@@ -213,6 +213,8 @@
         )
         for (grad_home, far), (near, farther) in zip(returned, swapped):
             early.append((grad_home, near, far, farther))
+        if m + 1 == micro_count:
+            home, sib = leaving(*sent, home_first)
         settled = [settle(home, sib, first, second, to_home_first)]
         sib = arriving[0] if arriving else None
     [(grad_home, grad_sib)] = settled

time: 75.1 us -> 76.4 us (1.017); the launches traced: 76.4 us -> 75.9 us
  starting transfers between devices: 23.5 us -> 29.7 us
  waiting for transfers between devices: 29.3 us -> 23.7 us
    ppermute x4, starting transfers between devices: 10 us -> 16.3 us  [one(): moved = lax.ppermute(moved, 'rep', route)]
    ppermute x4, waiting for transfers between devices: 23.4 us -> 19 us  [one(): moved = lax.ppermute(moved, 'rep', route)]
    ppermute x14, waiting for transfers between devices: 5.96 us -> 4.68 us  [swap(): return lax.ppermute(block, axis, [(i, i ^ bit) for i in range(count)])]
  transfers between devices with their start and end apart: 18 -> 18, of which waited for: 9 -> 8; matrix products, arithmetic and copies ran while one was open for 9% -> 9% of each run, Pallas kernels for 7% -> 7%
where the time goes in v8:
time: 76.4 us; the launch traced here: 75.9 us
  starting transfers between devices  29.7 us (39%)
  waiting for transfers between devices  23.7 us (31%)
  matrix products  9.09 us (12%)
  Pallas kernels  5.66 us (7%)
  between operations  3.48 us (5%)
  other arithmetic  3.11 us (4%)
  local copies, waits for them, and re-layouts  0.91 us (1%)
    ppermute x4, waiting for transfers between devices, one(): moved = lax.ppermute(moved, 'rep', route)  19 us
    ppermute x4, starting transfers between devices, one(): moved = lax.ppermute(moved, 'rep', route)  16.3 us
    ppermute x14, starting transfers between devices, swap(): return lax.ppermute(block, axis, [(i, i ^ bit) for i in range(count)])  13.4 us
    ppermute x14, waiting for transfers between devices, swap(): return lax.ppermute(block, axis, [(i, i ^ bit) for i in range(count)])  4.68 us
    dot_general x4, matrix products, back(): jnp.einsum('rv,wv->rw', gradient, head_weight, preferred_element_type=jnp...  4.36 us
    pallas_call x1, Pallas kernels, head_gradient(): pl.pallas_call(head_kernel, grid=(vocab // step,), out_shape=jax.ShapeDty...  4.15 us
  transfers between devices with their start and end apart: 18, of which 8 were waited for; matrix products, arithmetic and copies ran while one was open for 9% of the time, Pallas kernels for 7%

profile of v8, /device:TPU:0, one launch (start us, length us, event | category | flops | bytes accessed | tf_op | source)
XLA Modules:
  0.0 75.9 jit_solution(14982746766687503688)
XLA Ops:
  0.7 0.8 %constant_dynamic-slice_fusion = s32[2,1,256]{2,1,0:T(1,128)S(1)} fusion(s32[2,8,256]{2,1,0:T(8,128)} %param.103, s32[]{:T(128)S(6)} %select_n.86), kind=kLoop, calls=%fused_computation.86 | loop fusion | bytes 4100 | tf_op jit(solution)/shard_map/jit(dynamic_index_in_dim)/dynamic_slice | solution.py:161
  1.7 1.2 %convolution_convert_fusion.3 = bf16[256,384]{1,0:T(8,128)(2,1)S(1)} fusion(pred[2,256,256]{2,1,0:T(32,128)(4,1)S(1)} %broadcast_compare_fusion, bf16[2,256,384]{2,1,0:T(8,128)(2,1)} %param.100), kind=kOutput, calls=%fused_computation.3 | convolution fusion | flops 50429952 | bytes 458752 | tf_op jit(solution)/shard_map/dot_general | solution.py:174
  6.2 3.0 %collective-permute-start.190 = (bf16[64,2048]{1,0:T(8,128)(2,1)S(1)}, bf16[64,2048]{1,0:T(8,128)(2,1)S(1)}, u32[]{:S(2)}, u32[]{:S(2)}) collective-permute-start(bf16[64,2048]{1,0:T(8,128)(2,1)S(1)} %fusion.2), channel_id=1, source_target_pairs={{0,4},{2,6},{4,0},{6,2},{8,12},{10,14},{12,8},{14,10},{16,20},{18,... | collective-permute-start | bytes 786440 | tf_op jit(solution)/shard_map/ppermute | solution.py:101
  9.3 1.5 %shard_map.59 = (s32[1]{0:T(128)}, s32[1]{0:T(128)}, s32[1]{0:T(128)}, s32[1]{0:T(128)}, s32[4,2048]{1,0:T(4,128)S(1)}) custom-call(s32[2,8]{1,0:T(2,128)S(1)} %copy-done.1), custom_call_target="tpu_custom_call" | custom-call | tf_op jit(solution)/shard_map/pallas_call | solution.py:74
  13.5 2.3 %collective-permute-done.190 = bf16[64,2048]{1,0:T(8,128)(2,1)S(1)} collective-permute-done((bf16[64,2048]{1,0:T(8,128)(2,1)S(1)}, bf16[64,2048]{1,0:T(8,128)(2,1)S(1)}, u32[]{:S(2)}, u32[]{:S(2)}) %collective-permute-start.190) | collective-permute-done | bytes 262176 | tf_op jit(solution)/shard_map/ppermute | solution.py:101
  16.0 11.6 %conditional.4 = (bf16[64,2048]{1,0:T(8,128)(2,1)S(1)}, bf16[64,2048]{1,0:T(8,128)(2,1)}) conditional(s32[]{:T(128)} %bitcast.4, (bf16[64,2048]{1,0:T(8,128)(2,1)S(1)}, bf16[64,2048]{1,0:T(8,128)(2,1)S(1)}) %tuple.379, (bf16[64,2048]{1,0:T(8,128)(2,1)S(1)}, bf16[64,2048]{1,0:T(8,128)(2,1)S(1)}) %tuple.380, ...), branch_computations={%region_0.1_spmd, %region_1.2_spmd, %region_2.3_spmd, %region_3.4_... | conditional | bytes 2621536 | solution.py:96
  16.0 3.7 %collective-permute-start.21 = (bf16[64,2048]{1,0:T(8,128)(2,1)S(1)}, bf16[64,2048]{1,0:T(8,128)(2,1)S(1)}, u32[]{:S(2)}, u32[]{:S(2)}) collective-permute-start(bf16[64,2048]{1,0:T(8,128)(2,1)S(1)} %get-tuple-element.407), channel_id=1, source_target_pairs={{0,8},{2,10},{4,12},{6,14},{8,24},{10,26},{12,28},{14,30},{16,16},... | collective-permute-start | bytes 786440 | tf_op jit(solution)/shard_map/cond/branch_11_fun/ppermute | solution.py:92
  19.7 1.6 %collective-permute-start.22 = (bf16[64,2048]{1,0:T(8,128)(2,1)S(1)}, bf16[64,2048]{1,0:T(8,128)(2,1)}, u32[]{:S(2)}, u32[]{:S(2)}) collective-permute-start(bf16[64,2048]{1,0:T(8,128)(2,1)S(1)} %get-tuple-element.408), channel_id=1, source_target_pairs={{0,4},{2,6},{4,0},{6,2},{8,12},{10,14},{12,8},{14,10},{16,20},{18,... | collective-permute-start | bytes 786440 | tf_op jit(solution)/shard_map/cond/branch_11_fun/ppermute | solution.py:101
  21.3 6.2 %collective-permute-done.21 = bf16[64,2048]{1,0:T(8,128)(2,1)S(1)} collective-permute-done((bf16[64,2048]{1,0:T(8,128)(2,1)S(1)}, bf16[64,2048]{1,0:T(8,128)(2,1)S(1)}, u32[]{:S(2)}, u32[]{:S(2)}) %collective-permute-start.21) | collective-permute-done | bytes 262176 | tf_op jit(solution)/shard_map/cond/branch_11_fun/ppermute | solution.py:92
  27.6 0.8 %conditional.5 = (bf16[64,2048]{1,0:T(8,128)(2,1)S(1)}) conditional(s32[]{:T(128)} %bitcast.5, bf16[64,2048]{1,0:T(8,128)(2,1)S(1)} %get-tuple-element.582, bf16[64,2048]{1,0:T(8,128)(2,1)S(1)} %get-tuple-element.582, bf16[64,2048]{1,0:T(8,128)(2,1)S(1)} %get-tuple-element.582, ...), branch_computations={%region_24.25_spmd, %region_25.26_spmd, %region_26.27_spmd, %regio... | conditional | bytes 1572912 | solution.py:96
  27.6 0.7 collective-permute-start.50
  28.4 1.0 %broadcast_select_fusion = (bf16[64,2048]{1,0:T(8,128)(2,1)S(1)}, bf16[64,2048]{1,0:T(8,128)(2,1)S(1)}) fusion(bf16[64,2048]{1,0:T(8,128)(2,1)} %get-tuple-element.583, bf16[64,2048]{1,0:T(8,128)(2,1)S(1)} %get-tuple-element.606, pred[2048]{0:T(1024)(128)(4,1)S(1)} %get-tuple-element.600), kind=kLoop, calls=%fused_computation.48 | loop fusion | flops 262144 | bytes 1050624 | tf_op jit(solution)/shard_map/jit(_where)/select_n | solution.py:190
  29.6 16.2 %conditional.6 = (bf16[64,2048]{1,0:T(8,128)(2,1)}, bf16[64,2048]{1,0:T(8,128)(2,1)}) conditional(s32[]{:T(128)} %bitcast.6, (bf16[64,2048]{1,0:T(8,128)(2,1)S(1)}, bf16[64,2048]{1,0:T(8,128)(2,1)S(1)}) %tuple.384, (bf16[64,2048]{1,0:T(8,128)(2,1)S(1)}, bf16[64,2048]{1,0:T(8,128)(2,1)S(1)}) %tuple.385, ...), branch_computations={%region_48.49_spmd, %region_49.50_spmd, %region_50.51_spmd, %regio... | conditional | bytes 2097248 | solution.py:96
  29.6 9.7 %collective-permute-start.87 = (bf16[64,2048]{1,0:T(8,128)(2,1)S(1)}, bf16[64,2048]{1,0:T(8,128)(2,1)}, u32[]{:S(2)}, u32[]{:S(2)}) collective-permute-start(bf16[64,2048]{1,0:T(8,128)(2,1)S(1)} %get-tuple-element.451), channel_id=1, source_target_pairs={{0,8},{2,10},{4,12},{6,14},{8,16},{10,18},{12,20},{14,22},{16,24},... | collective-permute-start | bytes 786440 | tf_op jit(solution)/shard_map/cond/branch_9_fun/ppermute | solution.py:92
  39.3 1.5 %collective-permute-start.88 = (bf16[64,2048]{1,0:T(8,128)(2,1)S(1)}, bf16[64,2048]{1,0:T(8,128)(2,1)}, u32[]{:S(2)}, u32[]{:S(2)}) collective-permute-start(bf16[64,2048]{1,0:T(8,128)(2,1)S(1)} %get-tuple-element.452), channel_id=1, source_target_pairs={{0,4},{2,6},{4,0},{6,2},{8,12},{10,14},{12,8},{14,10},{16,20},{18,... | collective-permute-start | bytes 786440 | tf_op jit(solution)/shard_map/cond/branch_9_fun/ppermute | solution.py:101
  40.9 4.7 %collective-permute-done.87 = bf16[64,2048]{1,0:T(8,128)(2,1)} collective-permute-done((bf16[64,2048]{1,0:T(8,128)(2,1)S(1)}, bf16[64,2048]{1,0:T(8,128)(2,1)}, u32[]{:S(2)}, u32[]{:S(2)}) %collective-permute-start.87) | collective-permute-done | bytes 262176 | tf_op jit(solution)/shard_map/cond/branch_9_fun/ppermute | solution.py:92
  45.8 10.9 %conditional.7 = (bf16[64,2048]{1,0:T(8,128)(2,1)}, bf16[64,2048]{1,0:T(8,128)(2,1)}, bf16[64,2048]{1,0:T(8,128)(2,1)}) conditional(s32[]{:T(128)} %bitcast.7, (bf16[64,2048]{1,0:T(8,128)(2,1)S(1)}, bf16[64,2048]{1,0:T(8,128)(2,1)}, bf16[64,2048]{1,0:T(8,128)(2,1)S(1)}) %tuple.387, (bf16[64,2048]{1,0:T(8,128)(2,1)S(1)}, ...), branch_computations={%region_72.73_spmd, %region_73.74_spmd, %region_74.75_spmd, %regio... | conditional | bytes 3145872 | solution.py:96
  45.8 2.2 %collective-permute-start.164 = (bf16[64,2048]{1,0:T(8,128)(2,1)S(1)}, bf16[64,2048]{1,0:T(8,128)(2,1)}, u32[]{:S(2)}, u32[]{:S(2)}) collective-permute-start(bf16[64,2048]{1,0:T(8,128)(2,1)S(1)} %get-tuple-element.529), channel_id=1, source_target_pairs={{0,16},{2,18},{4,20},{6,22},{8,24},{10,26},{12,28},{14,30},{16,0},... | collective-permute-start | bytes 786440 | tf_op jit(solution)/shard_map/cond/branch_16_fun/ppermute | solution.py:92
  48.5 8.1 %collective-permute-done.164 = bf16[64,2048]{1,0:T(8,128)(2,1)} collective-permute-done((bf16[64,2048]{1,0:T(8,128)(2,1)S(1)}, bf16[64,2048]{1,0:T(8,128)(2,1)}, u32[]{:S(2)}, u32[]{:S(2)}) %collective-permute-start.164) | collective-permute-done | bytes 262176 | tf_op jit(solution)/shard_map/cond/branch_16_fun/ppermute | solution.py:92
  56.7 1.3 %multiply_convert_fusion.1 = (bf16[64,2048]{1,0:T(8,128)(2,1)S(1)}, bf16[64,2048]{1,0:T(8,128)(2,1)S(1)}) fusion(bf16[64,2048]{1,0:T(8,128)(2,1)} %get-tuple-element.587, bf16[64,2048]{1,0:T(8,128)(2,1)} %get-tuple-element.591, bf16[64,2048]{1,0:T(8,128)(2,1)S(1)} %get-tuple-element.584, bf16[64,2048]{1,0:T(8,128)(2,1)S(1)} %get-tuple-element.590, ...), kind=kLoop, calls=%fused_computation.31 | loop fusion | flops 1835008 | bytes 1576960 | tf_op jit(solution)/shard_map/convert_element_type | solution.py:106
  58.1 1.6 %collective-permute-start.195 = (bf16[64,2048]{1,0:T(8,128)(2,1)S(1)}, bf16[64,2048]{1,0:T(8,128)(2,1)S(1)}, u32[]{:S(2)}, u32[]{:S(2)}) collective-permute-start(bf16[64,2048]{1,0:T(8,128)(2,1)S(1)} %get-tuple-element.608), channel_id=1, source_target_pairs={{0,4},{2,6},{4,0},{6,2},{8,12},{10,14},{12,8},{14,10},{16,20},{18,... | collective-permute-start | bytes 786440 | tf_op jit(solution)/shard_map/ppermute | solution.py:101
  59.6 0.6 fusion.58
  60.2 1.6 %collective-permute-start.194 = (bf16[128,384]{1,0:T(8,128)(2,1)S(1)}, bf16[128,384]{1,0:T(8,128)(2,1)S(1)}, u32[]{:S(2)}, u32[]{:S(2)}) collective-permute-start(bf16[128,384]{1,0:T(8,128)(2,1)S(1)} %get-tuple-element.615), channel_id=1, source_target_pairs={{0,1},{1,0},{2,3},{3,2},{4,5},{5,4},{6,7},{7,6},{8,9},{9,8},{10,11... | collective-permute-start | bytes 294920 | tf_op jit(solution)/shard_map/ppermute | solution.py:101
  61.8 1.6 %fusion.59 = (bf16[128,384]{1,0:T(8,128)(2,1)S(1)}, f32[128,384]{1,0:T(8,128)S(1)}) fusion(bf16[384,2048]{1,0:T(8,128)(2,1)S(1)} %copy-done, bf16[64,2048]{1,0:T(8,128)(2,1)} %get-tuple-element.597.refs_4_, bf16[64,2048]{1,0:T(8,128)(2,1)} %get-tuple-element.595.refs_3_), kind=kOutput, calls=%fused_computation.94 | convolution fusion | flops 202424320 | bytes 2392064 | tf_op jit(solution)/shard_map/rv,wv->rw/dot_general | solution.py:233
  64.0 1.5 %fusion.60 = (bf16[128,384]{1,0:T(8,128)(2,1)S(1)}, f32[128,384]{1,0:T(8,128)S(1)}) fusion(bf16[384,2048]{1,0:T(8,128)(2,1)S(1)} %copy-done, bf16[64,2048]{1,0:T(8,128)(2,1)} %get-tuple-element.594.refs_2_, bf16[64,2048]{1,0:T(8,128)(2,1)S(1)} %get-tuple-element.592.refs_1_), kind=kOutput, calls=%fused_computation.95 | convolution fusion | flops 202424320 | bytes 2392064 | tf_op jit(solution)/shard_map/rv,wv->rw/dot_general | solution.py:233
  65.6 1.6 %collective-permute-start.192 = (bf16[128,384]{1,0:T(8,128)(2,1)S(1)}, bf16[128,384]{1,0:T(8,128)(2,1)S(1)}, u32[]{:S(2)}, u32[]{:S(2)}) collective-permute-start(bf16[128,384]{1,0:T(8,128)(2,1)S(1)} %get-tuple-element.619), channel_id=1, source_target_pairs={{0,1},{1,0},{2,3},{3,2},{4,5},{5,4},{6,7},{7,6},{8,9},{9,8},{10,11... | collective-permute-start | bytes 294920 | tf_op jit(solution)/shard_map/ppermute | solution.py:101
  67.6 0.8 %collective-permute-done.193 = bf16[128,384]{1,0:T(8,128)(2,1)S(1)} collective-permute-done((bf16[128,384]{1,0:T(8,128)(2,1)S(1)}, bf16[128,384]{1,0:T(8,128)(2,1)S(1)}, u32[]{:S(2)}, u32[]{:S(2)}) %collective-permute-start.193) | collective-permute-done | bytes 98336 | tf_op jit(solution)/shard_map/ppermute | solution.py:101
  68.5 0.7 collective-permute-done.196.refs_8_
  69.1 0.6 fusion.57
  69.7 0.7 collective-permute-start.197
  70.5 4.2 %shard_map.60 = bf16[384,2048]{1,0:T(8,128)(2,1)} custom-call(bf16[512,384]{1,0:T(8,128)(2,1)S(1)} %bitcast.37, bf16[64,2048]{1,0:T(8,128)(2,1)S(1)} %get-tuple-element.592.refs_1_, bf16[64,2048]{1,0:T(8,128)(2,1)} %get-tuple-element.594.refs_2_, bf16[64,2048]{1,0:T(8,128)(2,1)} %get-tuple-element.595.refs_3_, bf16[64,2048]{1,0:T(8,128)(2,1)} %get-tuple-element.597.refs_4_, ...), custom_call_target="tpu_custom_call" | custom-call | flops 805306368 | bytes 4063232 | tf_op jit(solution)/shard_map/pallas_call | solution.py:133
  74.7 1.2 %convolution_convert_fusion.1 = bf16[2,256,384]{2,1,0:T(8,128)(2,1)} fusion(bf16[1,128,384]{2,1,0:T(8,128)(2,1)S(1)} %fusion.40, bf16[1,128,384]{2,1,0:T(8,128)(2,1)S(1)} %fusion.39, bf16[1,128,384]{2,1,0:T(8,128)(2,1)S(1)} %fusion.38, bf16[1,128,384]{2,1,0:T(8,128)(2,1)S(1)} %fusion.37, s32[2,256]{1,0:T(2,128)S(1)} %bitcast.40, s32[256]{0:T(256)S(1)} %add_add_fusion.1), kind=kOutput, calls=%fused_computation.1 | convolution fusion | flops 102563840 | bytes 789504 | tf_op jit(solution)/shard_map/mei,mew->miw/dot_general | solution.py:242
  (49 shorter events, 6.1 us)
Async XLA Ops:
  0.6 2.3 %copy-start = (bf16[384,2048]{1,0:T(8,128)(2,1)S(1)}, bf16[384,2048]{1,0:T(8,128)(2,1)}, u32[]{:S(2)}) copy-start(bf16[384,2048]{1,0:T(8,128)(2,1)} %param.101) | copy-start | bytes 4718596
  1.7 2.2 %copy-start.2 = (bf16[2,256,384]{2,1,0:T(8,128)(2,1)S(1)}, bf16[2,256,384]{2,1,0:T(8,128)(2,1)}, u32[]{:S(2)}) copy-start(bf16[2,256,384]{2,1,0:T(8,128)(2,1)} %param.100) | copy-start | bytes 1179652
  3.4 2.8 %collective-permute-start.188 = (f32[128,2048]{1,0:T(8,128)S(1)}, f32[128,2048]{1,0:T(8,128)S(1)}, u32[]{:S(2)}, u32[]{:S(2)}) collective-permute-start(f32[128,2048]{1,0:T(8,128)S(1)} %fusion.45), channel_id=1, source_target_pairs={{0,2},{2,0},{4,6},{6,4},{8,10},{10,8},{12,14},{14,12},{16,18},{18,... | collective-permute-start | bytes 3145736 | tf_op jit(solution)/shard_map/ppermute | solution.py:101
  4.6 4.6 %collective-permute-start.189 = (f32[128,2048]{1,0:T(8,128)S(1)}, f32[128,2048]{1,0:T(8,128)S(1)}, u32[]{:S(2)}, u32[]{:S(2)}) collective-permute-start(f32[128,2048]{1,0:T(8,128)S(1)} %fusion.41), channel_id=1, source_target_pairs={{0,2},{2,0},{4,6},{6,4},{8,10},{10,8},{12,14},{14,12},{16,18},{18,... | collective-permute-start | bytes 3145736 | tf_op jit(solution)/shard_map/ppermute | solution.py:101
  6.2 3.1 %copy-start.1 = (s32[2,8]{1,0:T(2,128)S(1)}, s32[2,8]{1,0:T(2,128)}, u32[]{:S(2)}) copy-start(s32[2,8]{1,0:T(2,128)} %order_ref) | copy-start | bytes 196
  6.2 9.6 %collective-permute-start.190 = (bf16[64,2048]{1,0:T(8,128)(2,1)S(1)}, bf16[64,2048]{1,0:T(8,128)(2,1)S(1)}, u32[]{:S(2)}, u32[]{:S(2)}) collective-permute-start(bf16[64,2048]{1,0:T(8,128)(2,1)S(1)} %fusion.2), channel_id=1, source_target_pairs={{0,4},{2,6},{4,0},{6,2},{8,12},{10,14},{12,8},{14,10},{16,20},{18,... | collective-permute-start | bytes 786440 | tf_op jit(solution)/shard_map/ppermute | solution.py:101
  16.0 11.5 %collective-permute-start.21 = (bf16[64,2048]{1,0:T(8,128)(2,1)S(1)}, bf16[64,2048]{1,0:T(8,128)(2,1)S(1)}, u32[]{:S(2)}, u32[]{:S(2)}) collective-permute-start(bf16[64,2048]{1,0:T(8,128)(2,1)S(1)} %get-tuple-element.407), channel_id=1, source_target_pairs={{0,8},{2,10},{4,12},{6,14},{8,24},{10,26},{12,28},{14,30},{16,16},... | collective-permute-start | bytes 786440 | tf_op jit(solution)/shard_map/cond/branch_11_fun/ppermute | solution.py:92
  19.7 7.8 %collective-permute-start.22 = (bf16[64,2048]{1,0:T(8,128)(2,1)S(1)}, bf16[64,2048]{1,0:T(8,128)(2,1)}, u32[]{:S(2)}, u32[]{:S(2)}) collective-permute-start(bf16[64,2048]{1,0:T(8,128)(2,1)S(1)} %get-tuple-element.408), channel_id=1, source_target_pairs={{0,4},{2,6},{4,0},{6,2},{8,12},{10,14},{12,8},{14,10},{16,20},{18,... | collective-permute-start | bytes 786440 | tf_op jit(solution)/shard_map/cond/branch_11_fun/ppermute | solution.py:101
  27.6 0.7 collective-permute-start.50
  29.6 15.9 %collective-permute-start.87 = (bf16[64,2048]{1,0:T(8,128)(2,1)S(1)}, bf16[64,2048]{1,0:T(8,128)(2,1)}, u32[]{:S(2)}, u32[]{:S(2)}) collective-permute-start(bf16[64,2048]{1,0:T(8,128)(2,1)S(1)} %get-tuple-element.451), channel_id=1, source_target_pairs={{0,8},{2,10},{4,12},{6,14},{8,16},{10,18},{12,20},{14,22},{16,24},... | collective-permute-start | bytes 786440 | tf_op jit(solution)/shard_map/cond/branch_9_fun/ppermute | solution.py:92
  39.3 6.5 %collective-permute-start.88 = (bf16[64,2048]{1,0:T(8,128)(2,1)S(1)}, bf16[64,2048]{1,0:T(8,128)(2,1)}, u32[]{:S(2)}, u32[]{:S(2)}) collective-permute-start(bf16[64,2048]{1,0:T(8,128)(2,1)S(1)} %get-tuple-element.452), channel_id=1, source_target_pairs={{0,4},{2,6},{4,0},{6,2},{8,12},{10,14},{12,8},{14,10},{16,20},{18,... | collective-permute-start | bytes 786440 | tf_op jit(solution)/shard_map/cond/branch_9_fun/ppermute | solution.py:101
  45.8 10.9 %collective-permute-start.164 = (bf16[64,2048]{1,0:T(8,128)(2,1)S(1)}, bf16[64,2048]{1,0:T(8,128)(2,1)}, u32[]{:S(2)}, u32[]{:S(2)}) collective-permute-start(bf16[64,2048]{1,0:T(8,128)(2,1)S(1)} %get-tuple-element.529), channel_id=1, source_target_pairs={{0,16},{2,18},{4,20},{6,22},{8,24},{10,26},{12,28},{14,30},{16,0},... | collective-permute-start | bytes 786440 | tf_op jit(solution)/shard_map/cond/branch_16_fun/ppermute | solution.py:92
  48.0 8.7 %collective-permute-start.165 = (bf16[64,2048]{1,0:T(8,128)(2,1)S(1)}, bf16[64,2048]{1,0:T(8,128)(2,1)}, u32[]{:S(2)}, u32[]{:S(2)}) collective-permute-start(bf16[64,2048]{1,0:T(8,128)(2,1)S(1)} %get-tuple-element.530), channel_id=1, source_target_pairs={{0,2},{2,0},{4,6},{6,4},{8,10},{10,8},{12,14},{14,12},{16,18},{18,... | collective-permute-start | bytes 786440 | tf_op jit(solution)/shard_map/cond/branch_16_fun/ppermute | solution.py:101
  48.0 8.7 %collective-permute-start.166 = (bf16[64,2048]{1,0:T(8,128)(2,1)}, bf16[64,2048]{1,0:T(8,128)(2,1)}, u32[]{:S(2)}, u32[]{:S(2)}) collective-permute-start(bf16[64,2048]{1,0:T(8,128)(2,1)} %get-tuple-element.531), channel_id=1, source_target_pairs={{0,2},{2,0},{4,6},{6,4},{8,10},{10,8},{12,14},{14,12},{16,18},{18,... | collective-permute-start | bytes 786440 | tf_op jit(solution)/shard_map/cond/branch_16_fun/ppermute | solution.py:101
  58.0 1.7 %collective-permute-start.191 = (bf16[64,2048]{1,0:T(8,128)(2,1)S(1)}, bf16[64,2048]{1,0:T(8,128)(2,1)S(1)}, u32[]{:S(2)}, u32[]{:S(2)}) collective-permute-start(bf16[64,2048]{1,0:T(8,128)(2,1)S(1)} %get-tuple-element.607.refs_5_), channel_id=1, source_target_pairs={{0,2},{2,0},{4,6},{6,4},{8,10},{10,8},{12,14},{14,12},{16,18},{18,... | collective-permute-start | bytes 786440 | tf_op jit(solution)/shard_map/ppermute | solution.py:101
  58.1 9.5 %collective-permute-start.195 = (bf16[64,2048]{1,0:T(8,128)(2,1)S(1)}, bf16[64,2048]{1,0:T(8,128)(2,1)S(1)}, u32[]{:S(2)}, u32[]{:S(2)}) collective-permute-start(bf16[64,2048]{1,0:T(8,128)(2,1)S(1)} %get-tuple-element.608), channel_id=1, source_target_pairs={{0,4},{2,6},{4,0},{6,2},{8,12},{10,14},{12,8},{14,10},{16,20},{18,... | collective-permute-start | bytes 786440 | tf_op jit(solution)/shard_map/ppermute | solution.py:101
  60.2 7.4 %collective-permute-start.194 = (bf16[128,384]{1,0:T(8,128)(2,1)S(1)}, bf16[128,384]{1,0:T(8,128)(2,1)S(1)}, u32[]{:S(2)}, u32[]{:S(2)}) collective-permute-start(bf16[128,384]{1,0:T(8,128)(2,1)S(1)} %get-tuple-element.615), channel_id=1, source_target_pairs={{0,1},{1,0},{2,3},{3,2},{4,5},{5,4},{6,7},{7,6},{8,9},{9,8},{10,11... | collective-permute-start | bytes 294920 | tf_op jit(solution)/shard_map/ppermute | solution.py:101
  63.4 3.7 %copy-start.3 = (bf16[2,256,384]{2,1,0:T(8,128)(2,1)S(1)}, bf16[2,256,384]{2,1,0:T(8,128)(2,1)}, u32[]{:S(2)}) copy-start(bf16[2,256,384]{2,1,0:T(8,128)(2,1)} %param.100) | copy-start | bytes 1179652
  63.5 5.0 %collective-permute-start.193 = (bf16[128,384]{1,0:T(8,128)(2,1)S(1)}, bf16[128,384]{1,0:T(8,128)(2,1)S(1)}, u32[]{:S(2)}, u32[]{:S(2)}) collective-permute-start(bf16[128,384]{1,0:T(8,128)(2,1)S(1)} %get-tuple-element.617), channel_id=1, source_target_pairs={{0,1},{1,0},{2,3},{3,2},{4,5},{5,4},{6,7},{7,6},{8,9},{9,8},{10,11... | collective-permute-start | bytes 294920 | tf_op jit(solution)/shard_map/ppermute | solution.py:101
  65.6 4.9 %collective-permute-start.192 = (bf16[128,384]{1,0:T(8,128)(2,1)S(1)}, bf16[128,384]{1,0:T(8,128)(2,1)S(1)}, u32[]{:S(2)}, u32[]{:S(2)}) collective-permute-start(bf16[128,384]{1,0:T(8,128)(2,1)S(1)} %get-tuple-element.619), channel_id=1, source_target_pairs={{0,1},{1,0},{2,3},{3,2},{4,5},{5,4},{6,7},{7,6},{8,9},{9,8},{10,11... | collective-permute-start | bytes 294920 | tf_op jit(solution)/shard_map/ppermute | solution.py:101
  67.5 1.6 %collective-permute-start.196 = (bf16[64,2048]{1,0:T(8,128)(2,1)S(1)}, bf16[64,2048]{1,0:T(8,128)(2,1)S(1)}, u32[]{:S(2)}, u32[]{:S(2)}) collective-permute-start(bf16[64,2048]{1,0:T(8,128)(2,1)S(1)} %collective-permute-done.195.refs_7_), channel_id=1, source_target_pairs={{0,2},{2,0},{4,6},{6,4},{8,10},{10,8},{12,14},{14,12},{16,18},{18,... | collective-permute-start | bytes 786440 | tf_op jit(solution)/shard_map/ppermute | solution.py:101
  69.7 4.9 %collective-permute-start.197 = (bf16[128,384]{1,0:T(8,128)(2,1)S(1)}, bf16[128,384]{1,0:T(8,128)(2,1)S(1)}, u32[]{:S(2)}, u32[]{:S(2)}) collective-permute-start(bf16[128,384]{1,0:T(8,128)(2,1)S(1)} %get-tuple-element.613), channel_id=1, source_target_pairs={{0,1},{1,0},{2,3},{3,2},{4,5},{5,4},{6,7},{7,6},{8,9},{9,8},{10,11... | collective-permute-start | bytes 294920 | tf_op jit(solution)/shard_map/ppermute | solution.py:101

commit v9 on v8

--- a/solution.py
+++ b/solution.py
@@ -129,7 +129,7 @@
 def head_gradient(rows, blocks):
     count, width = rows.shape
     height, vocab = blocks[0].shape
-    step = vocab // 4
+    step = vocab // 2
     return pl.pallas_call(
         head_kernel,
         grid=(vocab // step,),
@@ -200,10 +200,10 @@
     for m in range(micro_count):
         home = logits[m][0]
         branches, (home_first, to_home_first) = codes[m]
+        if m > 0:
+            home, sib = (after(block, *settled[0]) for block in (home, sib))
         sent = leaving(home, sib, home_first)
         nexts = [] if m + 1 == micro_count else [logits[m + 1][1]]
-        if m > 0:
-            sent = [after(block, *settled[0]) for block in sent]
         first, (arriving, returned) = move_pairs(
             sent[0], branches[0], pairs, beside, nexts, settled
         )

time: 76.4 us -> 74.5 us (0.975)
  the two profiles are of different devices: /device:TPU:0 before, /device:TPU:8 now
where the time goes in v9:
time: 74.5 us; the launch traced here: 73.5 us
  waiting for transfers between devices  27 us (36%)
  starting transfers between devices  25.1 us (34%)
  matrix products  9.09 us (12%)
  Pallas kernels  4.68 us (6%)
  between operations  3.43 us (5%)
  other arithmetic  3.11 us (4%)
  local copies, waits for them, and re-layouts  0.9 us (1%)
    ppermute x4, waiting for transfers between devices, one(): moved = lax.ppermute(moved, 'rep', route)  21.5 us
    ppermute x4, starting transfers between devices, one(): moved = lax.ppermute(moved, 'rep', route)  12.9 us
    ppermute x14, starting transfers between devices, swap(): return lax.ppermute(block, axis, [(i, i ^ bit) for i in range(count)])  12.2 us
    ppermute x14, waiting for transfers between devices, swap(): return lax.ppermute(block, axis, [(i, i ^ bit) for i in range(count)])  5.51 us
    dot_general x4, matrix products, back(): jnp.einsum('rv,wv->rw', gradient, head_weight, preferred_element_type=jnp...  4.36 us
    pallas_call x1, Pallas kernels, head_gradient(): pl.pallas_call(head_kernel, grid=(vocab // step,), out_shape=jax.ShapeDty...  3.18 us
    pallas_call x1, Pallas kernels, routes(): pl.pallas_call(route_kernel, out_shape=[jax.ShapeDtypeStruct((1,), jnp.in...  1.51 us
  transfers between devices with their start and end apart: 18, of which 9 were waited for; matrix products, arithmetic and copies ran while one was open for 9% of the time, Pallas kernels for 6%

profile of v9, /device:TPU:8, one launch (start us, length us, event | category | flops | bytes accessed | tf_op | source)
XLA Modules:
  0.0 73.5 jit_solution(12071786692546134208)
XLA Ops:
  0.7 0.8 %constant_dynamic-slice_fusion = s32[2,1,256]{2,1,0:T(1,128)S(1)} fusion(s32[2,8,256]{2,1,0:T(8,128)} %param.103, s32[]{:T(128)S(6)} %select_n.86), kind=kLoop, calls=%fused_computation.86 | loop fusion | bytes 4100 | tf_op jit(solution)/shard_map/jit(dynamic_index_in_dim)/dynamic_slice | solution.py:161
  1.7 1.2 %convolution_convert_fusion.3 = bf16[256,384]{1,0:T(8,128)(2,1)S(1)} fusion(pred[2,256,256]{2,1,0:T(32,128)(4,1)S(1)} %broadcast_compare_fusion, bf16[2,256,384]{2,1,0:T(8,128)(2,1)} %param.100), kind=kOutput, calls=%fused_computation.3 | convolution fusion | flops 50429952 | bytes 458752 | tf_op jit(solution)/shard_map/dot_general | solution.py:174
  6.2 1.6 %collective-permute-start.190 = (bf16[64,2048]{1,0:T(8,128)(2,1)S(1)}, bf16[64,2048]{1,0:T(8,128)(2,1)S(1)}, u32[]{:S(2)}, u32[]{:S(2)}) collective-permute-start(bf16[64,2048]{1,0:T(8,128)(2,1)S(1)} %fusion.2), channel_id=1, source_target_pairs={{0,4},{2,6},{4,0},{6,2},{8,12},{10,14},{12,8},{14,10},{16,20},{18,... | collective-permute-start | bytes 786440 | tf_op jit(solution)/shard_map/ppermute | solution.py:101
  7.9 1.5 %shard_map.59 = (s32[1]{0:T(128)}, s32[1]{0:T(128)}, s32[1]{0:T(128)}, s32[1]{0:T(128)}, s32[4,2048]{1,0:T(4,128)S(1)}) custom-call(s32[2,8]{1,0:T(2,128)S(1)} %copy-done.1), custom_call_target="tpu_custom_call" | custom-call | tf_op jit(solution)/shard_map/pallas_call | solution.py:74
  12.0 2.6 %collective-permute-done.190 = bf16[64,2048]{1,0:T(8,128)(2,1)S(1)} collective-permute-done((bf16[64,2048]{1,0:T(8,128)(2,1)S(1)}, bf16[64,2048]{1,0:T(8,128)(2,1)S(1)}, u32[]{:S(2)}, u32[]{:S(2)}) %collective-permute-start.190) | collective-permute-done | bytes 262176 | tf_op jit(solution)/shard_map/ppermute | solution.py:101
  14.7 8.6 %conditional.4 = (bf16[64,2048]{1,0:T(8,128)(2,1)S(1)}, bf16[64,2048]{1,0:T(8,128)(2,1)}) conditional(s32[]{:T(128)} %bitcast.4, (bf16[64,2048]{1,0:T(8,128)(2,1)S(1)}, bf16[64,2048]{1,0:T(8,128)(2,1)S(1)}) %tuple.379, (bf16[64,2048]{1,0:T(8,128)(2,1)S(1)}, bf16[64,2048]{1,0:T(8,128)(2,1)S(1)}) %tuple.380, ...), branch_computations={%region_0.1_spmd, %region_1.2_spmd, %region_2.3_spmd, %region_3.4_... | conditional | bytes 2621536 | solution.py:96
  15.1 1.7 %collective-permute-start.26 = (bf16[64,2048]{1,0:T(8,128)(2,1)S(1)}, bf16[64,2048]{1,0:T(8,128)(2,1)}, u32[]{:S(2)}, u32[]{:S(2)}) collective-permute-start(bf16[64,2048]{1,0:T(8,128)(2,1)S(1)} %get-tuple-element.412), channel_id=1, source_target_pairs={{0,4},{2,6},{4,0},{6,2},{8,12},{10,14},{12,8},{14,10},{16,20},{18,... | collective-permute-start | bytes 786440 | tf_op jit(solution)/shard_map/cond/branch_13_fun/ppermute | solution.py:101
  16.8 6.5 %collective-permute-done.25 = bf16[64,2048]{1,0:T(8,128)(2,1)S(1)} collective-permute-done((bf16[64,2048]{1,0:T(8,128)(2,1)S(1)}, bf16[64,2048]{1,0:T(8,128)(2,1)S(1)}, u32[]{:S(2)}, u32[]{:S(2)}) %collective-permute-start.25) | collective-permute-done | bytes 262176 | tf_op jit(solution)/shard_map/cond/branch_13_fun/ppermute | solution.py:92
  23.3 8.6 %conditional.5 = (bf16[64,2048]{1,0:T(8,128)(2,1)S(1)}) conditional(s32[]{:T(128)} %bitcast.5, bf16[64,2048]{1,0:T(8,128)(2,1)S(1)} %get-tuple-element.582, bf16[64,2048]{1,0:T(8,128)(2,1)S(1)} %get-tuple-element.582, bf16[64,2048]{1,0:T(8,128)(2,1)S(1)} %get-tuple-element.582, ...), branch_computations={%region_24.25_spmd, %region_25.26_spmd, %region_26.27_spmd, %regio... | conditional | bytes 1572912 | solution.py:96
  23.4 3.7 %collective-permute-start.50 = (bf16[64,2048]{1,0:T(8,128)(2,1)S(1)}, bf16[64,2048]{1,0:T(8,128)(2,1)S(1)}, u32[]{:S(2)}, u32[]{:S(2)}) collective-permute-start(bf16[64,2048]{1,0:T(8,128)(2,1)S(1)} %param.28), channel_id=1, source_target_pairs={{0,0},{2,2},{4,4},{6,6},{8,24},{10,26},{12,28},{14,30},{16,8},{18,... | collective-permute-start | bytes 786440 | tf_op jit(solution)/shard_map/cond/branch_4_fun/ppermute | solution.py:92
  27.0 4.8 %collective-permute-done.50 = bf16[64,2048]{1,0:T(8,128)(2,1)S(1)} collective-permute-done((bf16[64,2048]{1,0:T(8,128)(2,1)S(1)}, bf16[64,2048]{1,0:T(8,128)(2,1)S(1)}, u32[]{:S(2)}, u32[]{:S(2)}) %collective-permute-start.50) | collective-permute-done | bytes 262176 | tf_op jit(solution)/shard_map/cond/branch_4_fun/ppermute | solution.py:92
  32.1 1.0 %broadcast_select_fusion = (bf16[64,2048]{1,0:T(8,128)(2,1)S(1)}, bf16[64,2048]{1,0:T(8,128)(2,1)S(1)}) fusion(bf16[64,2048]{1,0:T(8,128)(2,1)} %get-tuple-element.585, bf16[64,2048]{1,0:T(8,128)(2,1)S(1)} %get-tuple-element.583, pred[2048]{0:T(1024)(128)(4,1)S(1)} %get-tuple-element.600), kind=kLoop, calls=%fused_computation.48 | loop fusion | flops 262144 | bytes 1050624 | tf_op jit(solution)/shard_map/jit(_where)/select_n | solution.py:190
  33.1 10.6 %conditional.6 = (bf16[64,2048]{1,0:T(8,128)(2,1)}, bf16[64,2048]{1,0:T(8,128)(2,1)}) conditional(s32[]{:T(128)} %bitcast.6, (bf16[64,2048]{1,0:T(8,128)(2,1)S(1)}, bf16[64,2048]{1,0:T(8,128)(2,1)S(1)}) %tuple.384, (bf16[64,2048]{1,0:T(8,128)(2,1)S(1)}, bf16[64,2048]{1,0:T(8,128)(2,1)S(1)}) %tuple.385, ...), branch_computations={%region_48.49_spmd, %region_49.50_spmd, %region_50.51_spmd, %regio... | conditional | bytes 2097248 | solution.py:96
  33.2 2.7 %collective-permute-start.89 = (bf16[64,2048]{1,0:T(8,128)(2,1)S(1)}, bf16[64,2048]{1,0:T(8,128)(2,1)}, u32[]{:S(2)}, u32[]{:S(2)}) collective-permute-start(bf16[64,2048]{1,0:T(8,128)(2,1)S(1)} %get-tuple-element.453), channel_id=1, source_target_pairs={{0,8},{2,10},{4,12},{6,14},{8,24},{10,26},{12,28},{14,30},{16,0},{... | collective-permute-start | bytes 786440 | tf_op jit(solution)/shard_map/cond/branch_10_fun/ppermute | solution.py:92
  35.9 1.5 %collective-permute-start.90 = (bf16[64,2048]{1,0:T(8,128)(2,1)S(1)}, bf16[64,2048]{1,0:T(8,128)(2,1)}, u32[]{:S(2)}, u32[]{:S(2)}) collective-permute-start(bf16[64,2048]{1,0:T(8,128)(2,1)S(1)} %get-tuple-element.454), channel_id=1, source_target_pairs={{0,4},{2,6},{4,0},{6,2},{8,12},{10,14},{12,8},{14,10},{16,20},{18,... | collective-permute-start | bytes 786440 | tf_op jit(solution)/shard_map/cond/branch_10_fun/ppermute | solution.py:101
  37.4 6.3 %collective-permute-done.89 = bf16[64,2048]{1,0:T(8,128)(2,1)} collective-permute-done((bf16[64,2048]{1,0:T(8,128)(2,1)S(1)}, bf16[64,2048]{1,0:T(8,128)(2,1)}, u32[]{:S(2)}, u32[]{:S(2)}) %collective-permute-start.89) | collective-permute-done | bytes 262176 | tf_op jit(solution)/shard_map/cond/branch_10_fun/ppermute | solution.py:92
  43.7 10.7 %conditional.7 = (bf16[64,2048]{1,0:T(8,128)(2,1)}, bf16[64,2048]{1,0:T(8,128)(2,1)}, bf16[64,2048]{1,0:T(8,128)(2,1)}) conditional(s32[]{:T(128)} %bitcast.7, (bf16[64,2048]{1,0:T(8,128)(2,1)S(1)}, bf16[64,2048]{1,0:T(8,128)(2,1)}, bf16[64,2048]{1,0:T(8,128)(2,1)S(1)}) %tuple.387, (bf16[64,2048]{1,0:T(8,128)(2,1)S(1)}, ...), branch_computations={%region_72.73_spmd, %region_73.74_spmd, %region_74.75_spmd, %regio... | conditional | bytes 3145872 | solution.py:96
  43.7 6.3 %collective-permute-start.164 = (bf16[64,2048]{1,0:T(8,128)(2,1)S(1)}, bf16[64,2048]{1,0:T(8,128)(2,1)}, u32[]{:S(2)}, u32[]{:S(2)}) collective-permute-start(bf16[64,2048]{1,0:T(8,128)(2,1)S(1)} %get-tuple-element.529), channel_id=1, source_target_pairs={{0,16},{2,18},{4,20},{6,22},{8,24},{10,26},{12,28},{14,30},{16,0},... | collective-permute-start | bytes 786440 | tf_op jit(solution)/shard_map/cond/branch_16_fun/ppermute | solution.py:92
  50.5 3.9 %collective-permute-done.164 = bf16[64,2048]{1,0:T(8,128)(2,1)} collective-permute-done((bf16[64,2048]{1,0:T(8,128)(2,1)S(1)}, bf16[64,2048]{1,0:T(8,128)(2,1)}, u32[]{:S(2)}, u32[]{:S(2)}) %collective-permute-start.164) | collective-permute-done | bytes 262176 | tf_op jit(solution)/shard_map/cond/branch_16_fun/ppermute | solution.py:92
  54.4 1.3 %multiply_convert_fusion.1 = (bf16[64,2048]{1,0:T(8,128)(2,1)S(1)}, bf16[64,2048]{1,0:T(8,128)(2,1)S(1)}) fusion(bf16[64,2048]{1,0:T(8,128)(2,1)} %get-tuple-element.587, bf16[64,2048]{1,0:T(8,128)(2,1)} %get-tuple-element.591, bf16[64,2048]{1,0:T(8,128)(2,1)S(1)} %get-tuple-element.610, bf16[64,2048]{1,0:T(8,128)(2,1)S(1)} %get-tuple-element.590, ...), kind=kLoop, calls=%fused_computation.31 | loop fusion | flops 1835008 | bytes 1576960 | tf_op jit(solution)/shard_map/convert_element_type | solution.py:106
  55.8 1.6 %collective-permute-start.195 = (bf16[64,2048]{1,0:T(8,128)(2,1)S(1)}, bf16[64,2048]{1,0:T(8,128)(2,1)S(1)}, u32[]{:S(2)}, u32[]{:S(2)}) collective-permute-start(bf16[64,2048]{1,0:T(8,128)(2,1)S(1)} %get-tuple-element.608), channel_id=1, source_target_pairs={{0,4},{2,6},{4,0},{6,2},{8,12},{10,14},{12,8},{14,10},{16,20},{18,... | collective-permute-start | bytes 786440 | tf_op jit(solution)/shard_map/ppermute | solution.py:101
  58.0 1.6 %collective-permute-start.194 = (bf16[128,384]{1,0:T(8,128)(2,1)S(1)}, bf16[128,384]{1,0:T(8,128)(2,1)S(1)}, u32[]{:S(2)}, u32[]{:S(2)}) collective-permute-start(bf16[128,384]{1,0:T(8,128)(2,1)S(1)} %get-tuple-element.615), channel_id=1, source_target_pairs={{0,1},{1,0},{2,3},{3,2},{4,5},{5,4},{6,7},{7,6},{8,9},{9,8},{10,11... | collective-permute-start | bytes 294920 | tf_op jit(solution)/shard_map/ppermute | solution.py:101
  59.5 1.6 %fusion.59 = (bf16[128,384]{1,0:T(8,128)(2,1)S(1)}, f32[128,384]{1,0:T(8,128)S(1)}) fusion(bf16[384,2048]{1,0:T(8,128)(2,1)S(1)} %copy-done, bf16[64,2048]{1,0:T(8,128)(2,1)} %get-tuple-element.597.refs_4_, bf16[64,2048]{1,0:T(8,128)(2,1)} %get-tuple-element.595.refs_3_), kind=kOutput, calls=%fused_computation.94 | convolution fusion | flops 202424320 | bytes 2392064 | tf_op jit(solution)/shard_map/rv,wv->rw/dot_general | solution.py:233
  61.8 1.5 %fusion.60 = (bf16[128,384]{1,0:T(8,128)(2,1)S(1)}, f32[128,384]{1,0:T(8,128)S(1)}) fusion(bf16[384,2048]{1,0:T(8,128)(2,1)S(1)} %copy-done, bf16[64,2048]{1,0:T(8,128)(2,1)} %get-tuple-element.594.refs_2_, bf16[64,2048]{1,0:T(8,128)(2,1)S(1)} %get-tuple-element.592.refs_1_), kind=kOutput, calls=%fused_computation.95 | convolution fusion | flops 202424320 | bytes 2392064 | tf_op jit(solution)/shard_map/rv,wv->rw/dot_general | solution.py:233
  63.3 1.6 %collective-permute-start.192 = (bf16[128,384]{1,0:T(8,128)(2,1)S(1)}, bf16[128,384]{1,0:T(8,128)(2,1)S(1)}, u32[]{:S(2)}, u32[]{:S(2)}) collective-permute-start(bf16[128,384]{1,0:T(8,128)(2,1)S(1)} %get-tuple-element.619), channel_id=1, source_target_pairs={{0,1},{1,0},{2,3},{3,2},{4,5},{5,4},{6,7},{7,6},{8,9},{9,8},{10,11... | collective-permute-start | bytes 294920 | tf_op jit(solution)/shard_map/ppermute | solution.py:101
  65.4 0.8 %collective-permute-done.193 = bf16[128,384]{1,0:T(8,128)(2,1)S(1)} collective-permute-done((bf16[128,384]{1,0:T(8,128)(2,1)S(1)}, bf16[128,384]{1,0:T(8,128)(2,1)S(1)}, u32[]{:S(2)}, u32[]{:S(2)}) %collective-permute-start.193) | collective-permute-done | bytes 98336 | tf_op jit(solution)/shard_map/ppermute | solution.py:101
  66.2 0.7 collective-permute-done.196.refs_8_
  66.8 0.6 fusion.57
  67.4 0.8 %collective-permute-start.197 = (bf16[128,384]{1,0:T(8,128)(2,1)S(1)}, bf16[128,384]{1,0:T(8,128)(2,1)S(1)}, u32[]{:S(2)}, u32[]{:S(2)}) collective-permute-start(bf16[128,384]{1,0:T(8,128)(2,1)S(1)} %get-tuple-element.613), channel_id=1, source_target_pairs={{0,1},{1,0},{2,3},{3,2},{4,5},{5,4},{6,7},{7,6},{8,9},{9,8},{10,11... | collective-permute-start | bytes 294920 | tf_op jit(solution)/shard_map/ppermute | solution.py:101
  68.2 3.2 %shard_map.60 = bf16[384,2048]{1,0:T(8,128)(2,1)} custom-call(bf16[512,384]{1,0:T(8,128)(2,1)S(1)} %bitcast.37, bf16[64,2048]{1,0:T(8,128)(2,1)S(1)} %get-tuple-element.592.refs_1_, bf16[64,2048]{1,0:T(8,128)(2,1)} %get-tuple-element.594.refs_2_, bf16[64,2048]{1,0:T(8,128)(2,1)} %get-tuple-element.595.refs_3_, bf16[64,2048]{1,0:T(8,128)(2,1)} %get-tuple-element.597.refs_4_, ...), custom_call_target="tpu_custom_call" | custom-call | flops 805306368 | bytes 4063232 | tf_op jit(solution)/shard_map/pallas_call | solution.py:133
  71.4 0.9 %collective-permute-done.197 = bf16[128,384]{1,0:T(8,128)(2,1)S(1)} collective-permute-done((bf16[128,384]{1,0:T(8,128)(2,1)S(1)}, bf16[128,384]{1,0:T(8,128)(2,1)S(1)}, u32[]{:S(2)}, u32[]{:S(2)}) %collective-permute-start.197) | collective-permute-done | bytes 98336 | tf_op jit(solution)/shard_map/ppermute | solution.py:101
  72.4 1.2 %convolution_convert_fusion.1 = bf16[2,256,384]{2,1,0:T(8,128)(2,1)} fusion(bf16[1,128,384]{2,1,0:T(8,128)(2,1)S(1)} %fusion.40, bf16[1,128,384]{2,1,0:T(8,128)(2,1)S(1)} %fusion.39, bf16[1,128,384]{2,1,0:T(8,128)(2,1)S(1)} %fusion.38, bf16[1,128,384]{2,1,0:T(8,128)(2,1)S(1)} %fusion.37, s32[2,256]{1,0:T(2,128)S(1)} %bitcast.40, s32[256]{0:T(256)S(1)} %add_add_fusion.1), kind=kOutput, calls=%fused_computation.1 | convolution fusion | flops 102563840 | bytes 789504 | tf_op jit(solution)/shard_map/mei,mew->miw/dot_general | solution.py:242
  (47 shorter events, 6.5 us)
Async XLA Ops:
  0.6 2.3 %copy-start = (bf16[384,2048]{1,0:T(8,128)(2,1)S(1)}, bf16[384,2048]{1,0:T(8,128)(2,1)}, u32[]{:S(2)}) copy-start(bf16[384,2048]{1,0:T(8,128)(2,1)} %param.101) | copy-start | bytes 4718596
  1.7 1.8 %copy-start.2 = (bf16[2,256,384]{2,1,0:T(8,128)(2,1)S(1)}, bf16[2,256,384]{2,1,0:T(8,128)(2,1)}, u32[]{:S(2)}) copy-start(bf16[2,256,384]{2,1,0:T(8,128)(2,1)} %param.100) | copy-start | bytes 1179652
  3.4 2.7 %collective-permute-start.188 = (f32[128,2048]{1,0:T(8,128)S(1)}, f32[128,2048]{1,0:T(8,128)S(1)}, u32[]{:S(2)}, u32[]{:S(2)}) collective-permute-start(f32[128,2048]{1,0:T(8,128)S(1)} %fusion.45), channel_id=1, source_target_pairs={{0,2},{2,0},{4,6},{6,4},{8,10},{10,8},{12,14},{14,12},{16,18},{18,... | collective-permute-start | bytes 3145736 | tf_op jit(solution)/shard_map/ppermute | solution.py:101
  4.2 3.6 %collective-permute-start.189 = (f32[128,2048]{1,0:T(8,128)S(1)}, f32[128,2048]{1,0:T(8,128)S(1)}, u32[]{:S(2)}, u32[]{:S(2)}) collective-permute-start(f32[128,2048]{1,0:T(8,128)S(1)} %fusion.41), channel_id=1, source_target_pairs={{0,2},{2,0},{4,6},{6,4},{8,10},{10,8},{12,14},{14,12},{16,18},{18,... | collective-permute-start | bytes 3145736 | tf_op jit(solution)/shard_map/ppermute | solution.py:101
  6.2 1.7 %copy-start.1 = (s32[2,8]{1,0:T(2,128)S(1)}, s32[2,8]{1,0:T(2,128)}, u32[]{:S(2)}) copy-start(s32[2,8]{1,0:T(2,128)} %order_ref) | copy-start | bytes 196
  6.2 8.4 %collective-permute-start.190 = (bf16[64,2048]{1,0:T(8,128)(2,1)S(1)}, bf16[64,2048]{1,0:T(8,128)(2,1)S(1)}, u32[]{:S(2)}, u32[]{:S(2)}) collective-permute-start(bf16[64,2048]{1,0:T(8,128)(2,1)S(1)} %fusion.2), channel_id=1, source_target_pairs={{0,4},{2,6},{4,0},{6,2},{8,12},{10,14},{12,8},{14,10},{16,20},{18,... | collective-permute-start | bytes 786440 | tf_op jit(solution)/shard_map/ppermute | solution.py:101
  14.8 8.5 %collective-permute-start.25 = (bf16[64,2048]{1,0:T(8,128)(2,1)S(1)}, bf16[64,2048]{1,0:T(8,128)(2,1)S(1)}, u32[]{:S(2)}, u32[]{:S(2)}) collective-permute-start(bf16[64,2048]{1,0:T(8,128)(2,1)S(1)} %get-tuple-element.411), channel_id=1, source_target_pairs={{0,16},{2,18},{4,20},{6,22},{8,0},{10,2},{12,4},{14,6},{16,24},{18... | collective-permute-start | bytes 786440 | tf_op jit(solution)/shard_map/cond/branch_13_fun/ppermute | solution.py:92
  15.1 8.2 %collective-permute-start.26 = (bf16[64,2048]{1,0:T(8,128)(2,1)S(1)}, bf16[64,2048]{1,0:T(8,128)(2,1)}, u32[]{:S(2)}, u32[]{:S(2)}) collective-permute-start(bf16[64,2048]{1,0:T(8,128)(2,1)S(1)} %get-tuple-element.412), channel_id=1, source_target_pairs={{0,4},{2,6},{4,0},{6,2},{8,12},{10,14},{12,8},{14,10},{16,20},{18,... | collective-permute-start | bytes 786440 | tf_op jit(solution)/shard_map/cond/branch_13_fun/ppermute | solution.py:101
  23.4 8.5 %collective-permute-start.50 = (bf16[64,2048]{1,0:T(8,128)(2,1)S(1)}, bf16[64,2048]{1,0:T(8,128)(2,1)S(1)}, u32[]{:S(2)}, u32[]{:S(2)}) collective-permute-start(bf16[64,2048]{1,0:T(8,128)(2,1)S(1)} %param.28), channel_id=1, source_target_pairs={{0,0},{2,2},{4,4},{6,6},{8,24},{10,26},{12,28},{14,30},{16,8},{18,... | collective-permute-start | bytes 786440 | tf_op jit(solution)/shard_map/cond/branch_4_fun/ppermute | solution.py:92
  33.2 10.5 %collective-permute-start.89 = (bf16[64,2048]{1,0:T(8,128)(2,1)S(1)}, bf16[64,2048]{1,0:T(8,128)(2,1)}, u32[]{:S(2)}, u32[]{:S(2)}) collective-permute-start(bf16[64,2048]{1,0:T(8,128)(2,1)S(1)} %get-tuple-element.453), channel_id=1, source_target_pairs={{0,8},{2,10},{4,12},{6,14},{8,24},{10,26},{12,28},{14,30},{16,0},{... | collective-permute-start | bytes 786440 | tf_op jit(solution)/shard_map/cond/branch_10_fun/ppermute | solution.py:92
  35.9 7.8 %collective-permute-start.90 = (bf16[64,2048]{1,0:T(8,128)(2,1)S(1)}, bf16[64,2048]{1,0:T(8,128)(2,1)}, u32[]{:S(2)}, u32[]{:S(2)}) collective-permute-start(bf16[64,2048]{1,0:T(8,128)(2,1)S(1)} %get-tuple-element.454), channel_id=1, source_target_pairs={{0,4},{2,6},{4,0},{6,2},{8,12},{10,14},{12,8},{14,10},{16,20},{18,... | collective-permute-start | bytes 786440 | tf_op jit(solution)/shard_map/cond/branch_10_fun/ppermute | solution.py:101
  43.7 10.7 %collective-permute-start.164 = (bf16[64,2048]{1,0:T(8,128)(2,1)S(1)}, bf16[64,2048]{1,0:T(8,128)(2,1)}, u32[]{:S(2)}, u32[]{:S(2)}) collective-permute-start(bf16[64,2048]{1,0:T(8,128)(2,1)S(1)} %get-tuple-element.529), channel_id=1, source_target_pairs={{0,16},{2,18},{4,20},{6,22},{8,24},{10,26},{12,28},{14,30},{16,0},... | collective-permute-start | bytes 786440 | tf_op jit(solution)/shard_map/cond/branch_16_fun/ppermute | solution.py:92
  50.0 4.5 %collective-permute-start.165 = (bf16[64,2048]{1,0:T(8,128)(2,1)S(1)}, bf16[64,2048]{1,0:T(8,128)(2,1)}, u32[]{:S(2)}, u32[]{:S(2)}) collective-permute-start(bf16[64,2048]{1,0:T(8,128)(2,1)S(1)} %get-tuple-element.530), channel_id=1, source_target_pairs={{0,2},{2,0},{4,6},{6,4},{8,10},{10,8},{12,14},{14,12},{16,18},{18,... | collective-permute-start | bytes 786440 | tf_op jit(solution)/shard_map/cond/branch_16_fun/ppermute | solution.py:101
  50.0 4.5 %collective-permute-start.166 = (bf16[64,2048]{1,0:T(8,128)(2,1)}, bf16[64,2048]{1,0:T(8,128)(2,1)}, u32[]{:S(2)}, u32[]{:S(2)}) collective-permute-start(bf16[64,2048]{1,0:T(8,128)(2,1)} %get-tuple-element.531), channel_id=1, source_target_pairs={{0,2},{2,0},{4,6},{6,4},{8,10},{10,8},{12,14},{14,12},{16,18},{18,... | collective-permute-start | bytes 786440 | tf_op jit(solution)/shard_map/cond/branch_16_fun/ppermute | solution.py:101
  55.7 1.7 %collective-permute-start.191 = (bf16[64,2048]{1,0:T(8,128)(2,1)S(1)}, bf16[64,2048]{1,0:T(8,128)(2,1)S(1)}, u32[]{:S(2)}, u32[]{:S(2)}) collective-permute-start(bf16[64,2048]{1,0:T(8,128)(2,1)S(1)} %get-tuple-element.607.refs_5_), channel_id=1, source_target_pairs={{0,2},{2,0},{4,6},{6,4},{8,10},{10,8},{12,14},{14,12},{16,18},{18,... | collective-permute-start | bytes 786440 | tf_op jit(solution)/shard_map/ppermute | solution.py:101
  55.8 9.5 %collective-permute-start.195 = (bf16[64,2048]{1,0:T(8,128)(2,1)S(1)}, bf16[64,2048]{1,0:T(8,128)(2,1)S(1)}, u32[]{:S(2)}, u32[]{:S(2)}) collective-permute-start(bf16[64,2048]{1,0:T(8,128)(2,1)S(1)} %get-tuple-element.608), channel_id=1, source_target_pairs={{0,4},{2,6},{4,0},{6,2},{8,12},{10,14},{12,8},{14,10},{16,20},{18,... | collective-permute-start | bytes 786440 | tf_op jit(solution)/shard_map/ppermute | solution.py:101
  58.0 7.4 %collective-permute-start.194 = (bf16[128,384]{1,0:T(8,128)(2,1)S(1)}, bf16[128,384]{1,0:T(8,128)(2,1)S(1)}, u32[]{:S(2)}, u32[]{:S(2)}) collective-permute-start(bf16[128,384]{1,0:T(8,128)(2,1)S(1)} %get-tuple-element.615), channel_id=1, source_target_pairs={{0,1},{1,0},{2,3},{3,2},{4,5},{5,4},{6,7},{7,6},{8,9},{9,8},{10,11... | collective-permute-start | bytes 294920 | tf_op jit(solution)/shard_map/ppermute | solution.py:101
  61.2 5.0 %collective-permute-start.193 = (bf16[128,384]{1,0:T(8,128)(2,1)S(1)}, bf16[128,384]{1,0:T(8,128)(2,1)S(1)}, u32[]{:S(2)}, u32[]{:S(2)}) collective-permute-start(bf16[128,384]{1,0:T(8,128)(2,1)S(1)} %get-tuple-element.617), channel_id=1, source_target_pairs={{0,1},{1,0},{2,3},{3,2},{4,5},{5,4},{6,7},{7,6},{8,9},{9,8},{10,11... | collective-permute-start | bytes 294920 | tf_op jit(solution)/shard_map/ppermute | solution.py:101
  63.3 4.9 %collective-permute-start.192 = (bf16[128,384]{1,0:T(8,128)(2,1)S(1)}, bf16[128,384]{1,0:T(8,128)(2,1)S(1)}, u32[]{:S(2)}, u32[]{:S(2)}) collective-permute-start(bf16[128,384]{1,0:T(8,128)(2,1)S(1)} %get-tuple-element.619), channel_id=1, source_target_pairs={{0,1},{1,0},{2,3},{3,2},{4,5},{5,4},{6,7},{7,6},{8,9},{9,8},{10,11... | collective-permute-start | bytes 294920 | tf_op jit(solution)/shard_map/ppermute | solution.py:101
  65.2 1.6 %collective-permute-start.196 = (bf16[64,2048]{1,0:T(8,128)(2,1)S(1)}, bf16[64,2048]{1,0:T(8,128)(2,1)S(1)}, u32[]{:S(2)}, u32[]{:S(2)}) collective-permute-start(bf16[64,2048]{1,0:T(8,128)(2,1)S(1)} %collective-permute-done.195.refs_7_), channel_id=1, source_target_pairs={{0,2},{2,0},{4,6},{6,4},{8,10},{10,8},{12,14},{14,12},{16,18},{18,... | collective-permute-start | bytes 786440 | tf_op jit(solution)/shard_map/ppermute | solution.py:101
  67.4 4.9 %collective-permute-start.197 = (bf16[128,384]{1,0:T(8,128)(2,1)S(1)}, bf16[128,384]{1,0:T(8,128)(2,1)S(1)}, u32[]{:S(2)}, u32[]{:S(2)}) collective-permute-start(bf16[128,384]{1,0:T(8,128)(2,1)S(1)} %get-tuple-element.613), channel_id=1, source_target_pairs={{0,1},{1,0},{2,3},{3,2},{4,5},{5,4},{6,7},{7,6},{8,9},{9,8},{10,11... | collective-permute-start | bytes 294920 | tf_op jit(solution)/shard_map/ppermute | solution.py:101
